TPU v7x, 128 devices: a whole 4x4x4 slice. The times are simulated.
128 devices in a mesh: fluid: 16 (over z, x_hi, core), struct: 8 (over y, x_lo).
Axes of the slice: x: 4 (x_hi: 2, x_lo: 2; x = x_hi * 2 + x_lo), y: 4, z: 4, core: 2. Of those that a mesh axis runs over, the one named last changes fastest.
Arguments:
- fluid_adjoint: float32 [5, 65536], P(None, ('fluid', 'struct')), may hold values from -6 to 6
- fluid_rhs: float32 [5, 65536], P(None, ('fluid', 'struct')), may hold values from -6 to 6
- diag_inverse: float32 [5, 5, 65536], P(None, None, ('fluid', 'struct'))
- face_blocks: float32 [6, 5, 5, 65536], P(None, None, None, ('fluid', 'struct')), may hold values from -0.625 to 0.625
- face_index: int32 [6, 65536], P(None, ('fluid', 'struct')), may hold values from 0 to 1023, as said below
- surface_cell: int32 [32768], P(('fluid', 'struct')), may hold values from 0 to 511, as said below
- surface_count: int32 [128], P(('fluid', 'struct')), may hold values from 32 to 256, as said below
- transfer_node: int32 [3, 32768], P(None, ('fluid', 'struct')), may hold values from 0 to 4095
- transfer_weight: float32 [3, 32768], P(None, ('fluid', 'struct')), may hold values from 0.2 to 1
- load_sens: float32 [3, 5, 32768], P(None, None, ('fluid', 'struct')), may hold values from -4 to 4
- disp_sens: float32 [5, 3, 32768], P(None, None, ('fluid', 'struct')), may hold values from -2.4 to 2.4
- struct_adjoint: float32 [24576], P('struct'), may hold values from -6 to 6
- struct_rhs: float32 [24576], P('struct'), may hold values from -6 to 6
- shell_blocks: float32 [4, 256, 9216], P(None, 'struct'), may hold values from -0.15625 to 0.15625
- shell_inverse: float32 [256, 9216], P('struct')
- shell_columns: int32 [4, 256], P(None, 'struct'), may hold values from 0 to 255
Outputs:
- fluid_out: float32 [5, 65536], P(None, ('fluid', 'struct'))
- struct_out: float32 [24576], P('struct')
Inputs may be any that keep to these rules, and one draw needn't show every extreme that they name: `face_index`: neighbour positions lie within 256 cells of the cell's own position in the extended block; the two ends of the range are taken. `surface_cell`: distinct within each block of 256 slots; every block holds the first and the last cell of the block. `surface_count`: some block has all its slots live and some has 32.
All inputs are finite; a program needn't handle non-finite values.
Results may differ from a plain program's by a relative error of at most 0.00021.
Values sent between devices are 32-bit elements; how exact they have to be, the bound alone decides.
No kernel may reach another device: no remote copies, remote signals or barrier semaphores. Data moves between devices by JAX's collectives and lax.ppermute only.
A program may use at most 64 MiB of HBM per device.

v0:
```python
import jax
import jax.numpy as jnp
from jax import lax
from jax.sharding import PartitionSpec as P

NVAR = 5
FACES = 6
TMAP = 3
DOF = 6
BLK = 96
NB = 4
SWEEPS = 6
ITERS = 2


def padded(block, sides, width):
    for axis, dim in sides:
        count = lax.axis_size(axis)
        forward = [(i, i + 1) for i in range(count - 1)]
        backward = [(target, source) for source, target in forward]
        low = lax.ppermute(
            lax.slice_in_dim(block, block.shape[dim] - width, None, axis=dim), axis, forward
        )
        high = lax.ppermute(lax.slice_in_dim(block, 0, width, axis=dim), axis, backward)
        block = jnp.concatenate([low, block, high], axis=dim)
    return block


def body(
    fluid_adjoint,
    fluid_rhs,
    diag_inverse,
    face_blocks,
    face_index,
    surface_cell,
    surface_count,
    transfer_node,
    transfer_weight,
    load_sens,
    disp_sens,
    struct_adjoint,
    struct_rhs,
    shell_blocks,
    shell_inverse,
    shell_columns,
):
    highest = lax.Precision.HIGHEST
    cell_dev = fluid_adjoint.shape[1]
    halo_width = cell_dev // 2
    cell_block = min(256, cell_dev)
    block_total = cell_dev // cell_block
    window = cell_block + 2 * halo_width
    struct_count = lax.axis_size("struct")
    surf_slots = surface_cell.shape[0]
    live_slot = (jnp.arange(surf_slots, dtype=jnp.int32) < surface_count[0]).astype(jnp.float32)
    shard_len = struct_adjoint.shape[0]
    whole_len = shard_len * struct_count
    block_rows = shard_len // BLK
    node_total = whole_len // DOF
    shell_total = whole_len // BLK
    block_starts = jnp.arange(block_total, dtype=jnp.int32) * cell_block
    face_local = (
        face_index.reshape(FACES, block_total, cell_block) - block_starts[None, :, None]
    ).transpose(1, 0, 2)
    window_ids = jnp.arange(window, dtype=jnp.int32)
    surf_table = live_slot[:, None] * (
        surface_cell[:, None] == jnp.arange(cell_dev, dtype=jnp.int32)[None, :]
    ).astype(jnp.float32)
    node_ids = jnp.arange(node_total, dtype=jnp.int32)
    transfer_table = jnp.zeros((node_total, surf_slots), jnp.float32)
    for term in range(TMAP):
        transfer_table = transfer_table + transfer_weight[term][None, :] * (
            transfer_node[term][None, :] == node_ids[:, None]
        ).astype(jnp.float32)
    column_table = (
        shell_columns[:, :, None] == jnp.arange(shell_total, dtype=jnp.int32)[None, None, :]
    ).astype(jnp.float32)
    fluid_state = fluid_adjoint
    struct_state = struct_adjoint
    for iteration in range(ITERS):
        group_adjoint = lax.all_gather(struct_state, "struct", axis=0, tiled=True)
        node_adjoint = group_adjoint.reshape(node_total, DOF)[:, 0:3]
        displaced = jnp.einsum("nj,ns->js", node_adjoint, transfer_table, precision=highest)
        load_adj = jnp.einsum("jvs,js->vs", load_sens, displaced, precision=highest)
        coupling = jnp.dot(load_adj, surf_table, precision=highest)
        shell_rows = jnp.einsum(
            "mbn,nq->mbq", column_table, group_adjoint.reshape(shell_total, BLK), precision=highest
        )
        shell_terms = jnp.einsum(
            "mbqp,mbq->bp",
            shell_blocks.reshape(NB, block_rows, BLK, BLK),
            shell_rows,
            precision=highest,
        )
        for sweep_step in range(SWEEPS):
            extended = padded(fluid_state, ((("fluid", "struct"), 1),), halo_width)

            def neighbour_block(pair):
                start, local = pair
                piece = lax.dynamic_slice_in_dim(extended, start, window, 1)
                selector = (window_ids[None, :, None] == local[:, None, :]).astype(jnp.float32)
                return jnp.einsum("uw,kwc->ukc", piece, selector, precision=highest)

            blocks_out = lax.map(neighbour_block, (block_starts, face_local))
            beside = blocks_out.transpose(1, 2, 0, 3).reshape(NVAR, FACES, cell_dev)
            face_terms = jnp.einsum("kuvc,ukc->vc", face_blocks, beside, precision=highest)
            fluid_state = jnp.einsum(
                "vuc,uc->vc", diag_inverse, fluid_rhs + coupling - face_terms, precision=highest
            )
        surface_state = jnp.einsum("vc,sc->vs", fluid_state, surf_table, precision=highest)
        surface_sens = jnp.einsum("vjs,vs->js", disp_sens, surface_state, precision=highest)
        node_part = jnp.einsum("ns,js->nj", transfer_table, surface_sens, precision=highest)
        node_forces = jnp.concatenate(
            [node_part, jnp.zeros((node_total, DOF - 3), jnp.float32)], axis=1
        ).reshape(-1)
        summed_share = lax.psum_scatter(node_forces, "struct", scatter_dimension=0, tiled=True)
        forces = lax.psum(summed_share, "fluid")
        struct_total = (
            struct_rhs.reshape(block_rows, BLK) + forces.reshape(block_rows, BLK) - shell_terms
        )
        struct_state = jnp.einsum(
            "bpq,bq->bp",
            shell_inverse.reshape(block_rows, BLK, BLK),
            struct_total,
            precision=highest,
        ).reshape(-1)
    return (fluid_state, struct_state)


def solution(mesh):
    placed = (
        P(None, ("fluid", "struct")),
        P(None, ("fluid", "struct")),
        P(None, None, ("fluid", "struct")),
        P(None, None, None, ("fluid", "struct")),
        P(None, ("fluid", "struct")),
        P(("fluid", "struct")),
        P(("fluid", "struct")),
        P(None, ("fluid", "struct")),
        P(None, ("fluid", "struct")),
        P(None, None, ("fluid", "struct")),
        P(None, None, ("fluid", "struct")),
        P("struct"),
        P("struct"),
        P(None, "struct", None),
        P("struct", None),
        P(None, "struct"),
    )
    return jax.shard_map(
        body,
        mesh=mesh,
        in_specs=placed,
        out_specs=(P(None, ("fluid", "struct")), P("struct")),
        check_vma=False,
    )
```

profile of v0, /device:TPU:0, one launch (start us, length us, event | category | flops | bytes accessed | tf_op | source)
XLA Modules:
  0.0 625.6 jit_solution(6083328963461523287)
XLA Ops:
  7.9 3.5 collective-permute-start
  15.0 30.9 %all_gather.6 = f32[24576]{0:T(1024)S(1)} all-gather(f32[3072]{0:T(1024)} %param.51), channel_id=1, replica_groups=mesh['fluid'=16,'struct'=8] {'struct'}, dimensions={0}, use_global_device_ids=true | all-gather | bytes 110592 | tf_op jit(solution)/shard_map/all_gather | solution.py:81
  45.9 3.5 reshape.128
  49.4 6.2 fusion.115
  56.3 8.3 %while.132 = (s32[]{:T(128)}, f32[2,5,6,256]{3,1,2,0:T(8,128)S(1)}, s32[2]{0:T(128)S(1)}, f32[5,1024]{1,0:T(8,128)S(1)}, s32[2,6,256]{2,1,0:T(8,128)S(1)}, /*index=5*/s32[]{:T(128)}, s32[]{:T(128)}, s32[]{:T(128)}) while((s32[]{:T(128)}, f32[2,5,6,256]{3,1,2,0:T(8,128)S(1)}, s32[2]{0:T(128)S(1)}, f32[5,1024]{1,0:T(8,128)S(1)}, ...), condition=%wide.region_1.2_spmd.clone, body=%wide.region_0.1_spmd.clone.sunk | while | flops 71958528 | bytes 94359 | solution.py:104
  58.9 1.6 fusion.242
  63.0 1.6 fusion.242
  64.9 2.4 collective-permute-start.2
  68.6 4.2 collective-permute-done.3
  72.9 8.3 %while.133 = (s32[]{:T(128)}, f32[2,5,6,256]{3,1,2,0:T(8,128)S(1)}, s32[2]{0:T(128)S(1)}, f32[5,1024]{1,0:T(8,128)S(1)}, s32[2,6,256]{2,1,0:T(8,128)S(1)}, /*index=5*/s32[]{:T(128)}, s32[]{:T(128)}, s32[]{:T(128)}) while((s32[]{:T(128)}, f32[2,5,6,256]{3,1,2,0:T(8,128)S(1)}, s32[2]{0:T(128)S(1)}, f32[5,1024]{1,0:T(8,128)S(1)}, ...), condition=%wide.region_3.4_spmd.clone, body=%wide.region_2.3_spmd.clone.sunk | while | flops 71958528 | bytes 94359 | solution.py:104
  75.4 1.6 fusion.244
  79.5 1.6 fusion.244
  81.4 3.1 collective-permute-start.4
  85.9 4.2 collective-permute-done.5
  90.1 8.3 %while.134 = (s32[]{:T(128)}, f32[2,5,6,256]{3,1,2,0:T(8,128)S(1)}, s32[2]{0:T(128)S(1)}, f32[5,1024]{1,0:T(8,128)S(1)}, s32[2,6,256]{2,1,0:T(8,128)S(1)}, /*index=5*/s32[]{:T(128)}, s32[]{:T(128)}, s32[]{:T(128)}) while((s32[]{:T(128)}, f32[2,5,6,256]{3,1,2,0:T(8,128)S(1)}, s32[2]{0:T(128)S(1)}, f32[5,1024]{1,0:T(8,128)S(1)}, ...), condition=%wide.region_5.6_spmd.clone, body=%wide.region_4.5_spmd.clone.sunk | while | flops 71958528 | bytes 94359 | solution.py:104
  92.6 1.6 fusion.246
  96.8 1.6 fusion.246
  98.6 2.8 collective-permute-start.6
  103.1 3.9 collective-permute-done.7
  107.0 8.3 %while.135 = (s32[]{:T(128)}, f32[2,5,6,256]{3,1,2,0:T(8,128)S(1)}, s32[2]{0:T(128)S(1)}, f32[5,1024]{1,0:T(8,128)S(1)}, s32[2,6,256]{2,1,0:T(8,128)S(1)}, /*index=5*/s32[]{:T(128)}, s32[]{:T(128)}, s32[]{:T(128)}) while((s32[]{:T(128)}, f32[2,5,6,256]{3,1,2,0:T(8,128)S(1)}, s32[2]{0:T(128)S(1)}, f32[5,1024]{1,0:T(8,128)S(1)}, ...), condition=%wide.region_7.8_spmd.clone, body=%wide.region_6.7_spmd.clone.sunk | while | flops 71958528 | bytes 94359 | solution.py:104
  109.6 1.6 fusion.248
  113.7 1.6 fusion.248
  115.6 3.4 collective-permute-start.8
  120.5 6.5 %reshape.138 = f32[4,32,96,96]{3,2,1,0:T(8,128)} reshape(f32[4,32,9216]{2,1,0:T(8,128)} %param.53) | data formatting | bytes 9437184 | tf_op jit(solution)/shard_map/reshape | solution.py:91
  127.1 8.3 %while.136 = (s32[]{:T(128)}, f32[2,5,6,256]{3,1,2,0:T(8,128)S(1)}, s32[2]{0:T(128)S(1)}, f32[5,1024]{1,0:T(8,128)S(1)}, s32[2,6,256]{2,1,0:T(8,128)S(1)}, /*index=5*/s32[]{:T(128)}, s32[]{:T(128)}, s32[]{:T(128)}) while((s32[]{:T(128)}, f32[2,5,6,256]{3,1,2,0:T(8,128)S(1)}, s32[2]{0:T(128)S(1)}, f32[5,1024]{1,0:T(8,128)S(1)}, ...), condition=%wide.region_9.10_spmd.clone, body=%wide.region_8.9_spmd.clone.sunk | while | flops 71958528 | bytes 94359 | solution.py:104
  129.6 1.6 fusion.250
  133.8 1.6 fusion.250
  135.6 4.7 collective-permute-start.10
  141.6 8.8 %fusion.110 = f32[32,1,96,1]{2,1,3,0:T(1,128)S(1)} fusion(f32[4,32,96,96]{3,2,1,0:T(8,128)} %reshape.138, f32[4,32,96,1]{2,1,0,3:T(8,128)S(1)} %convolution_bitcast_fusion.1), kind=kOutput, calls=%fused_computation.122 | convolution fusion | flops 14155776 | bytes 4780032 | tf_op jit(solution)/shard_map/mbqp,mbq->bp/dot_general | solution.py:89
  152.3 8.3 %while.137 = (s32[]{:T(128)}, f32[2,5,6,256]{3,1,2,0:T(8,128)S(1)}, s32[2]{0:T(128)S(1)}, f32[5,1024]{1,0:T(8,128)S(1)}, s32[2,6,256]{2,1,0:T(8,128)S(1)}, /*index=5*/s32[]{:T(128)}, s32[]{:T(128)}, s32[]{:T(128)}) while((s32[]{:T(128)}, f32[2,5,6,256]{3,1,2,0:T(8,128)S(1)}, s32[2]{0:T(128)S(1)}, f32[5,1024]{1,0:T(8,128)S(1)}, ...), condition=%wide.region_11.12_spmd.clone, body=%wide.region_10.11_spmd.clone.sunk | while | flops 71958528 | bytes 94359 | solution.py:104
  154.9 1.6 fusion.252
  159.0 1.6 fusion.252
  161.4 5.2 collective-permute-start.12
  166.6 1.8 collective-permute-start.13
  168.4 4.5 fusion.114
  174.4 3.8 reshape.136
  178.4 8.3 %while.138 = (s32[]{:T(128)}, f32[2,5,6,256]{3,1,2,0:T(8,128)S(1)}, s32[2]{0:T(128)S(1)}, f32[5,1024]{1,0:T(8,128)S(1)}, s32[2,6,256]{2,1,0:T(8,128)S(1)}, /*index=5*/s32[]{:T(128)}, s32[]{:T(128)}, s32[]{:T(128)}) while((s32[]{:T(128)}, f32[2,5,6,256]{3,1,2,0:T(8,128)S(1)}, s32[2]{0:T(128)S(1)}, f32[5,1024]{1,0:T(8,128)S(1)}, ...), condition=%wide.region_15.16_spmd.clone, body=%wide.region_14.15_spmd.clone.sunk | while | flops 71958528 | bytes 94359 | solution.py:104
  181.0 1.6 fusion.254
  186.9 83.6 %all-reduce.7.cloned.1.call-done = f32[24576]{0:T(1024)} async-done(((f32[24576]{0:T(1024)}), f32[24576]{0:T(1024)}) %all-reduce.7.cloned.1.call-update) | async-done | bytes 98320
  271.2 64.9 %psum.14 = f32[3072]{0:T(1024)S(1)} all-reduce(f32[3072]{0:T(1024)S(1)} %dynamic-slice.1), channel_id=1, replica_groups=mesh['fluid'=16,'struct'=8] {'fluid'}, use_global_device_ids=true, to_apply=%region_13.14 | all-reduce | flops 3072 | bytes 24576 | tf_op jit(solution)/shard_map/psum | solution.py:117
  336.2 2.5 fusion.205
  338.8 28.4 %all_gather.7 = f32[24576]{0:T(1024)S(1)} all-gather(f32[3072]{0:T(1024)S(1)} %reshape.140), channel_id=1, replica_groups=mesh['fluid'=16,'struct'=8] {'struct'}, dimensions={0}, use_global_device_ids=true | all-gather | bytes 110592 | tf_op jit(solution)/shard_map/all_gather | solution.py:81
  367.2 3.5 reshape.141
  370.7 5.9 fusion.146
  379.8 4.2 collective-permute-done.15
  384.0 8.3 %while.139 = (s32[]{:T(128)}, f32[2,5,6,256]{3,1,2,0:T(8,128)S(1)}, s32[2]{0:T(128)S(1)}, f32[5,1024]{1,0:T(8,128)S(1)}, s32[2,6,256]{2,1,0:T(8,128)S(1)}, /*index=5*/s32[]{:T(128)}, s32[]{:T(128)}, s32[]{:T(128)}) while((s32[]{:T(128)}, f32[2,5,6,256]{3,1,2,0:T(8,128)S(1)}, s32[2]{0:T(128)S(1)}, f32[5,1024]{1,0:T(8,128)S(1)}, ...), condition=%wide.region_17.18_spmd.clone, body=%wide.region_16.17_spmd.clone.sunk | while | flops 71958528 | bytes 94359 | solution.py:104
  392.6 4.2 collective-permute-start.16
  398.1 4.2 collective-permute-done.17
  402.3 8.3 %while.140 = (s32[]{:T(128)}, f32[2,5,6,256]{3,1,2,0:T(8,128)S(1)}, s32[2]{0:T(128)S(1)}, f32[5,1024]{1,0:T(8,128)S(1)}, s32[2,6,256]{2,1,0:T(8,128)S(1)}, /*index=5*/s32[]{:T(128)}, s32[]{:T(128)}, s32[]{:T(128)}) while((s32[]{:T(128)}, f32[2,5,6,256]{3,1,2,0:T(8,128)S(1)}, s32[2]{0:T(128)S(1)}, f32[5,1024]{1,0:T(8,128)S(1)}, ...), condition=%wide.region_19.20_spmd.clone, body=%wide.region_18.19_spmd.clone.sunk | while | flops 71958528 | bytes 94359 | solution.py:104
  410.9 2.8 collective-permute-start.18
  415.1 4.2 collective-permute-done.19
  419.3 8.3 %while.141 = (s32[]{:T(128)}, f32[2,5,6,256]{3,1,2,0:T(8,128)S(1)}, s32[2]{0:T(128)S(1)}, f32[5,1024]{1,0:T(8,128)S(1)}, s32[2,6,256]{2,1,0:T(8,128)S(1)}, /*index=5*/s32[]{:T(128)}, s32[]{:T(128)}, s32[]{:T(128)}) while((s32[]{:T(128)}, f32[2,5,6,256]{3,1,2,0:T(8,128)S(1)}, s32[2]{0:T(128)S(1)}, f32[5,1024]{1,0:T(8,128)S(1)}, ...), condition=%wide.region_21.22_spmd.clone, body=%wide.region_20.21_spmd.clone.sunk | while | flops 71958528 | bytes 94359 | solution.py:104
  427.8 3.4 collective-permute-start.20
  432.6 4.1 collective-permute-done.21
  436.7 7.8 %while.142 = (s32[]{:T(128)}, f32[2,5,6,256]{3,1,2,0:T(8,128)S(1)}, s32[2]{0:T(128)S(1)}, f32[5,1024]{1,0:T(8,128)S(1)}, s32[2,6,256]{2,1,0:T(8,128)S(1)}, /*index=5*/s32[]{:T(128)}, s32[]{:T(128)}, s32[]{:T(128)}) while((s32[]{:T(128)}, f32[2,5,6,256]{3,1,2,0:T(8,128)S(1)}, s32[2]{0:T(128)S(1)}, f32[5,1024]{1,0:T(8,128)S(1)}, ...), condition=%wide.region_23.24_spmd.clone, body=%wide.region_22.23_spmd.clone.sunk | while | flops 71958528 | bytes 94359 | solution.py:104
  444.9 4.0 collective-permute-start.22
  450.4 4.0 collective-permute-done.23
  454.4 8.5 %while.143 = (s32[]{:T(128)}, f32[2,5,6,256]{3,1,2,0:T(8,128)S(1)}, s32[2]{0:T(128)S(1)}, f32[5,1024]{1,0:T(8,128)S(1)}, s32[2,6,256]{2,1,0:T(8,128)S(1)}, /*index=5*/s32[]{:T(128)}, s32[]{:T(128)}, s32[]{:T(128)}) while((s32[]{:T(128)}, f32[2,5,6,256]{3,1,2,0:T(8,128)S(1)}, s32[2]{0:T(128)S(1)}, f32[5,1024]{1,0:T(8,128)S(1)}, ...), condition=%wide.region_25.26_spmd.clone, body=%wide.region_24.25_spmd.clone.sunk | while | flops 71958528 | bytes 94359 | solution.py:104
  463.8 4.5 fusion.112
  469.9 3.8 reshape.148
  473.7 9.0 %fusion.108 = f32[32,1,96,1]{2,1,3,0:T(1,128)S(1)} fusion(f32[4,32,96,96]{3,2,1,0:T(8,128)} %reshape.138, f32[4,32,96,1]{2,1,0,3:T(8,128)S(1)} %convolution_bitcast_fusion), kind=kOutput, calls=%fused_computation.120 | convolution fusion | flops 14155776 | bytes 4780032 | tf_op jit(solution)/shard_map/mbqp,mbq->bp/dot_general | solution.py:89
  482.7 66.7 %all-reduce.9.cloned.1.call-done = f32[24576]{0:T(1024)} async-done(((f32[24576]{0:T(1024)}), f32[24576]{0:T(1024)}) %all-reduce.9.cloned.1.call-update) | async-done | bytes 98320
  550.1 64.9 %psum.15 = f32[3072]{0:T(1024)S(1)} all-reduce(f32[3072]{0:T(1024)S(1)} %dynamic-slice.3), channel_id=1, replica_groups=mesh['fluid'=16,'struct'=8] {'fluid'}, use_global_device_ids=true, to_apply=%region_27.28 | all-reduce | flops 3072 | bytes 24576 | tf_op jit(solution)/shard_map/psum | solution.py:117
  615.1 2.5 fusion.206
  (244 shorter events, 62.5 us)
Async XLA Ops:
  7.2 263.3 %all-reduce.7.cloned.1.call-start = ((), (), s32[]{:S(2)}) async-start(), calls=%async_computation | async-start | bytes 196608
  7.9 48.3 %collective-permute-start = (f32[5,256]{1,0:T(8,128)S(1)}, f32[5,256]{1,0:T(8,128)S(1)}, u32[]{:S(2)}, u32[]{:S(2)}) collective-permute-start(f32[5,256]{1,0:T(8,128)S(1)} %get-tuple-element.684), channel_id=1, source_target_pairs={{0,1},{1,2},{2,3},{3,4},{4,5},{5,6},{6,7},{7,8},{8,9},{9,10},{10,1... | collective-permute-start | bytes 15368 | tf_op jit(solution)/shard_map/ppermute | solution.py:21
  11.4 44.9 %collective-permute-start.1 = (f32[5,256]{1,0:T(8,128)S(1)}, f32[5,256]{1,0:T(8,128)S(1)}, u32[]{:S(2)}, u32[]{:S(2)}) collective-permute-start(f32[5,256]{1,0:T(8,128)S(1)} %get-tuple-element.685), channel_id=1, source_target_pairs={{1,0},{2,1},{3,2},{4,3},{5,4},{6,5},{7,6},{8,7},{9,8},{10,9},{11,1... | collective-permute-start | bytes 15368 | tf_op jit(solution)/shard_map/ppermute | solution.py:24
  49.4 6.3 %copy-start.3 = (f32[3,5,256]{2,0,1:T(4,128)S(1)}, f32[3,5,256]{2,0,1:T(4,128)}, u32[]{:S(2)}) copy-start(f32[3,5,256]{2,0,1:T(4,128)} %param.49) | copy-start | bytes 46084
  49.4 6.3 %copy-start.10 = (f32[5,512]{1,0:T(8,128)S(1)}, f32[5,512]{1,0:T(8,128)}, u32[]{:S(2)}) copy-start(f32[5,512]{1,0:T(8,128)} %param.41) | copy-start | bytes 30724
  49.4 6.3 %copy-start.11 = (s32[256]{0:T(256)S(1)}, s32[256]{0:T(256)}, u32[]{:S(2)}) copy-start(s32[256]{0:T(256)} %param.45) | copy-start | bytes 3076
  49.4 6.8 %copy-start.8 = (s32[6,512]{1,0:T(8,128)S(1)}, s32[6,512]{1,0:T(8,128)}, u32[]{:S(2)}) copy-start(s32[6,512]{1,0:T(8,128)} %param.44) | copy-start | bytes 36868
  49.4 6.9 %copy-start.5 = (f32[5,512]{1,0:T(8,128)S(1)}, f32[5,512]{1,0:T(8,128)}, u32[]{:S(2)}) copy-start(f32[5,512]{1,0:T(8,128)} %param.40) | copy-start | bytes 30724
  55.7 9.1 %copy-start = (f32[6,5,5,512]{3,0,2,1:T(8,128)S(1)}, f32[6,5,5,512]{3,0,2,1:T(8,128)}, u32[]{:S(2)}) copy-start(f32[6,5,5,512]{3,0,2,1:T(8,128)} %param.43) | copy-start | bytes 921604
  55.7 9.2 %copy-start.1 = (f32[5,5,512]{2,1,0:T(8,128)S(1)}, f32[5,5,512]{2,1,0:T(8,128)}, u32[]{:S(2)}) copy-start(f32[5,5,512]{2,1,0:T(8,128)} %param.42) | copy-start | bytes 153604
  64.9 3.8 collective-permute-start.2
  67.3 5.5 collective-permute-start.3
  81.4 4.5 collective-permute-start.4
  84.5 5.5 collective-permute-start.5
  98.5 21.8 %copy-start.9 = (s32[4,32]{1,0:T(4,128)S(1)}, s32[4,32]{1,0:T(4,128)}, u32[]{:S(2)}) copy-start(s32[4,32]{1,0:T(4,128)} %param.55) | copy-start | bytes 1540
  98.6 4.4 collective-permute-start.6
  101.5 5.5 collective-permute-start.7
  115.6 11.5 %collective-permute-start.8 = (f32[5,256]{1,0:T(8,128)S(1)}, f32[5,256]{1,0:T(8,128)S(1)}, u32[]{:S(2)}, u32[]{:S(2)}) collective-permute-start(f32[5,256]{1,0:T(8,128)S(1)} %get-tuple-element.676), channel_id=1, source_target_pairs={{0,1},{1,2},{2,3},{3,4},{4,5},{5,6},{6,7},{7,8},{8,9},{9,10},{10,1... | collective-permute-start | bytes 15368 | tf_op jit(solution)/shard_map/ppermute | solution.py:21
  118.9 8.1 %collective-permute-start.9 = (f32[5,256]{1,0:T(8,128)S(1)}, f32[5,256]{1,0:T(8,128)S(1)}, u32[]{:S(2)}, u32[]{:S(2)}) collective-permute-start(f32[5,256]{1,0:T(8,128)S(1)} %get-tuple-element.677), channel_id=1, source_target_pairs={{1,0},{2,1},{3,2},{4,3},{5,4},{6,5},{7,6},{8,7},{9,8},{10,9},{11,1... | collective-permute-start | bytes 15368 | tf_op jit(solution)/shard_map/ppermute | solution.py:24
  135.3 15.0 %copy-start.2 = (f32[32,9216]{1,0:T(8,128)S(1)}, f32[32,9216]{1,0:T(8,128)}, u32[]{:S(2)}) copy-start(f32[32,9216]{1,0:T(8,128)} %param.54) | copy-start | bytes 3538948
  135.6 16.7 %collective-permute-start.10 = (f32[5,256]{1,0:T(8,128)S(1)}, f32[5,256]{1,0:T(8,128)S(1)}, u32[]{:S(2)}, u32[]{:S(2)}) collective-permute-start(f32[5,256]{1,0:T(8,128)S(1)} %get-tuple-element.674), channel_id=1, source_target_pairs={{0,1},{1,2},{2,3},{3,4},{4,5},{5,6},{6,7},{7,8},{8,9},{9,10},{10,1... | collective-permute-start | bytes 15368 | tf_op jit(solution)/shard_map/ppermute | solution.py:21
  140.3 10.7 %copy-start.12 = (u32[128]{0:T(128)S(1)}, u32[128]{0:T(128)}, u32[]{:S(2)}) copy-start(u32[128]{0:T(128)} %constant.168) | copy-start | bytes 1540
  140.3 12.0 %collective-permute-start.11 = (f32[5,256]{1,0:T(8,128)S(1)}, f32[5,256]{1,0:T(8,128)S(1)}, u32[]{:S(2)}, u32[]{:S(2)}) collective-permute-start(f32[5,256]{1,0:T(8,128)S(1)} %get-tuple-element.675), channel_id=1, source_target_pairs={{1,0},{2,1},{3,2},{4,3},{5,4},{6,5},{7,6},{8,7},{9,8},{10,9},{11,1... | collective-permute-start | bytes 15368 | tf_op jit(solution)/shard_map/ppermute | solution.py:24
  151.0 17.4 %copy-start.4 = (f32[5,3,256]{2,1,0:T(4,128)S(1)}, f32[5,3,256]{2,1,0:T(4,128)}, u32[]{:S(2)}) copy-start(f32[5,3,256]{2,1,0:T(4,128)} %param.50) | copy-start | bytes 46084
  161.4 16.9 %collective-permute-start.12 = (f32[5,256]{1,0:T(8,128)S(1)}, f32[5,256]{1,0:T(8,128)S(1)}, u32[]{:S(2)}, u32[]{:S(2)}) collective-permute-start(f32[5,256]{1,0:T(8,128)S(1)} %get-tuple-element.672), channel_id=1, source_target_pairs={{0,1},{1,2},{2,3},{3,4},{4,5},{5,6},{6,7},{7,8},{8,9},{9,10},{10,1... | collective-permute-start | bytes 15368 | tf_op jit(solution)/shard_map/ppermute | solution.py:21
  166.6 11.8 %collective-permute-start.13 = (f32[5,256]{1,0:T(8,128)S(1)}, f32[5,256]{1,0:T(8,128)S(1)}, u32[]{:S(2)}, u32[]{:S(2)}) collective-permute-start(f32[5,256]{1,0:T(8,128)S(1)} %get-tuple-element.673), channel_id=1, source_target_pairs={{1,0},{2,1},{3,2},{4,3},{5,4},{6,5},{7,6},{8,7},{9,8},{10,9},{11,1... | collective-permute-start | bytes 15368 | tf_op jit(solution)/shard_map/ppermute | solution.py:24
  178.3 157.8 %copy-start.6 = (f32[3072]{0:T(1024)S(1)}, f32[3072]{0:T(1024)}, u32[]{:S(2)}) copy-start(f32[3072]{0:T(1024)} %param.52) | copy-start | bytes 36868
  178.3 371.1 %all-reduce.9.cloned.1.call-start = ((), (), s32[]{:S(2)}) async-start(), calls=%async_computation.1 | async-start | bytes 196608
  377.2 2.6 collective-permute-start.14
  378.4 5.5 collective-permute-start.15
  392.6 5.6 collective-permute-start.16
  396.8 5.5 collective-permute-start.17
  410.9 4.2 collective-permute-start.18
  413.7 5.5 collective-permute-start.19
  427.8 4.8 collective-permute-start.20
  431.2 5.5 collective-permute-start.21
  444.9 5.6 collective-permute-start.22
  448.9 5.5 collective-permute-start.23
  463.2 5.2 copy-start.7
Sparse Core Ops, SparseCore 0:
  178.4 92.0 all-reduce.6
  473.8 75.4 all-reduce.8
where the time goes:
time: 636 us; the launch traced here: 626 us
  blocking collectives  189 us (30%)
  waiting for transfers between devices  184 us (29%)
  matrix products  84.6 us (13%)
  starting transfers between devices  57 us (9%)
  loops' own time  46.8 us (7%)
  local copies, waits for them, and re-layouts  46.1 us (7%)
  between operations  16.9 us (3%)
    unnamed x4, waiting for transfers between devices  150 us
    psum x2, blocking collectives, body(): forces = lax.psum(summed_share, 'fluid')  130 us
    all_gather x2, blocking collectives, body(): group_adjoint = lax.all_gather(struct_state, 'struct', axis=0, tiled=True)  59.3 us
    another operation x12, loops' own time, body(): blocks_out = lax.map(neighbour_block, (block_starts, face_local))  46.8 us
    ppermute x12, starting transfers between devices, padded(): lax.ppermute(lax.slice_in_dim(block, block.shape[dim] - width, None, axis...  40.7 us
    dot_general x24, matrix products, neighbour_block(): return jnp.einsum('uw,kwc->ukc', piece, selector, precision=highest)  37.9 us
    ppermute x12, waiting for transfers between devices, padded(): lax.ppermute(lax.slice_in_dim(block, 0, width, axis=dim), axis, backward)  33 us
    dot_general x2, matrix products, body(): jnp.einsum('mbqp,mbq->bp', shell_blocks.reshape(NB, block_rows, BLK, BLK)...  17.7 us
  transfers between devices with their start and end apart: 26, of which 10 were waited for; matrix products, arithmetic and copies ran while one was open for 8% of the time, Pallas kernels for 0%

commit v1 on v0

v1 whole, which is shorter than its diff:
```python
import functools

import jax
import jax.numpy as jnp
from jax import lax
from jax.experimental import pallas as pl
from jax.experimental.pallas import tpu as pltpu
from jax.sharding import PartitionSpec as P

NVAR = 5
FACES = 6
TMAP = 3
DOF = 6
BLK = 96
NB = 4
SWEEPS = 6
ITERS = 2
CELL = 512
HALF = 256
SURF = 256
LANES = 128
FLUID = 16
STRUCT = 8
DEVS = FLUID * STRUCT
PIECE_NODES = 32
PIECE = PIECE_NODES * 3
ROW = 3 * LANES
BOTH = ("fluid", "struct")

G_FACE = 0
G_DIAG = 30
G_RHS = 35
G_STATE = 36
G_LOAD = 38
G_MISC = 41
G_ALL = 44
M_INDEX = 0
M_NODE = 6
M_WEIGHT = 9
M_CELL = 12
M_LIVE = 13

f32 = jnp.float32
bf16 = jnp.bfloat16
NN = (((1,), (0,)), ((), ()))
NT = (((1,), (1,)), ((), ()))


def split(x):
    hi = x.astype(bf16)
    return hi, (x - hi.astype(f32)).astype(bf16)


def split3(x):
    hi = x.astype(bf16)
    rest = x - hi.astype(f32)
    mid = rest.astype(bf16)
    return hi, mid, (rest - mid.astype(f32)).astype(bf16)


def dot(a, b, dims):
    return lax.dot_general(a, b, dims, preferred_element_type=f32)


def iota(shape, axis):
    return lax.broadcasted_iota(jnp.int32, shape, axis)


def one_hot(mask):
    return jnp.where(mask, f32(1.0), f32(0.0)).astype(bf16)


def component_perm(half):
    row, col = iota((PIECE, BLK), 0), iota((PIECE, BLK), 1)
    dof = col % DOF
    return one_hot((dof < 3) & (row == dof * PIECE_NODES + half * 16 + col // DOF))


def live_row(count):
    return jnp.where(iota((1, SURF), 1) < count, f32(1.0), f32(0.0))


def by_device(node):
    return ((node >> 5) & 15) * STRUCT + (node >> 9)


def by_piece(node):
    return node >> 5


def pack_kernel(face, diag, rhs, state, load, index, node, weight, cell, count, adjoint,
                pack_low, pack_high, diag_t, rows):
    for v in range(NVAR):
        for u in range(NVAR):
            diag_t[u, v:v + 1, :] = diag[v, u:u + 1, :]
    live = live_row(count[0])
    for pack, lo in ((pack_low, HALF), (pack_high, 0)):
        cols = slice(lo, lo + HALF)
        pack[G_FACE:G_DIAG] = face[:, :, cols]
        pack[G_DIAG:G_RHS] = diag_t[:, :, cols]
        pack[G_RHS] = rhs[:, cols]
        pack[G_STATE] = state[:, 0:HALF]
        pack[G_STATE + 1] = state[:, HALF:CELL]
        pack[G_LOAD:G_MISC] = load[...]

        def misc(at, value):
            pack[G_MISC + at // 5, at % 5:at % 5 + 1, :] = value

        for k in range(FACES):
            misc(M_INDEX + k, index[k:k + 1, cols].astype(f32))
        for t in range(TMAP):
            misc(M_NODE + t, node[t:t + 1, :].astype(f32))
            misc(M_WEIGHT + t, weight[t:t + 1, :])
        misc(M_CELL, cell[...].astype(f32))
        misc(M_LIVE, live)
        misc(14, jnp.zeros((1, SURF), f32))
    first, second = adjoint[:, 0:BLK], adjoint[:, BLK:2 * BLK]
    comps = jnp.zeros((FLUID, PIECE), f32)
    for half, part in enumerate((first, second)):
        perm = component_perm(half)
        for term in split3(part):
            comps += dot(term, perm, NT)
    for s in range(STRUCT):
        rows[s, :, 0:BLK] = first
        rows[s, :, LANES:LANES + BLK] = second
        rows[s, :, 2 * LANES:2 * LANES + PIECE] = comps
        for j in range(3):
            rows[s, :, j * LANES + BLK:(j + 1) * LANES] = jnp.zeros((FLUID, LANES - BLK), f32)


def couple(struct_t, node, weight, load, cell, live, row_of, cells, base):
    parts = []
    for t in range(TMAP):
        pick = one_hot(iota((DEVS, SURF), 0) == row_of(node[t]))
        found = dot(struct_t[0], pick, NN) + dot(struct_t[1], pick, NN)
        gain = jnp.where(iota((PIECE_NODES, SURF), 0) == (node[t] & 31), weight[t], f32(0.0))
        parts.append((found, gain))
    shown = None
    for j in range(3):
        total = None
        for found, gain in parts:
            term = found[j * PIECE_NODES:(j + 1) * PIECE_NODES] * gain
            total = term if total is None else total + term
        moved = jnp.sum(total, axis=0, keepdims=True)
        term = load[j] * moved
        shown = term if shown is None else shown + term
    shown = shown * live
    at = one_hot(iota((cells, SURF), 0) + base == cell)
    hi, lo = split(shown)
    return dot(hi, at, NT) + dot(lo, at, NT)


def fluid_kernel(first, whole_rows, last, from_pack, *refs):
    refs = list(refs)
    take = lambda n: [refs.pop(0) for _ in range(n)]
    face, diag_t, rhs, index, low, high, state = take(7)
    if not from_pack:
        state_low, state_high = take(2)
    if first:
        struct_rows, load = take(2)
    else:
        (coupled,) = take(1)
    if first or last:
        node, weight, cell, count = take(4)
    if last:
        (disp,) = take(1)
    (out,) = take(1)
    if first:
        (coupled,) = take(1)
    if last:
        (shares,) = take(1)
    x0, x1, picks = take(3)

    x0[0:NVAR, CELL:2 * CELL] = state[...]
    if from_pack:
        for pack, at in ((low, 0), (high, 2 * CELL)):
            x0[0:NVAR, at:at + HALF] = pack[G_STATE]
            x0[0:NVAR, at + HALF:at + CELL] = pack[G_STATE + 1]
    else:
        x0[0:NVAR, 0:CELL] = state_low[...]
        x0[0:NVAR, 2 * CELL:3 * CELL] = state_high[...]

    def misc(pack, at):
        return pack[G_MISC + at // 5, at % 5:at % 5 + 1, :]

    picks[FACES:8, :] = jnp.zeros((8 - FACES, 2 * CELL), jnp.int32)
    picks[0:FACES, HALF:HALF + CELL] = index[...]
    for k in range(FACES):
        picks[k:k + 1, 0:HALF] = misc(low, M_INDEX + k).astype(jnp.int32) - CELL
        picks[k:k + 1, HALF + CELL:2 * CELL] = misc(high, M_INDEX + k).astype(jnp.int32) + CELL

    if first:
        turned = jnp.transpose(struct_rows[:, 2 * LANES:3 * LANES])
        struct_t = split(turned)
        row_of = by_piece if whole_rows else by_device
        coupled[:, HALF:HALF + CELL] = couple(
            struct_t,
            [node[t:t + 1, :] for t in range(TMAP)],
            [weight[t:t + 1, :] for t in range(TMAP)],
            [load[j] for j in range(3)],
            cell[...], live_row(count[0]), row_of, CELL, 0,
        )
        for pack, at, base in ((low, 0, HALF), (high, HALF + CELL, 0)):
            coupled[:, at:at + HALF] = couple(
                struct_t,
                [misc(pack, M_NODE + t).astype(jnp.int32) for t in range(TMAP)],
                [misc(pack, M_WEIGHT + t) for t in range(TMAP)],
                [pack[G_LOAD + j] for j in range(3)],
                misc(pack, M_CELL).astype(jnp.int32), misc(pack, M_LIVE), row_of, HALF, base,
            )

    def sweep(source, shift, at):
        if at < 0:
            lane = at + HALF
            block = lambda i: low[G_FACE + i, :, lane:lane + LANES]
            inv = lambda u: low[G_DIAG + u, :, lane:lane + LANES]
            right = low[G_RHS, :, lane:lane + LANES]
        elif at >= CELL:
            lane = at - CELL
            block = lambda i: high[G_FACE + i, :, lane:lane + LANES]
            inv = lambda u: high[G_DIAG + u, :, lane:lane + LANES]
            right = high[G_RHS, :, lane:lane + LANES]
        else:
            block = lambda i: face[i, :, at:at + LANES]
            inv = lambda u: diag_t[u, :, at:at + LANES]
            right = rhs[:, at:at + LANES]
        place = picks[:, at + HALF:at + HALF + LANES] - at
        lane_of, chunk_of = place & (LANES - 1), place >> 7
        terms = None
        for u in range(NVAR):
            near = None
            for o in range(5):
                begin = at - HALF + o * LANES + shift
                row = jnp.broadcast_to(source[u:u + 1, begin:begin + LANES], (8, LANES))
                found = jnp.take_along_axis(row, lane_of, axis=1, mode="promise_in_bounds")
                near = found if near is None else jnp.where(chunk_of == o, found, near)
            for k in range(FACES):
                term = block(k * NVAR + u) * near[k:k + 1, :]
                terms = term if terms is None else terms + term
        left = right + coupled[:, at + HALF:at + HALF + LANES] - terms
        new = None
        for u in range(NVAR):
            term = inv(u) * left[u:u + 1, :]
            new = term if new is None else new + term
        return new

    for at in range(-HALF, CELL + HALF, LANES):
        x1[0:NVAR, at + HALF:at + HALF + LANES] = sweep(x0, CELL, at)
    for at in range(0, CELL, LANES):
        out[:, at:at + LANES] = sweep(x1, HALF, at)

    if last:
        at = one_hot(iota((CELL, SURF), 0) == cell[...])
        hi, lo = split(out[...])
        surface = dot(hi, at, NN) + dot(lo, at, NN)
        sens = None
        for v in range(NVAR):
            term = disp[v] * surface[v:v + 1, :]
            sens = term if sens is None else sens + term
        sens = sens * live_row(count[0])
        total = None
        for t in range(TMAP):
            nodes = node[t:t + 1, :]
            pick = one_hot(iota((DEVS, SURF), 0) == by_device(nodes))
            gain = jnp.where(iota((PIECE_NODES, SURF), 0) == (nodes & 31),
                             weight[t:t + 1, :], f32(0.0))
            value = jnp.concatenate([gain * sens[j:j + 1, :] for j in range(3)], axis=0)
            for part in split(value):
                term = dot(pick, part, NT)
                total = term if total is None else total + term
        shares[:, 0:PIECE] = total
        shares[:, PIECE:LANES] = jnp.zeros((DEVS, LANES - PIECE), f32)


def shell_kernel(whole_rows, struct_rows, blocks, columns, out):
    for half in range(2):
        total = jnp.zeros((1, BLK), f32)
        for m in range(NB):
            column = columns[m, half]
            piece = column // 2
            row = piece if whole_rows else (piece % FLUID) * STRUCT + piece // FLUID
            line = struct_rows[pl.ds(row, 1), :]
            x = jnp.where(column % 2 == 0, line[:, 0:BLK], line[:, LANES:LANES + BLK])
            x_hi, x_lo = split(x)
            b_hi, b_lo = split(blocks[m, half])
            total += dot(x_hi, b_hi, NN) + dot(x_lo, b_hi, NN) + dot(x_hi, b_lo, NN)
        out[half:half + 1, :] = total


def solve_kernel(received, rhs, shell, inverse, out):
    force = jnp.sum(received[...], axis=0, keepdims=True)[:, 0:PIECE]
    parts = split3(force)
    comps = jnp.zeros((1, PIECE), f32)
    new = []
    for half in range(2):
        perm = component_perm(half)
        load = dot(parts[0], perm, NN) + dot(parts[1], perm, NN) + dot(parts[2], perm, NN)
        right = rhs[half:half + 1, :] + load - shell[half:half + 1, :]
        r_hi, r_lo = split(right)
        i_hi, i_lo = split(inverse[half])
        x = dot(r_hi, i_hi, NT) + dot(r_lo, i_hi, NT) + dot(r_hi, i_lo, NT)
        new.append(x)
        for term in split3(x):
            comps += dot(term, perm, NT)
    count = out.shape[0]
    for j, part in enumerate((new[0], new[1], comps)):
        if (j + 1) * LANES <= out.shape[1]:
            out[:, j * LANES:j * LANES + BLK] = jnp.broadcast_to(part, (count, BLK))
            out[:, j * LANES + BLK:(j + 1) * LANES] = jnp.zeros((count, LANES - BLK), f32)


VMEM = pl.BlockSpec(memory_space=pltpu.VMEM)
SMEM = pl.BlockSpec(memory_space=pltpu.SMEM)


def call(kernel, name, out_shapes, specs, scratch=()):
    return pl.pallas_call(
        kernel,
        name=name,
        out_shape=[jax.ShapeDtypeStruct(s, f32) for s in out_shapes],
        in_specs=specs,
        out_specs=[VMEM] * len(out_shapes),
        scratch_shapes=list(scratch),
        compiler_params=pltpu.CompilerParams(vmem_limit_bytes=48 * 1024 * 1024),
    )


FLUID_SCRATCH = (
    pltpu.VMEM((8, 3 * CELL), f32),
    pltpu.VMEM((8, 2 * CELL), f32),
    pltpu.VMEM((8, 2 * CELL), jnp.int32),
)


def body(
    fluid_adjoint,
    fluid_rhs,
    diag_inverse,
    face_blocks,
    face_index,
    surface_cell,
    surface_count,
    transfer_node,
    transfer_weight,
    load_sens,
    disp_sens,
    struct_adjoint,
    struct_rhs,
    shell_blocks,
    shell_inverse,
    shell_columns,
):
    face = face_blocks.reshape(FACES * NVAR, NVAR, CELL)
    cell = surface_cell.reshape(1, SURF)
    up = [(i, i + 1) for i in range(DEVS - 1)]
    down = [(i + 1, i) for i in range(DEVS - 1)]

    pack_low, pack_high, diag_t, rows = call(
        pack_kernel, "pack",
        [(G_ALL, NVAR, HALF), (G_ALL, NVAR, HALF), (NVAR, NVAR, CELL), (STRUCT, FLUID, ROW)],
        [VMEM] * 9 + [SMEM, VMEM],
    )(face, diag_inverse, fluid_rhs, fluid_adjoint, load_sens, face_index, transfer_node,
      transfer_weight, cell, surface_count, struct_adjoint.reshape(FLUID, 2 * BLK))
    low = lax.ppermute(pack_low, BOTH, up)
    high = lax.ppermute(pack_high, BOTH, down)
    struct_rows = lax.all_to_all(rows, "struct", 0, 0, tiled=True).reshape(DEVS, ROW)

    mine = 2 * lax.axis_index("fluid")
    own = lambda a, axis: lax.dynamic_slice_in_dim(a, mine, 2, axis)
    blocks = own(shell_blocks, 1).reshape(NB, 2, BLK, BLK)
    inverse = own(shell_inverse, 0).reshape(2, BLK, BLK)
    columns = own(shell_columns, 1)
    rhs_rows = own(struct_rhs.reshape(2 * FLUID, BLK), 0)

    state = fluid_adjoint
    for iteration in range(ITERS):
        start = iteration == 0
        (shell,) = call(
            functools.partial(shell_kernel, start), "shell", [(2, BLK)], [VMEM, VMEM, SMEM]
        )(struct_rows, blocks, columns)
        for phase in range(3):
            first, last = phase == 0, phase == 2
            from_pack = start and first
            args = [face, diag_t, fluid_rhs, face_index, low, high, state]
            if not from_pack:
                args += [lax.ppermute(state, BOTH, up), lax.ppermute(state, BOTH, down)]
            args += [struct_rows, load_sens] if first else [coupled]
            specs = [VMEM] * len(args)
            if first or last:
                args += [transfer_node, transfer_weight, cell, surface_count]
                specs += [VMEM] * 3 + [SMEM]
            if last:
                args += [disp_sens]
                specs += [VMEM]
            outs = [(NVAR, CELL)]
            if first:
                outs.append((NVAR, 2 * CELL))
            if last:
                outs.append((DEVS, LANES))
            result = call(
                functools.partial(fluid_kernel, first, start, last, from_pack),
                "fluid", outs, specs, FLUID_SCRATCH,
            )(*args)
            state = result[0]
            if first:
                coupled = result[1]
            if last:
                shares = result[1]
        received = lax.all_to_all(shares, BOTH, 0, 0, tiled=True)
        final = iteration == ITERS - 1
        (solved,) = call(
            solve_kernel, "solve", [(FLUID, 2 * LANES) if final else (DEVS, ROW)], [VMEM] * 4
        )(received, rhs_rows, shell, inverse)
        if final:
            group = lax.all_to_all(solved, "fluid", 0, 0, tiled=True)
            struct_state = group.reshape(FLUID, 2, LANES)[:, :, 0:BLK].reshape(-1)
        else:
            struct_rows = lax.all_to_all(solved, BOTH, 0, 0, tiled=True)
    return (state, struct_state)


def solution(mesh):
    placed = (
        P(None, ("fluid", "struct")),
        P(None, ("fluid", "struct")),
        P(None, None, ("fluid", "struct")),
        P(None, None, None, ("fluid", "struct")),
        P(None, ("fluid", "struct")),
        P(("fluid", "struct")),
        P(("fluid", "struct")),
        P(None, ("fluid", "struct")),
        P(None, ("fluid", "struct")),
        P(None, None, ("fluid", "struct")),
        P(None, None, ("fluid", "struct")),
        P("struct"),
        P("struct"),
        P(None, "struct", None),
        P("struct", None),
        P(None, "struct"),
    )
    return jax.shard_map(
        body,
        mesh=mesh,
        in_specs=placed,
        out_specs=(P(None, ("fluid", "struct")), P("struct")),
        check_vma=False,
    )
```

time: 636 us -> 164 us (0.26); the launches traced: 626 us -> 162 us
  blocking collectives: 189 us -> 10.9 us
  waiting for transfers between devices: 184 us -> 50.2 us
  matrix products: 84.6 us -> 0 us
  loops' own time: 46.8 us -> 0 us
  local copies, waits for them, and re-layouts: 46.1 us -> 17.4 us
  between operations: 16.9 us -> 1.62 us
  starting transfers between devices: 57 us -> 70.1 us
  Pallas kernels: 0 us -> 11.6 us
    unnamed x4 -> x0, waiting for transfers between devices: 150 us -> none
    psum x2 -> x0, blocking collectives: 130 us -> none  [body(): forces = lax.psum(summed_share, 'fluid')]
    dot_general x36 -> x0, matrix products: 75.5 us -> none  [the longest x24 37.9 us: neighbour_block(): return jnp.einsum('uw,kwc->ukc', piece, selector, precision=highest)]
    all_gather x2 -> x0, blocking collectives: 59.3 us -> none  [body(): group_adjoint = lax.all_gather(struct_state, 'struct', axis=0, tiled=True)]
    another operation x12 -> x0, loops' own time: 46.8 us -> none  [body(): blocks_out = lax.map(neighbour_block, (block_starts, face_local))]
    all_to_all x0 -> x4, starting transfers between devices: none -> 43.1 us  [the longest x2 31.9 us: body(): received = lax.all_to_all(shares, BOTH, 0, 0, tiled=True)]
    all_to_all x0 -> x4, waiting for transfers between devices: none -> 34.4 us  [the longest x2 16.9 us: body(): received = lax.all_to_all(shares, BOTH, 0, 0, tiled=True)]
    ppermute x24 -> x12, starting transfers between devices: 56.9 us -> 27 us  [the longest x10 22.3 us: body(): args += [lax.ppermute(state, BOTH, up), lax.ppermute(state, BOTH, down)]]
  transfers between devices with their start and end apart: 26 -> 16, of which waited for: 10 -> 11; matrix products, arithmetic and copies ran while one was open for 8% -> 2% of each run, Pallas kernels for 0% -> 1%
where the time goes in v1:
time: 164 us; the launch traced here: 162 us
  starting transfers between devices  70.1 us (43%)
  waiting for transfers between devices  50.2 us (31%)
  local copies, waits for them, and re-layouts  17.4 us (11%)
  Pallas kernels  11.6 us (7%)
  blocking collectives  10.9 us (7%)
    all_to_all x2, starting transfers between devices, body(): received = lax.all_to_all(shares, BOTH, 0, 0, tiled=True)  31.9 us
    ppermute x10, starting transfers between devices, body(): args += [lax.ppermute(state, BOTH, up), lax.ppermute(state, BOTH, down)]  22.3 us
    all_to_all x2, waiting for transfers between devices, body(): received = lax.all_to_all(shares, BOTH, 0, 0, tiled=True)  16.9 us
    ppermute x10, waiting for transfers between devices, body(): args += [lax.ppermute(state, BOTH, up), lax.ppermute(state, BOTH, down)]  15.7 us
    all_to_all x1, waiting for transfers between devices, body(): lax.all_to_all(rows, 'struct', 0, 0, tiled=True).reshape(DEVS, ROW)  11.6 us
    unnamed x47, local copies, waits for them, and re-layouts  11.4 us
    all_to_all x1, blocking collectives, body(): group = lax.all_to_all(solved, 'fluid', 0, 0, tiled=True)  10.9 us
    pallas_call x6, Pallas kernels, body(): call(functools.partial(fluid_kernel, first, start, last, from_pack), 'flu...  7.75 us
  transfers between devices with their start and end apart: 16, of which 11 were waited for; matrix products, arithmetic and copies ran while one was open for 2% of the time, Pallas kernels for 1%

profile of v1, /device:TPU:0, one launch (start us, length us, event | category | flops | bytes accessed | tf_op | source)
XLA Modules:
  0.0 161.8 jit_solution(666737470785511227)
XLA Ops:
  0.6 0.0 copy-start
  0.7 0.0 copy-start.9
  0.7 1.3 copy.26
  2.7 0.7 copy.27.load.refs_8_.refs_10_
  3.4 0.8 reshape.42.adjoint
  4.2 0.7 copy-done.1
  4.9 0.7 copy-done.4
  5.6 0.7 copy-done.7
  6.3 0.7 copy-done.10
  7.0 0.9 copy-done.13
  7.9 0.7 copy-done.15
  8.6 0.7 copy-done.17
  9.3 1.0 pack.1
  10.2 3.5 %collective-permute-start = (f32[44,5,256]{2,1,0:T(8,128)}, f32[44,5,256]{2,1,0:T(8,128)S(1)}, u32[]{:S(2)}, u32[]{:S(2)}) collective-permute-start(f32[44,5,256]{2,1,0:T(8,128)} %get-tuple-element.15), channel_id=1, source_target_pairs={{0,1},{1,2},{2,3},{3,4},{4,5},{5,6},{6,7},{7,8},{8,9},{9,10},{10,1... | collective-permute-start | bytes 675848 | tf_op jit(solution)/shard_map/ppermute | solution.py:364
  13.7 1.3 collective-permute-start.1
  15.0 6.5 %all-to-all-start = ((f32[8,16,384]{2,1,0:T(8,128)}), f32[8,16,384]{2,1,0:T(8,128)S(1)}, u32[]{:S(2)}, u32[]{:S(2)}) async-start(f32[8,16,384]{2,1,0:T(8,128)} %get-tuple-element.17), calls=%async_computation | async-start | bytes 393216 | tf_op jit(solution)/shard_map/all_to_all | solution.py:366
  21.6 2.1 %constant_dynamic-slice_fusion.2 = f32[4,2,9216]{2,1,0:T(2,128)} fusion(f32[4,32,9216]{2,1,0:T(8,128)} %param.29, s32[]{:T(128)S(6)} %select_n.2), kind=kLoop, calls=%fused_computation.3 | loop fusion | bytes 589828 | tf_op jit(solution)/shard_map/dynamic_slice | solution.py:369
  23.7 11.6 %all-to-all-done = f32[8,16,384]{2,1,0:T(8,128)S(1)} async-done(((f32[8,16,384]{2,1,0:T(8,128)}), f32[8,16,384]{2,1,0:T(8,128)S(1)}, u32[]{:S(2)}, u32[]{:S(2)}) %all-to-all-start) | async-done | bytes 196640 | tf_op jit(solution)/shard_map/all_to_all | solution.py:366
  35.2 0.7 copy-done.2
  36.0 0.7 copy-done.5
  36.7 0.7 copy-done.8
  37.4 0.7 copy-done.11
  38.0 0.7 copy-done.16
  38.8 0.7 copy-done.18
  39.4 1.4 fluid.6
  40.9 3.1 %collective-permute-start.2 = (f32[5,512]{1,0:T(8,128)S(1)}, f32[5,512]{1,0:T(8,128)S(1)}, u32[]{:S(2)}, u32[]{:S(2)}) collective-permute-start(f32[5,512]{1,0:T(8,128)S(1)} %get-tuple-element.18.refs_6_), channel_id=1, source_target_pairs={{0,1},{1,2},{2,3},{3,4},{4,5},{5,6},{6,7},{7,8},{8,9},{9,10},{10,1... | collective-permute-start | bytes 30728 | tf_op jit(solution)/shard_map/ppermute | solution.py:386
  44.0 1.3 collective-permute-start.3
  45.4 0.1 collective-permute-done.2.refs_7_
  45.4 4.2 %collective-permute-done.3.refs_8_ = f32[5,512]{1,0:T(8,128)S(1)} collective-permute-done((f32[5,512]{1,0:T(8,128)S(1)}, f32[5,512]{1,0:T(8,128)S(1)}, u32[]{:S(2)}, u32[]{:S(2)}) %collective-permute-start.3) | collective-permute-done | bytes 10272 | tf_op jit(solution)/shard_map/ppermute | solution.py:386
  49.6 0.5 fluid.7.refs_6_
  50.1 3.3 %collective-permute-start.4 = (f32[5,512]{1,0:T(8,128)S(1)}, f32[5,512]{1,0:T(8,128)S(1)}, u32[]{:S(2)}, u32[]{:S(2)}) collective-permute-start(f32[5,512]{1,0:T(8,128)S(1)} %fluid.7.refs_6_), channel_id=1, source_target_pairs={{0,1},{1,2},{2,3},{3,4},{4,5},{5,6},{6,7},{7,8},{8,9},{9,10},{10,1... | collective-permute-start | bytes 30728 | tf_op jit(solution)/shard_map/ppermute | solution.py:386
  53.4 1.3 collective-permute-start.5
  54.7 0.1 constant_dynamic-slice_fusion.1.columns
  54.8 1.2 reshape.45.blocks
  56.0 0.1 reshape.46.inverse
  56.2 0.1 reshape.44
  56.3 2.8 %collective-permute-done.5.refs_8_ = f32[5,512]{1,0:T(8,128)S(1)} collective-permute-done((f32[5,512]{1,0:T(8,128)S(1)}, f32[5,512]{1,0:T(8,128)S(1)}, u32[]{:S(2)}, u32[]{:S(2)}) %collective-permute-start.5) | collective-permute-done | bytes 10272 | tf_op jit(solution)/shard_map/ppermute | solution.py:386
  59.1 2.0 %fluid.8 = (f32[5,512]{1,0:T(8,128)S(1)}, f32[128,128]{1,0:T(8,128)}) custom-call(f32[30,5,512]{2,1,0:T(8,128)S(1)} %bitcast.21, f32[5,5,512]{2,1,0:T(8,128)S(1)} %get-tuple-element.14.refs_1_, f32[5,512]{1,0:T(8,128)S(1)} %copy-done.3, s32[6,512]{1,0:T(8,128)S(1)} %copy-done.6, f32[44,5,256]{2,1,0:T(8,128)S(1)} %collective-permute-done.refs_4_, ...), custom_call_target="tpu_custom_call" | custom-call | tf_op jit(solution)/shard_map/fluid/pallas_call | solution.py:400
  61.0 16.1 %all-to-all-start.1 = ((f32[128,1,128]{2,1,0:T(1,128)}), f32[128,1,128]{2,1,0:T(1,128)S(1)}, u32[]{:S(2)}, u32[]{:S(2)}) async-start(f32[128,1,128]{2,1,0:T(1,128)} %bitcast.4), calls=%async_computation.1 | async-start | bytes 131072 | tf_op jit(solution)/shard_map/all_to_all | solution.py:409
  77.2 0.8 shell.2
  78.0 8.5 %all-to-all-done.1 = f32[128,1,128]{2,1,0:T(1,128)S(1)} async-done(((f32[128,1,128]{2,1,0:T(1,128)}), f32[128,1,128]{2,1,0:T(1,128)S(1)}, u32[]{:S(2)}, u32[]{:S(2)}) %all-to-all-start.1) | async-done | bytes 65568 | tf_op jit(solution)/shard_map/all_to_all | solution.py:409
  86.5 0.9 solve.2
  87.3 0.9 copy.30
  88.2 4.6 %all-to-all-start.2 = ((f32[128,1,384]{2,1,0:T(1,128)}), f32[128,1,384]{2,1,0:T(1,128)S(1)}, u32[]{:S(2)}, u32[]{:S(2)}) async-start(f32[128,1,384]{2,1,0:T(1,128)} %copy.30), calls=%async_computation.2 | async-start | bytes 393216 | tf_op jit(solution)/shard_map/all_to_all | solution.py:418
  92.8 2.8 %collective-permute-start.6 = (f32[5,512]{1,0:T(8,128)S(1)}, f32[5,512]{1,0:T(8,128)S(1)}, u32[]{:S(2)}, u32[]{:S(2)}) collective-permute-start(f32[5,512]{1,0:T(8,128)S(1)} %get-tuple-element.20.refs_6_), channel_id=1, source_target_pairs={{0,1},{1,2},{2,3},{3,4},{4,5},{5,6},{6,7},{7,8},{8,9},{9,10},{10,1... | collective-permute-start | bytes 30728 | tf_op jit(solution)/shard_map/ppermute | solution.py:386
  95.6 1.3 collective-permute-start.7
  96.9 5.9 %all-to-all-done.2 = f32[128,1,384]{2,1,0:T(1,128)S(1)} async-done(((f32[128,1,384]{2,1,0:T(1,128)}), f32[128,1,384]{2,1,0:T(1,128)S(1)}, u32[]{:S(2)}, u32[]{:S(2)}) %all-to-all-start.2) | async-done | bytes 196640 | tf_op jit(solution)/shard_map/all_to_all | solution.py:418
  102.9 1.4 fluid.9
  104.4 2.6 %collective-permute-start.8 = (f32[5,512]{1,0:T(8,128)S(1)}, f32[5,512]{1,0:T(8,128)S(1)}, u32[]{:S(2)}, u32[]{:S(2)}) collective-permute-start(f32[5,512]{1,0:T(8,128)S(1)} %get-tuple-element.22.refs_6_), channel_id=1, source_target_pairs={{0,1},{1,2},{2,3},{3,4},{4,5},{5,6},{6,7},{7,8},{8,9},{9,10},{10,1... | collective-permute-start | bytes 30728 | tf_op jit(solution)/shard_map/ppermute | solution.py:386
  107.0 1.3 collective-permute-start.9
  108.3 0.1 collective-permute-done.8.refs_7_
  108.4 4.2 %collective-permute-done.9.refs_8_ = f32[5,512]{1,0:T(8,128)S(1)} collective-permute-done((f32[5,512]{1,0:T(8,128)S(1)}, f32[5,512]{1,0:T(8,128)S(1)}, u32[]{:S(2)}, u32[]{:S(2)}) %collective-permute-start.9) | collective-permute-done | bytes 10272 | tf_op jit(solution)/shard_map/ppermute | solution.py:386
  112.6 0.5 fluid.10.refs_6_
  113.1 4.0 %collective-permute-start.10 = (f32[5,512]{1,0:T(8,128)S(1)}, f32[5,512]{1,0:T(8,128)S(1)}, u32[]{:S(2)}, u32[]{:S(2)}) collective-permute-start(f32[5,512]{1,0:T(8,128)S(1)} %fluid.10.refs_6_), channel_id=1, source_target_pairs={{0,1},{1,2},{2,3},{3,4},{4,5},{5,6},{6,7},{7,8},{8,9},{9,10},{10,1... | collective-permute-start | bytes 30728 | tf_op jit(solution)/shard_map/ppermute | solution.py:386
  117.1 1.3 collective-permute-start.11
  118.4 0.1 collective-permute-done.10.refs_7_
  118.5 4.2 %collective-permute-done.11.refs_8_ = f32[5,512]{1,0:T(8,128)S(1)} collective-permute-done((f32[5,512]{1,0:T(8,128)S(1)}, f32[5,512]{1,0:T(8,128)S(1)}, u32[]{:S(2)}, u32[]{:S(2)}) %collective-permute-start.11) | collective-permute-done | bytes 10272 | tf_op jit(solution)/shard_map/ppermute | solution.py:386
  122.7 2.0 %fluid.11 = (f32[5,512]{1,0:T(8,128)}, f32[128,128]{1,0:T(8,128)}) custom-call(f32[30,5,512]{2,1,0:T(8,128)S(1)} %bitcast.24, f32[5,5,512]{2,1,0:T(8,128)S(1)} %get-tuple-element.14.refs_1_, f32[5,512]{1,0:T(8,128)S(1)} %copy-done.3, s32[6,512]{1,0:T(8,128)S(1)} %copy-done.6, f32[44,5,256]{2,1,0:T(8,128)S(1)} %collective-permute-done.refs_4_, ...), custom_call_target="tpu_custom_call" | custom-call | tf_op jit(solution)/shard_map/fluid/pallas_call | solution.py:400
  124.7 15.8 %all-to-all-start.3 = ((f32[128,1,128]{2,1,0:T(1,128)}), f32[128,1,128]{2,1,0:T(1,128)S(1)}, u32[]{:S(2)}, u32[]{:S(2)}) async-start(f32[128,1,128]{2,1,0:T(1,128)} %bitcast.8), calls=%async_computation.3 | async-start | bytes 131072 | tf_op jit(solution)/shard_map/all_to_all | solution.py:409
  140.5 0.8 shell.3
  141.4 8.5 %all-to-all-done.3 = f32[128,1,128]{2,1,0:T(1,128)S(1)} async-done(((f32[128,1,128]{2,1,0:T(1,128)}), f32[128,1,128]{2,1,0:T(1,128)S(1)}, u32[]{:S(2)}, u32[]{:S(2)}) %all-to-all-start.3) | async-done | bytes 65568 | tf_op jit(solution)/shard_map/all_to_all | solution.py:409
  149.8 0.3 solve.3
  150.2 10.9 %all_to_all.47 = f32[16,1,256]{2,1,0:T(1,128)S(1)} all-to-all(f32[16,1,256]{2,1,0:T(1,128)S(1)} %copy.33), channel_id=1, replica_groups=mesh['fluid'=16,'struct'=8] {'fluid'}, dimensions={0} | all-to-all | bytes 32768 | tf_op jit(solution)/shard_map/all_to_all | solution.py:415
  161.1 0.7 reshape.48
  (38 shorter events, 0.2 us)
Async XLA Ops:
  0.6 44.7 %copy-start = (f32[32,9216]{1,0:T(8,128)S(1)}, f32[32,9216]{1,0:T(8,128)}, u32[]{:S(2)}) copy-start(f32[32,9216]{1,0:T(8,128)} %param.30) | copy-start | bytes 3538948
  0.6 58.4 %copy-start.3 = (f32[5,512]{1,0:T(8,128)S(1)}, f32[5,512]{1,0:T(8,128)}, u32[]{:S(2)}) copy-start(f32[5,512]{1,0:T(8,128)} %refs_2_.11) | copy-start | bytes 30724
  0.7 58.4 %copy-start.6 = (s32[6,512]{1,0:T(8,128)S(1)}, s32[6,512]{1,0:T(8,128)}, u32[]{:S(2)}) copy-start(s32[6,512]{1,0:T(8,128)} %refs_3_.11) | copy-start | bytes 36868
  0.7 58.4 %copy-start.9 = (s32[3,256]{1,0:T(4,128)S(1)}, s32[3,256]{1,0:T(4,128)}, u32[]{:S(2)}) copy-start(s32[3,256]{1,0:T(4,128)} %refs_10_.6) | copy-start | bytes 9220
  0.7 58.4 %copy-start.12 = (f32[3,256]{1,0:T(4,128)S(1)}, f32[3,256]{1,0:T(4,128)}, u32[]{:S(2)}) copy-start(f32[3,256]{1,0:T(4,128)} %refs_11_.5) | copy-start | bytes 9220
  0.7 54.0 %copy-start.21 = (s32[4,32]{1,0:T(4,128)S(1)}, s32[4,32]{1,0:T(4,128)}, u32[]{:S(2)}) copy-start(s32[4,32]{1,0:T(4,128)} %param.31) | copy-start | bytes 1540
  0.7 55.5 %copy-start.20 = (f32[3072]{0:T(1024)S(1)}, f32[3072]{0:T(1024)}, u32[]{:S(2)}) copy-start(f32[3072]{0:T(1024)} %param.28) | copy-start | bytes 36868
  0.7 58.4 %copy-start.14 = (f32[5,3,256]{2,1,0:T(4,128)S(1)}, f32[5,3,256]{2,1,0:T(4,128)}, u32[]{:S(2)}) copy-start(f32[5,3,256]{2,1,0:T(4,128)} %refs_14_.4) | copy-start | bytes 46084
  4.2 0.7 copy-start.1
  4.9 0.7 copy-start.4
  5.6 0.7 copy-start.7
  6.3 0.7 copy-start.10
  7.0 0.9 copy-start.13
  7.9 0.7 copy-start.15
  8.6 0.7 copy-start.17
  9.3 93.7 %copy-start.19 = (s32[256]{0:T(256)S(1)}, s32[256]{0:T(256)}, u32[]{:S(2)}) copy-start(s32[256]{0:T(256)} %param.21) | copy-start | bytes 3076
  10.2 25.0 %collective-permute-start = (f32[44,5,256]{2,1,0:T(8,128)}, f32[44,5,256]{2,1,0:T(8,128)S(1)}, u32[]{:S(2)}, u32[]{:S(2)}) collective-permute-start(f32[44,5,256]{2,1,0:T(8,128)} %get-tuple-element.15), channel_id=1, source_target_pairs={{0,1},{1,2},{2,3},{3,4},{4,5},{5,6},{6,7},{7,8},{8,9},{9,10},{10,1... | collective-permute-start | bytes 675848 | tf_op jit(solution)/shard_map/ppermute | solution.py:364
  13.7 21.5 %collective-permute-start.1 = (f32[44,5,256]{2,1,0:T(8,128)S(1)}, f32[44,5,256]{2,1,0:T(8,128)S(1)}, u32[]{:S(2)}, u32[]{:S(2)}) collective-permute-start(f32[44,5,256]{2,1,0:T(8,128)S(1)} %get-tuple-element.16), channel_id=1, source_target_pairs={{1,0},{2,1},{3,2},{4,3},{5,4},{6,5},{7,6},{8,7},{9,8},{10,9},{11,1... | collective-permute-start | bytes 675848 | tf_op jit(solution)/shard_map/ppermute | solution.py:365
  15.0 20.2 %all-to-all-start = ((f32[8,16,384]{2,1,0:T(8,128)}), f32[8,16,384]{2,1,0:T(8,128)S(1)}, u32[]{:S(2)}, u32[]{:S(2)}) async-start(f32[8,16,384]{2,1,0:T(8,128)} %get-tuple-element.17), calls=%async_computation | async-start | bytes 393216 | tf_op jit(solution)/shard_map/all_to_all | solution.py:366
  35.2 0.7 copy-start.2
  36.0 0.7 copy-start.5
  36.7 0.7 copy-start.8
  37.4 0.7 copy-start.11
  38.0 0.7 copy-start.16
  38.8 0.7 copy-start.18
  40.9 4.6 %collective-permute-start.2 = (f32[5,512]{1,0:T(8,128)S(1)}, f32[5,512]{1,0:T(8,128)S(1)}, u32[]{:S(2)}, u32[]{:S(2)}) collective-permute-start(f32[5,512]{1,0:T(8,128)S(1)} %get-tuple-element.18.refs_6_), channel_id=1, source_target_pairs={{0,1},{1,2},{2,3},{3,4},{4,5},{5,6},{6,7},{7,8},{8,9},{9,10},{10,1... | collective-permute-start | bytes 30728 | tf_op jit(solution)/shard_map/ppermute | solution.py:386
  44.0 5.6 %collective-permute-start.3 = (f32[5,512]{1,0:T(8,128)S(1)}, f32[5,512]{1,0:T(8,128)S(1)}, u32[]{:S(2)}, u32[]{:S(2)}) collective-permute-start(f32[5,512]{1,0:T(8,128)S(1)} %get-tuple-element.18.refs_6_), channel_id=1, source_target_pairs={{1,0},{2,1},{3,2},{4,3},{5,4},{6,5},{7,6},{8,7},{9,8},{10,9},{11,1... | collective-permute-start | bytes 30728 | tf_op jit(solution)/shard_map/ppermute | solution.py:386
  50.1 6.1 %collective-permute-start.4 = (f32[5,512]{1,0:T(8,128)S(1)}, f32[5,512]{1,0:T(8,128)S(1)}, u32[]{:S(2)}, u32[]{:S(2)}) collective-permute-start(f32[5,512]{1,0:T(8,128)S(1)} %fluid.7.refs_6_), channel_id=1, source_target_pairs={{0,1},{1,2},{2,3},{3,4},{4,5},{5,6},{6,7},{7,8},{8,9},{9,10},{10,1... | collective-permute-start | bytes 30728 | tf_op jit(solution)/shard_map/ppermute | solution.py:386
  53.4 5.6 %collective-permute-start.5 = (f32[5,512]{1,0:T(8,128)S(1)}, f32[5,512]{1,0:T(8,128)S(1)}, u32[]{:S(2)}, u32[]{:S(2)}) collective-permute-start(f32[5,512]{1,0:T(8,128)S(1)} %fluid.7.refs_6_), channel_id=1, source_target_pairs={{1,0},{2,1},{3,2},{4,3},{5,4},{6,5},{7,6},{8,7},{9,8},{10,9},{11,1... | collective-permute-start | bytes 30728 | tf_op jit(solution)/shard_map/ppermute | solution.py:386
  61.0 25.4 %all-to-all-start.1 = ((f32[128,1,128]{2,1,0:T(1,128)}), f32[128,1,128]{2,1,0:T(1,128)S(1)}, u32[]{:S(2)}, u32[]{:S(2)}) async-start(f32[128,1,128]{2,1,0:T(1,128)} %bitcast.4), calls=%async_computation.1 | async-start | bytes 131072 | tf_op jit(solution)/shard_map/all_to_all | solution.py:409
  88.2 14.7 %all-to-all-start.2 = ((f32[128,1,384]{2,1,0:T(1,128)}), f32[128,1,384]{2,1,0:T(1,128)S(1)}, u32[]{:S(2)}, u32[]{:S(2)}) async-start(f32[128,1,384]{2,1,0:T(1,128)} %copy.30), calls=%async_computation.2 | async-start | bytes 393216 | tf_op jit(solution)/shard_map/all_to_all | solution.py:418
  92.8 10.1 %collective-permute-start.6 = (f32[5,512]{1,0:T(8,128)S(1)}, f32[5,512]{1,0:T(8,128)S(1)}, u32[]{:S(2)}, u32[]{:S(2)}) collective-permute-start(f32[5,512]{1,0:T(8,128)S(1)} %get-tuple-element.20.refs_6_), channel_id=1, source_target_pairs={{0,1},{1,2},{2,3},{3,4},{4,5},{5,6},{6,7},{7,8},{8,9},{9,10},{10,1... | collective-permute-start | bytes 30728 | tf_op jit(solution)/shard_map/ppermute | solution.py:386
  95.6 7.3 %collective-permute-start.7 = (f32[5,512]{1,0:T(8,128)S(1)}, f32[5,512]{1,0:T(8,128)S(1)}, u32[]{:S(2)}, u32[]{:S(2)}) collective-permute-start(f32[5,512]{1,0:T(8,128)S(1)} %get-tuple-element.20.refs_6_), channel_id=1, source_target_pairs={{1,0},{2,1},{3,2},{4,3},{5,4},{6,5},{7,6},{8,7},{9,8},{10,9},{11,1... | collective-permute-start | bytes 30728 | tf_op jit(solution)/shard_map/ppermute | solution.py:386
  104.4 4.0 %collective-permute-start.8 = (f32[5,512]{1,0:T(8,128)S(1)}, f32[5,512]{1,0:T(8,128)S(1)}, u32[]{:S(2)}, u32[]{:S(2)}) collective-permute-start(f32[5,512]{1,0:T(8,128)S(1)} %get-tuple-element.22.refs_6_), channel_id=1, source_target_pairs={{0,1},{1,2},{2,3},{3,4},{4,5},{5,6},{6,7},{7,8},{8,9},{9,10},{10,1... | collective-permute-start | bytes 30728 | tf_op jit(solution)/shard_map/ppermute | solution.py:386
  107.0 5.6 %collective-permute-start.9 = (f32[5,512]{1,0:T(8,128)S(1)}, f32[5,512]{1,0:T(8,128)S(1)}, u32[]{:S(2)}, u32[]{:S(2)}) collective-permute-start(f32[5,512]{1,0:T(8,128)S(1)} %get-tuple-element.22.refs_6_), channel_id=1, source_target_pairs={{1,0},{2,1},{3,2},{4,3},{5,4},{6,5},{7,6},{8,7},{9,8},{10,9},{11,1... | collective-permute-start | bytes 30728 | tf_op jit(solution)/shard_map/ppermute | solution.py:386
  113.1 5.4 %collective-permute-start.10 = (f32[5,512]{1,0:T(8,128)S(1)}, f32[5,512]{1,0:T(8,128)S(1)}, u32[]{:S(2)}, u32[]{:S(2)}) collective-permute-start(f32[5,512]{1,0:T(8,128)S(1)} %fluid.10.refs_6_), channel_id=1, source_target_pairs={{0,1},{1,2},{2,3},{3,4},{4,5},{5,6},{6,7},{7,8},{8,9},{9,10},{10,1... | collective-permute-start | bytes 30728 | tf_op jit(solution)/shard_map/ppermute | solution.py:386
  117.1 5.6 %collective-permute-start.11 = (f32[5,512]{1,0:T(8,128)S(1)}, f32[5,512]{1,0:T(8,128)S(1)}, u32[]{:S(2)}, u32[]{:S(2)}) collective-permute-start(f32[5,512]{1,0:T(8,128)S(1)} %fluid.10.refs_6_), channel_id=1, source_target_pairs={{1,0},{2,1},{3,2},{4,3},{5,4},{6,5},{7,6},{8,7},{9,8},{10,9},{11,1... | collective-permute-start | bytes 30728 | tf_op jit(solution)/shard_map/ppermute | solution.py:386
  124.7 25.1 %all-to-all-start.3 = ((f32[128,1,128]{2,1,0:T(1,128)}), f32[128,1,128]{2,1,0:T(1,128)S(1)}, u32[]{:S(2)}, u32[]{:S(2)}) async-start(f32[128,1,128]{2,1,0:T(1,128)} %bitcast.8), calls=%async_computation.3 | async-start | bytes 131072 | tf_op jit(solution)/shard_map/all_to_all | solution.py:409

commit v2 on v0

v2 whole, which is shorter than its diff:
```python
import functools

import jax
import jax.numpy as jnp
from jax import lax
from jax.experimental import pallas as pl
from jax.experimental.pallas import tpu as pltpu
from jax.sharding import PartitionSpec as P

NVAR = 5
FACES = 6
TMAP = 3
DOF = 6
BLK = 96
NB = 4
CELL = 512
HALF = 256
SURF = 256
LANES = 128
FLUID = 16
STRUCT = 8
DEVS = FLUID * STRUCT
PIECE_NODES = 32
PIECE = PIECE_NODES * 3
BOTH = ("fluid", "struct")
OFFSETS = (-3, -2, -1, 1, 2, 3)
CHUNKS = NVAR * CELL // LANES
SIDE = 5
G_FACE = 0
G_DIAG = 25
G_ALL = 30
R_PLACE = 0
R_RHS = 6
R_STATE = 11
R_OTHER = 16
R_NODE = 21
R_WEIGHT = 24
R_CELL = 27
R_LIVE = 28
R_ALL = 2 * 25

f32 = jnp.float32
bf16 = jnp.bfloat16
NN = (((1,), (0,)), ((), ()))
NT = (((1,), (1,)), ((), ()))


def split(x):
    hi = x.astype(bf16)
    return hi, (x - hi.astype(f32)).astype(bf16)


def split3(x):
    hi = x.astype(bf16)
    rest = x - hi.astype(f32)
    mid = rest.astype(bf16)
    return hi, mid, (rest - mid.astype(f32)).astype(bf16)


def dot(a, b, dims):
    return lax.dot_general(a, b, dims, preferred_element_type=f32)


def iota(shape, axis):
    return lax.broadcasted_iota(jnp.int32, shape, axis)


def one_hot(mask):
    return jnp.where(mask, f32(1.0), f32(0.0)).astype(bf16)


def component_perm(half):
    row, col = iota((PIECE, BLK), 0), iota((PIECE, BLK), 1)
    dof = col % DOF
    return one_hot((dof < 3) & (row == dof * PIECE_NODES + half * 16 + col // DOF))


def live_row(count):
    return jnp.where(iota((1, SURF), 1) < count, f32(1.0), f32(0.0))


def get_row(pack, at, lanes=slice(None)):
    return pack[at // 2, FACES + at % 2:FACES + at % 2 + 1, lanes]


def get_rows(pack, at, count, lanes=slice(None)):
    return jnp.concatenate([get_row(pack, at + i, lanes) for i in range(count)], axis=0)


def spread(part):
    return jnp.concatenate([part, jnp.zeros((part.shape[0], LANES - part.shape[1]), f32)], axis=1)


def components(parts):
    total = None
    for half, part in enumerate(parts):
        perm = component_perm(half)
        for term in split3(part):
            product = dot(term, perm, NT)
            total = product if total is None else total + product
    return total


def by_device(node):
    return ((node >> 5) & 15) * STRUCT + (node >> 9)


def by_piece(node):
    return node >> 5


def start_copies(pairs, sems):
    copies = [pltpu.make_async_copy(s, d, sems.at[i]) for i, (s, d) in enumerate(pairs)]
    for copy in copies:
        copy.start()
    return copies


def pack_kernel(face, diag, rhs, state, load, place, node, weight, cell, adjoint, count,
                own, rows,
                face_v, diag_v, rhs_v, state_v, load_v, place_v, node_v, weight_v, cell_v,
                adjoint_v, own_v, rows_v, sems, out_sems):
    copies = start_copies(
        [(face, face_v), (diag, diag_v), (rhs, rhs_v), (state, state_v), (load, load_v),
         (place, place_v), (node, node_v), (weight, weight_v), (cell, cell_v),
         (adjoint, adjoint_v)], sems)
    for copy in copies:
        copy.wait()
    live = live_row(count[0])
    sent = []
    for half in range(2):
        cols = slice(half * HALF, (half + 1) * HALF)
        other = slice((1 - half) * HALF, (2 - half) * HALF)
        pack = own_v.at[half]

        def put(at, value):
            pack[at // 2, FACES + at % 2:FACES + at % 2 + 1, :] = value

        for u in range(NVAR):
            for v in range(NVAR):
                pack[G_FACE + u * NVAR + v, 0:FACES, :] = face_v[u, v, :, cols]
                pack[G_DIAG + u, v:v + 1, :] = diag_v[v, u:u + 1, cols]
            pack[G_DIAG + u, 5:8, :] = load_v[u]
        shift = iota((1, HALF), 1) // LANES * LANES + half * HALF
        for k in range(FACES):
            put(R_PLACE + k, (place_v[k:k + 1, cols] - shift).astype(f32))
        for v in range(NVAR):
            put(R_RHS + v, rhs_v[v:v + 1, cols])
            put(R_STATE + v, state_v[v:v + 1, cols])
            put(R_OTHER + v, state_v[v:v + 1, other])
        for t in range(TMAP):
            put(R_NODE + t, node_v[t:t + 1, :].astype(f32))
            put(R_WEIGHT + t, weight_v[t:t + 1, :])
        put(R_CELL, cell_v[...].astype(f32))
        put(R_LIVE, live)
        for at in range(R_LIVE + 1, R_ALL):
            put(at, jnp.zeros((1, HALF), f32))
        sent.append(pltpu.make_async_copy(own_v.at[half], own.at[half], out_sems.at[half]))
        sent[-1].start()
    wide = spread(adjoint_v[...])
    for s in range(STRUCT):
        rows_v[s] = wide
    sent.append(pltpu.make_async_copy(rows_v, rows, out_sems.at[2]))
    sent[-1].start()
    for copy in sent:
        copy.wait()


def slots(pack):
    node = get_rows(pack, R_NODE, TMAP).astype(jnp.int32)
    weight = get_rows(pack, R_WEIGHT, TMAP)
    cell = get_row(pack, R_CELL).astype(jnp.int32)
    live = get_row(pack, R_LIVE)
    return node, weight, cell, live


def surface_loads(struct_t, pack, row_of):
    node, weight, cell, live = slots(pack)
    total = [None] * 3
    for t in range(TMAP):
        nodes = node[t:t + 1, :]
        pick = one_hot(iota((DEVS, SURF), 0) == row_of(nodes))
        found = dot(struct_t[0], pick, NN) + dot(struct_t[1], pick, NN)
        gain = jnp.where(iota((PIECE_NODES, SURF), 0) == (nodes & 31), weight[t:t + 1, :], f32(0.0))
        for j in range(3):
            term = found[j * PIECE_NODES:(j + 1) * PIECE_NODES] * gain
            total[j] = term if total[j] is None else total[j] + term
    moved = [jnp.sum(x, axis=0, keepdims=True) * live for x in total]
    shown = []
    for v in range(NVAR):
        term = None
        for j in range(3):
            part = pack[G_DIAG + v, 5 + j:6 + j, :] * moved[j]
            term = part if term is None else term + part
        shown.append(term)
    shown.append(jnp.zeros((8 - NVAR, SURF), f32))
    return split(jnp.concatenate(shown, axis=0))


def fluid_kernel(start, *refs):
    refs = list(refs)
    take = lambda n: [refs.pop(0) for _ in range(n)]
    pack_refs = take(len(PACKS))
    struct_ref, disp_ref = take(2)
    if not start:
        (state_ref,) = take(1)
    out, shares = take(2)
    packs, x0, x1, source, places, struct_v, disp_v, chunks = take(8)
    if not start:
        (state_v,) = take(1)
    (sems,) = take(1)

    side = SIDE
    pairs = [(struct_ref, struct_v)]
    for ref, (at, count) in zip(pack_refs, PACKS):
        pairs.append((ref, packs.at[pl.ds(side + at, count)] if count > 1 else packs.at[side + at]))
    pairs.append((disp_ref, disp_v))
    if not start:
        pairs.append((state_ref, state_v))
    copies = start_copies(pairs, sems)
    for copy in copies:
        copy.wait()

    base = 2 * (side + 1)
    if start:
        for h in range(-side, side + 2):
            wanted = [(h, R_STATE)]
            wanted += [(h - 1, R_OTHER)] * (h == -side) + [(h + 1, R_OTHER)] * (h == side + 1)
            for at, row in wanted:
                for v in range(NVAR):
                    line = get_row(packs.at[side + h], row + v)
                    for c in range(2):
                        x0[base + 2 * at + c, v:v + 1, :] = line[:, c * LANES:(c + 1) * LANES]
    else:
        chunks[...] = struct_v[pl.ds(3, DEVS, stride=4), :]
        for c in range(4):
            x0[base + c, 0:NVAR, :] = state_v[:, c * LANES:(c + 1) * LANES]
            for k, offset in enumerate(OFFSETS):
                row = k * CHUNKS + c * NVAR
                x0[base + 4 * offset + c, 0:NVAR, :] = chunks[row:row + NVAR, :]

    if start:
        parts = [struct_v[pl.ds(half, DEVS, stride=2), :][:, 0:BLK] for half in range(2)]
        struct_t = split(jnp.transpose(spread(components(parts))))
    else:
        struct_t = split(jnp.transpose(struct_v[pl.ds(2, DEVS, stride=4), :]))
    row_of = by_piece if start else by_device
    halves = list(range(-side, side + 2))
    for block in sorted(set(h // 2 for h in halves)):
        present = [h for h in halves if h // 2 == block]
        pack = packs.at[side + present[0]]
        loads = surface_loads(struct_t, pack, row_of)
        cell = get_row(pack, R_CELL).astype(jnp.int32)
        for h in present:
            at = one_hot(iota((HALF, SURF), 0) + (h % 2) * HALF == cell)
            coupled = dot(loads[0], at, NT) + dot(loads[1], at, NT)
            value = coupled[0:NVAR] + get_rows(packs.at[side + h], R_RHS, NVAR)
            place = get_rows(packs.at[side + h], R_PLACE, FACES).astype(jnp.int32)
            for c in range(2):
                lanes = slice(c * LANES, (c + 1) * LANES)
                chunk = 2 * (side + h) + c
                source[chunk, 0:NVAR, :] = value[:, lanes]
                places[chunk, 0:FACES, :] = place[:, lanes]
                places[chunk, FACES:8, :] = jnp.full((8 - FACES, LANES), -1, jnp.int32)

    def sweep_half(x_in, x_out, half, write):
        for c in range(2):
            lanes = slice(c * LANES, (c + 1) * LANES)
            chunk = 2 * half + c
            place = places[chunk]
            lane_of, chunk_of = place & (LANES - 1), place >> 7
            masks = [chunk_of == o for o in range(5)]
            sums = [None] * NVAR
            for u in range(NVAR):
                near = None
                for o in range(5):
                    row = jnp.broadcast_to(x_in[chunk + o, u:u + 1, :], (8, LANES))
                    found = jnp.take_along_axis(row, lane_of, axis=1, mode="promise_in_bounds")
                    near = jnp.where(masks[o], found, f32(0.0) if o == 0 else near)
                for v in range(NVAR):
                    term = packs[half, G_FACE + u * NVAR + v, :, lanes] * near
                    sums[v] = term if sums[v] is None else sums[v] + term
            new = None
            for u in range(NVAR):
                left = source[chunk, u:u + 1, :] - jnp.sum(sums[u], axis=0, keepdims=True)
                term = packs[half, G_DIAG + u, 0:NVAR, lanes] * left
                new = term if new is None else new + term
            write(chunk, new)

    x_in, x_out = x0, x1
    for step in range(SIDE + 1):
        reach = SIDE - step
        done = step == SIDE
        if done:
            def write(chunk, new):
                at = (chunk - 2 * side) * LANES
                out[:, at:at + LANES] = new
        else:
            def write(chunk, new, x_out=x_out):
                x_out[chunk + 2, 0:NVAR, :] = new
        first, end = side - reach, side + 2 + reach
        for half in range(first, end):
            sweep_half(x_in, x_out, half, write)
        x_in, x_out = x_out, x_in

    node, weight, cell, live = slots(packs.at[side])
    at = one_hot(iota((CELL, SURF), 0) == cell)
    hi, lo = split(out[...])
    surface = dot(hi, at, NN) + dot(lo, at, NN)
    sens = None
    for v in range(NVAR):
        term = disp_v[v] * surface[v:v + 1, :]
        sens = term if sens is None else sens + term
    sens = sens * live
    total = None
    for t in range(TMAP):
        nodes = node[t:t + 1, :]
        pick = one_hot(iota((DEVS, SURF), 0) == by_device(nodes))
        gain = jnp.where(iota((PIECE_NODES, SURF), 0) == (nodes & 31),
                         weight[t:t + 1, :], f32(0.0))
        value = jnp.concatenate([gain * sens[j:j + 1, :] for j in range(3)], axis=0)
        for part in split(value):
            term = dot(pick, part, NT)
            total = term if total is None else total + term
    wide = spread(total)
    if not start:
        shares[...] = wide
    else:
        shares[pl.ds(0, DEVS, stride=2), :] = wide
        for k in range(len(OFFSETS)):
            for c in range(4):
                row = k * CHUNKS + c * NVAR
                chunks[row:row + NVAR, :] = out[:, c * LANES:(c + 1) * LANES]
        rest = len(OFFSETS) * CHUNKS
        chunks[rest:DEVS, :] = jnp.zeros((DEVS - rest, LANES), f32)
        shares[pl.ds(1, DEVS, stride=2), :] = chunks[...]


PACKS = ((0, 2), (-2, 2), (2, 2), (-4, 2), (4, 2), (-5, 1), (6, 1))


def fluid(start, packs, struct_rows, disp, state=None):
    args = list(packs) + [struct_rows, disp] + ([] if start else [state])
    halves = 2 * SIDE + 2
    scratch = [
        pltpu.VMEM((halves, G_ALL, 8, HALF), f32),
        pltpu.VMEM((2 * halves + 4, 8, LANES), f32),
        pltpu.VMEM((2 * halves + 4, 8, LANES), f32),
        pltpu.VMEM((2 * halves, 8, LANES), f32),
        pltpu.VMEM((2 * halves, 8, LANES), jnp.int32),
        pltpu.VMEM(struct_rows.shape, f32),
        pltpu.VMEM((NVAR, 3, SURF), f32),
        pltpu.VMEM((DEVS, LANES), f32),
    ]
    if not start:
        scratch.append(pltpu.VMEM((NVAR, CELL), f32))
    scratch.append(pltpu.SemaphoreType.DMA((len(args),)))
    outs = [(NVAR, CELL), (2 * DEVS if start else DEVS, LANES)]
    return call(functools.partial(fluid_kernel, start), "fluid", outs, [ANY] * len(args), scratch, vmem=63)(*args)


def shell_kernel(whole_rows, struct_rows, blocks, columns, out):
    for half in range(2):
        total = jnp.zeros((1, BLK), f32)
        for m in range(NB):
            column = columns[m, half]
            piece = column // 2
            row = (piece % FLUID) * STRUCT + piece // FLUID
            line = column if whole_rows else 4 * row + column % 2
            x = struct_rows[pl.ds(line, 1), :][:, 0:BLK]
            x_hi, x_lo = split(x)
            b_hi, b_lo = split(blocks[m, half])
            total += dot(x_hi, b_hi, NN) + dot(x_lo, b_hi, NN) + dot(x_hi, b_lo, NN)
        out[half:half + 1, :] = total


def solve_kernel(received, rhs, shell, inverse, relay, out, *padded):
    start = bool(padded)
    lines = received[pl.ds(0, DEVS, stride=2), :] if start else received[...]
    parts = split3(jnp.sum(lines, axis=0, keepdims=True)[:, 0:PIECE])
    new = []
    for half in range(2):
        perm = component_perm(half)
        load = dot(parts[0], perm, NN) + dot(parts[1], perm, NN) + dot(parts[2], perm, NN)
        right = rhs[half:half + 1, :] + load - shell[half:half + 1, :]
        r_hi, r_lo = split(right)
        i_hi, i_lo = split(inverse[half])
        new.append(dot(r_hi, i_hi, NT) + dot(r_lo, i_hi, NT) + dot(r_hi, i_lo, NT))
    rows = new + [components(new)] if start else new
    every = 4 if start else 2
    count = out.shape[0] // every
    for j, part in enumerate(rows):
        out[pl.ds(j, count, stride=every), :] = jnp.broadcast_to(spread(part), (count, LANES))
    if start:
        (lined,) = padded
        lined[0:8, :] = jnp.zeros((8, LANES), f32)
        lined[8:8 + DEVS, :] = received[pl.ds(1, DEVS, stride=2), :]
        lined[8 + DEVS:16 + DEVS, :] = jnp.zeros((8, LANES), f32)
        for k, offset in enumerate(OFFSETS):
            @pl.when(relay[0] == k)
            def _():
                out[pl.ds(3, DEVS, stride=4), :] = lined[8 + offset:8 + offset + DEVS, :]

        @pl.when(relay[0] >= len(OFFSETS))
        def _():
            out[pl.ds(3, DEVS, stride=4), :] = jnp.zeros((DEVS, LANES), f32)


VMEM = pl.BlockSpec(memory_space=pltpu.VMEM)
SMEM = pl.BlockSpec(memory_space=pltpu.SMEM)
ANY = pl.BlockSpec(memory_space=pltpu.HBM)


def call(kernel, name, out_shapes, specs, scratch=(), out_specs=None, vmem=16):
    return pl.pallas_call(
        kernel,
        name=name,
        out_shape=[jax.ShapeDtypeStruct(s, f32) for s in out_shapes],
        in_specs=specs,
        out_specs=out_specs or [VMEM] * len(out_shapes),
        scratch_shapes=list(scratch),
        compiler_params=pltpu.CompilerParams(vmem_limit_bytes=vmem * 1024 * 1024),
    )


def body(
    fluid_adjoint,
    fluid_rhs,
    diag_inverse,
    face_blocks,
    face_index,
    surface_cell,
    surface_count,
    transfer_node,
    transfer_weight,
    load_sens,
    disp_sens,
    struct_adjoint,
    struct_rhs,
    shell_blocks,
    shell_inverse,
    shell_columns,
):
    def shift(value, by):
        pairs = [(i, i + by) for i in range(DEVS) if 0 <= i + by < DEVS]
        return lax.ppermute(value, BOTH, pairs)

    sizes = [(NVAR, NVAR, FACES, CELL), (NVAR, NVAR, CELL), (NVAR, CELL), (NVAR, CELL),
             (NVAR, 3, SURF), (FACES, CELL), (TMAP, SURF), (TMAP, SURF), (1, SURF),
             (2 * FLUID, BLK)]
    kinds = [f32] * 5 + [jnp.int32] * 2 + [f32, jnp.int32, f32]
    own_shape = (2, G_ALL, 8, HALF)
    rows_shape = (STRUCT, 2 * FLUID, LANES)
    own, rows = call(
        pack_kernel, "pack", [own_shape, rows_shape], [ANY] * 10 + [SMEM],
        [pltpu.VMEM(s, k) for s, k in zip(sizes, kinds)]
        + [pltpu.VMEM(own_shape, f32), pltpu.VMEM(rows_shape, f32),
           pltpu.SemaphoreType.DMA((10,)), pltpu.SemaphoreType.DMA((3,))],
        [ANY] * 2, vmem=63,
    )(face_blocks.transpose(1, 2, 0, 3), diag_inverse, fluid_rhs, fluid_adjoint,
      load_sens.transpose(1, 0, 2), face_index, transfer_node, transfer_weight,
      surface_cell.reshape(1, SURF), struct_adjoint.reshape(2 * FLUID, BLK), surface_count)
    low = shift(own, 1)
    high = shift(own, -1)
    low_two = shift(own, 2)
    high_two = shift(own, -2)
    struct_rows = lax.all_to_all(rows, "struct", 0, 0, tiled=True).reshape(2 * DEVS, LANES)

    mine = 2 * lax.axis_index("fluid")
    take = lambda a, axis: lax.dynamic_slice_in_dim(a, mine, 2, axis)
    blocks = take(shell_blocks, 1).reshape(NB, 2, BLK, BLK)
    inverse = take(shell_inverse, 0).reshape(2, BLK, BLK)
    columns = take(shell_columns, 1)
    rhs_rows = take(struct_rhs.reshape(2 * FLUID, BLK), 0)

    packs = [own, low, high, low_two, high_two, shift(low[1], 2), shift(high[0], -2)]
    relay = ((lax.axis_index(BOTH)) // CHUNKS).astype(jnp.int32).reshape(1)

    def shell(struct_rows, start):
        (terms,) = call(
            functools.partial(shell_kernel, start), "shell", [(2, BLK)], [VMEM, VMEM, SMEM]
        )(struct_rows, blocks, columns)
        return terms

    def solve(shares, terms, shape, scratch):
        received = lax.all_to_all(shares, BOTH, 0, 0, tiled=True)
        (solved,) = call(solve_kernel, "solve", [shape], [VMEM] * 4 + [SMEM], scratch)(
            received, rhs_rows, terms, inverse, relay)
        return solved

    terms = shell(struct_rows, True)
    state, shares = fluid(True, packs, struct_rows, disp_sens)
    solved = solve(shares, terms, (4 * DEVS, LANES), [pltpu.VMEM((DEVS + 16, LANES), f32)])
    struct_rows = lax.all_to_all(solved, BOTH, 0, 0, tiled=True)
    terms = shell(struct_rows, False)
    state, shares = fluid(False, packs, struct_rows, disp_sens, state)
    solved = solve(shares, terms, (2 * FLUID, LANES), [])
    group = lax.all_to_all(solved, "fluid", 0, 0, tiled=True)
    return (state, group[:, 0:BLK].reshape(-1))


def solution(mesh):
    placed = (
        P(None, ("fluid", "struct")),
        P(None, ("fluid", "struct")),
        P(None, None, ("fluid", "struct")),
        P(None, None, None, ("fluid", "struct")),
        P(None, ("fluid", "struct")),
        P(("fluid", "struct")),
        P(("fluid", "struct")),
        P(None, ("fluid", "struct")),
        P(None, ("fluid", "struct")),
        P(None, None, ("fluid", "struct")),
        P(None, None, ("fluid", "struct")),
        P("struct"),
        P("struct"),
        P(None, "struct", None),
        P("struct", None),
        P(None, "struct"),
    )
    return jax.shard_map(
        body,
        mesh=mesh,
        in_specs=placed,
        out_specs=(P(None, ("fluid", "struct")), P("struct")),
        check_vma=False,
    )
```

time: 636 us -> 132 us (0.21); the launches traced: 626 us -> 130 us
  waiting for transfers between devices: 184 us -> 16.1 us
  blocking collectives: 189 us -> 26.3 us
  matrix products: 84.6 us -> 0 us
  loops' own time: 46.8 us -> 0 us
  local copies, waits for them, and re-layouts: 46.1 us -> 10.7 us
  Pallas kernels: 0 us -> 19.3 us
  between operations: 16.9 us -> 1.5 us
    unnamed x4 -> x0, waiting for transfers between devices: 150 us -> none
    psum x2 -> x0, blocking collectives: 130 us -> none  [body(): forces = lax.psum(summed_share, 'fluid')]
    dot_general x36 -> x0, matrix products: 75.5 us -> none  [the longest x24 37.9 us: neighbour_block(): return jnp.einsum('uw,kwc->ukc', piece, selector, precision=highest)]
    all_gather x2 -> x0, blocking collectives: 59.3 us -> none  [body(): group_adjoint = lax.all_gather(struct_state, 'struct', axis=0, tiled=True)]
    another operation x12 -> x0, loops' own time: 46.8 us -> none  [body(): blocks_out = lax.map(neighbour_block, (block_starts, face_local))]
    ppermute x24 -> x6, waiting for transfers between devices: 33.3 us -> 1.4 us  [shift(): return lax.ppermute(value, BOTH, pairs)]
    ppermute x24 -> x6, starting transfers between devices: 56.9 us -> 25.6 us  [shift(): return lax.ppermute(value, BOTH, pairs)]
    all_to_all x0 -> x3, starting transfers between devices: none -> 30.7 us  [the longest x2 22.6 us: solve(): received = lax.all_to_all(shares, BOTH, 0, 0, tiled=True)]
  transfers between devices with their start and end apart: 26 -> 9, of which waited for: 10 -> 5; matrix products, arithmetic and copies ran while one was open for 8% -> 3% of each run, Pallas kernels for 0% -> 1%
where the time goes in v2:
time: 132 us; the launch traced here: 130 us
  starting transfers between devices  56.3 us (43%)
  blocking collectives  26.3 us (20%)
  Pallas kernels  19.3 us (15%)
  waiting for transfers between devices  16.1 us (12%)
  local copies, waits for them, and re-layouts  10.7 us (8%)
  between operations  1.5 us (1%)
    ppermute x6, starting transfers between devices, shift(): return lax.ppermute(value, BOTH, pairs)  25.6 us
    all_to_all x2, starting transfers between devices, solve(): received = lax.all_to_all(shares, BOTH, 0, 0, tiled=True)  22.6 us
    all_to_all x1, blocking collectives, body(): struct_rows = lax.all_to_all(solved, BOTH, 0, 0, tiled=True)  15.4 us
    all_to_all x2, waiting for transfers between devices, solve(): received = lax.all_to_all(shares, BOTH, 0, 0, tiled=True)  14.7 us
    pallas_call x2, Pallas kernels, fluid(): call(functools.partial(fluid_kernel, start), 'fluid', outs, [ANY] * len(a...  14.6 us
    all_to_all x1, blocking collectives, body(): group = lax.all_to_all(solved, 'fluid', 0, 0, tiled=True)  10.9 us
    all_to_all x1, starting transfers between devices, body(): lax.all_to_all(rows, 'struct', 0, 0, tiled=True).reshape(2 * DEVS, LANES)  8.02 us
    unnamed x20, local copies, waits for them, and re-layouts  4.18 us
  transfers between devices with their start and end apart: 9, of which 5 were waited for; matrix products, arithmetic and copies ran while one was open for 3% of the time, Pallas kernels for 1%

profile of v2, /device:TPU:0, one launch (start us, length us, event | category | flops | bytes accessed | tf_op | source)
XLA Modules:
  0.0 130.1 jit_solution(4938447030208283005)
XLA Ops:
  0.6 0.0 copy-start
  1.3 1.4 %reshape.37.adjoint = f32[32,96]{1,0:T(8,128)} reshape(f32[3072]{0:T(1024)} %param.27) | data formatting | bytes 24576 | tf_op jit(solution)/shard_map/reshape | solution.py:462
  2.7 2.0 %pack.1 = (f32[2,30,8,256]{3,2,1,0:T(8,128)}, f32[8,32,128]{2,1,0:T(8,128)}) custom-call(f32[5,5,6,512]{3,2,1,0:T(8,128)} %bitcast.28, f32[5,5,512]{2,1,0:T(8,128)} %diag.1, f32[5,512]{1,0:T(8,128)} %rhs.1, f32[5,512]{1,0:T(8,128)} %state.1, f32[5,3,256]{2,1,0:T(4,128)} %bitcast.32, s32[6,512]{1,0:T(8,128)} %place.1, s32[3,256]{1,0:T(4,128)} %node.1, ...), custom_call_target="tpu_custom_call" | custom-call | tf_op jit(solution)/shard_map/pack/pallas_call | solution.py:454
  4.7 1.3 collective-permute-start.3
  6.0 4.6 %collective-permute-start.2 = (f32[2,30,8,256]{3,2,1,0:T(8,128)}, f32[2,30,8,256]{3,2,1,0:T(8,128)S(1)}, u32[]{:S(2)}, u32[]{:S(2)}) collective-permute-start(f32[2,30,8,256]{3,2,1,0:T(8,128)} %get-tuple-element.8.refs_0_), channel_id=1, source_target_pairs={{0,2},{1,3},{2,4},{3,5},{4,6},{5,7},{6,8},{7,9},{8,10},{9,11},{10,... | collective-permute-start | bytes 1474568 | tf_op jit(solution)/shard_map/ppermute | solution.py:446
  10.6 1.3 collective-permute-start.1
  11.9 4.6 %collective-permute-start = (f32[2,30,8,256]{3,2,1,0:T(8,128)}, f32[2,30,8,256]{3,2,1,0:T(8,128)S(1)}, u32[]{:S(2)}, u32[]{:S(2)}) collective-permute-start(f32[2,30,8,256]{3,2,1,0:T(8,128)} %get-tuple-element.8.refs_0_), channel_id=1, source_target_pairs={{0,1},{1,2},{2,3},{3,4},{4,5},{5,6},{6,7},{7,8},{8,9},{9,10},{10,1... | collective-permute-start | bytes 1474568 | tf_op jit(solution)/shard_map/ppermute | solution.py:446
  16.5 8.0 %all-to-all-start = ((f32[8,32,128]{2,1,0:T(8,128)}), f32[8,32,128]{2,1,0:T(8,128)S(1)}, u32[]{:S(2)}, u32[]{:S(2)}) async-start(f32[8,32,128]{2,1,0:T(8,128)} %get-tuple-element.9), calls=%async_computation | async-start | bytes 262144 | tf_op jit(solution)/shard_map/all_to_all | solution.py:467
  24.5 1.4 %constant_dynamic-slice_fusion.2 = f32[4,2,9216]{2,1,0:T(2,128)S(1)} fusion(f32[4,32,9216]{2,1,0:T(8,128)} %param.29, s32[]{:T(128)S(6)} %select_n.11), kind=kLoop, calls=%fused_computation.4 | loop fusion | bytes 589828 | tf_op jit(solution)/shard_map/dynamic_slice | solution.py:470
  25.9 0.7 collective-permute-done.1.refs_2_
  26.6 0.0 copy-start.4
  26.6 1.3 collective-permute-start.5
  27.9 0.1 collective-permute-done.refs_1_
  28.0 0.0 copy-start.5
  28.0 0.8 slice_bitcast_fusion.1
  28.8 12.6 %collective-permute-start.4 = (f32[30,8,256]{2,1,0:T(8,128)}, f32[30,8,256]{2,1,0:T(8,128)S(1)}, u32[]{:S(2)}, u32[]{:S(2)}) collective-permute-start(f32[30,8,256]{2,1,0:T(8,128)} %slice_bitcast_fusion.1), channel_id=1, source_target_pairs={{0,2},{1,3},{2,4},{3,5},{4,6},{5,7},{6,8},{7,9},{8,10},{9,11},{10,... | collective-permute-start | bytes 737288 | tf_op jit(solution)/shard_map/ppermute | solution.py:446
  41.4 1.0 constant_dynamic-slice_fusion
  42.4 0.8 reshape.39
  43.2 0.0 all-to-all-done
  43.2 0.0 copy-done.4
  43.2 0.0 copy-start.2
  43.2 0.0 collective-permute-done.3.refs_4_
  43.2 0.0 copy-done.5
  43.2 0.0 copy-start.6
  43.2 0.0 collective-permute-done.2.refs_3_
  43.2 0.8 copy-done.6
  44.0 0.0 copy-start.7
  44.0 0.0 collective-permute-done.5.refs_6_
  44.0 0.8 copy-done.7
  44.8 0.0 copy-start.8
  44.8 0.6 collective-permute-done.4.refs_5_
  45.4 0.0 copy-start.9
  45.4 0.7 copy-done.9
  46.1 0.0 copy-done.2
  46.1 0.0 copy-done.8
  46.1 7.5 %fluid.2 = (f32[5,512]{1,0:T(8,128)}, f32[256,128]{1,0:T(8,128)}) custom-call(f32[2,30,8,256]{3,2,1,0:T(8,128)} %get-tuple-element.8.refs_0_, f32[2,30,8,256]{3,2,1,0:T(8,128)} %copy-done.5, f32[2,30,8,256]{3,2,1,0:T(8,128)} %copy-done.4, f32[2,30,8,256]{3,2,1,0:T(8,128)} %copy-done.7, f32[2,30,8,256]{3,2,1,0:T(8,128)} %copy-done.6, ...), custom_call_target="tpu_custom_call" | custom-call | tf_op jit(solution)/shard_map/fluid/pallas_call | solution.py:359
  53.6 18.1 %all-to-all-start.1 = ((f32[128,2,128]{2,1,0:T(2,128)}), f32[128,2,128]{2,1,0:T(2,128)S(1)}, u32[]{:S(2)}, u32[]{:S(2)}) async-start(f32[128,2,128]{2,1,0:T(2,128)} %bitcast.29), calls=%async_computation.1 | async-start | bytes 262144 | tf_op jit(solution)/shard_map/all_to_all | solution.py:486
  71.7 0.1 reshape.41.inverse
  71.9 0.3 reshape.40.blocks
  72.2 0.0 copy-done
  72.2 0.1 constant_dynamic-slice_fusion.1.columns
  72.2 0.0 copy-start.3
  72.2 0.9 copy-done.3
  73.1 0.8 shell.2
  74.0 7.1 %all-to-all-done.1 = f32[128,2,128]{2,1,0:T(2,128)S(1)} async-done(((f32[128,2,128]{2,1,0:T(2,128)}), f32[128,2,128]{2,1,0:T(2,128)S(1)}, u32[]{:S(2)}, u32[]{:S(2)}) %all-to-all-start.1) | async-done | bytes 131104 | tf_op jit(solution)/shard_map/all_to_all | solution.py:486
  81.1 0.7 solve.2
  81.8 15.4 %all_to_all.50 = f32[128,4,128]{2,1,0:T(4,128)} all-to-all(f32[128,4,128]{2,1,0:T(4,128)S(1)} %bitcast.24), channel_id=1, replica_groups=mesh['fluid'=16,'struct'=8] {'fluid','struct'}, dimensions={0} | all-to-all | bytes 524288 | tf_op jit(solution)/shard_map/all_to_all | solution.py:494
  97.2 7.1 %fluid.3 = (f32[5,512]{1,0:T(8,128)}, f32[128,128]{1,0:T(8,128)}) custom-call(f32[2,30,8,256]{3,2,1,0:T(8,128)} %get-tuple-element.8.refs_0_, f32[2,30,8,256]{3,2,1,0:T(8,128)} %copy-done.5, f32[2,30,8,256]{3,2,1,0:T(8,128)} %copy-done.4, f32[2,30,8,256]{3,2,1,0:T(8,128)} %copy-done.7, f32[2,30,8,256]{3,2,1,0:T(8,128)} %copy-done.6, ...), custom_call_target="tpu_custom_call" | custom-call | tf_op jit(solution)/shard_map/fluid/pallas_call | solution.py:359
  104.3 4.6 %all-to-all-start.3 = ((f32[128,1,128]{2,1,0:T(1,128)}), f32[128,1,128]{2,1,0:T(1,128)S(1)}, u32[]{:S(2)}, u32[]{:S(2)}) async-start(f32[128,1,128]{2,1,0:T(1,128)} %bitcast.31), calls=%async_computation.3 | async-start | bytes 131072 | tf_op jit(solution)/shard_map/all_to_all | solution.py:486
  108.9 0.0 copy-start.1
  108.9 0.9 copy-done.1
  109.8 0.8 shell.3
  110.7 7.5 %all-to-all-done.3 = f32[128,1,128]{2,1,0:T(1,128)S(1)} async-done(((f32[128,1,128]{2,1,0:T(1,128)}), f32[128,1,128]{2,1,0:T(1,128)S(1)}, u32[]{:S(2)}, u32[]{:S(2)}) %all-to-all-start.3) | async-done | bytes 65568 | tf_op jit(solution)/shard_map/all_to_all | solution.py:486
  118.2 0.3 solve.3
  118.5 10.9 %all_to_all.51 = f32[16,2,128]{2,1,0:T(2,128)S(1)} all-to-all(f32[16,2,128]{2,1,0:T(2,128)S(1)} %bitcast.27), channel_id=1, replica_groups=mesh['fluid'=16,'struct'=8] {'fluid'}, dimensions={0} | all-to-all | bytes 32768 | tf_op jit(solution)/shard_map/all_to_all | solution.py:498
  129.4 0.7 reshape.43
  (2 shorter events, 0.0 us)
Async XLA Ops:
  0.6 71.5 %copy-start = (s32[4,32]{1,0:T(4,128)S(1)}, s32[4,32]{1,0:T(4,128)}, u32[]{:S(2)}) copy-start(s32[4,32]{1,0:T(4,128)} %param.31) | copy-start | bytes 1540
  4.7 38.5 %collective-permute-start.3 = (f32[2,30,8,256]{3,2,1,0:T(8,128)}, f32[2,30,8,256]{3,2,1,0:T(8,128)S(1)}, u32[]{:S(2)}, u32[]{:S(2)}) collective-permute-start(f32[2,30,8,256]{3,2,1,0:T(8,128)} %get-tuple-element.8.refs_0_), channel_id=1, source_target_pairs={{2,0},{3,1},{4,2},{5,3},{6,4},{7,5},{8,6},{9,7},{10,8},{11,9},{12,... | collective-permute-start | bytes 1474568 | tf_op jit(solution)/shard_map/ppermute | solution.py:446
  6.0 37.2 %collective-permute-start.2 = (f32[2,30,8,256]{3,2,1,0:T(8,128)}, f32[2,30,8,256]{3,2,1,0:T(8,128)S(1)}, u32[]{:S(2)}, u32[]{:S(2)}) collective-permute-start(f32[2,30,8,256]{3,2,1,0:T(8,128)} %get-tuple-element.8.refs_0_), channel_id=1, source_target_pairs={{0,2},{1,3},{2,4},{3,5},{4,6},{5,7},{6,8},{7,9},{8,10},{9,11},{10,... | collective-permute-start | bytes 1474568 | tf_op jit(solution)/shard_map/ppermute | solution.py:446
  10.6 16.0 %collective-permute-start.1 = (f32[2,30,8,256]{3,2,1,0:T(8,128)}, f32[2,30,8,256]{3,2,1,0:T(8,128)S(1)}, u32[]{:S(2)}, u32[]{:S(2)}) collective-permute-start(f32[2,30,8,256]{3,2,1,0:T(8,128)} %get-tuple-element.8.refs_0_), channel_id=1, source_target_pairs={{1,0},{2,1},{3,2},{4,3},{5,4},{6,5},{7,6},{8,7},{9,8},{10,9},{11,1... | collective-permute-start | bytes 1474568 | tf_op jit(solution)/shard_map/ppermute | solution.py:446
  11.9 16.1 %collective-permute-start = (f32[2,30,8,256]{3,2,1,0:T(8,128)}, f32[2,30,8,256]{3,2,1,0:T(8,128)S(1)}, u32[]{:S(2)}, u32[]{:S(2)}) collective-permute-start(f32[2,30,8,256]{3,2,1,0:T(8,128)} %get-tuple-element.8.refs_0_), channel_id=1, source_target_pairs={{0,1},{1,2},{2,3},{3,4},{4,5},{5,6},{6,7},{7,8},{8,9},{9,10},{10,1... | collective-permute-start | bytes 1474568 | tf_op jit(solution)/shard_map/ppermute | solution.py:446
  16.5 26.7 %all-to-all-start = ((f32[8,32,128]{2,1,0:T(8,128)}), f32[8,32,128]{2,1,0:T(8,128)S(1)}, u32[]{:S(2)}, u32[]{:S(2)}) async-start(f32[8,32,128]{2,1,0:T(8,128)} %get-tuple-element.9), calls=%async_computation | async-start | bytes 262144 | tf_op jit(solution)/shard_map/all_to_all | solution.py:467
  26.6 16.6 %copy-start.4 = (f32[2,30,8,256]{3,2,1,0:T(8,128)}, f32[2,30,8,256]{3,2,1,0:T(8,128)S(1)}, u32[]{:S(2)}) copy-start(f32[2,30,8,256]{3,2,1,0:T(8,128)S(1)} %collective-permute-done.1.refs_2_) | copy-start | bytes 1474564
  26.6 17.4 %collective-permute-start.5 = (f32[30,8,256]{2,1,0:T(8,128)S(1)}, f32[30,8,256]{2,1,0:T(8,128)S(1)}, u32[]{:S(2)}, u32[]{:S(2)}) collective-permute-start(f32[30,8,256]{2,1,0:T(8,128)S(1)} %slice_bitcast_fusion), channel_id=1, source_target_pairs={{2,0},{3,1},{4,2},{5,3},{6,4},{7,5},{8,6},{9,7},{10,8},{11,9},{12,... | collective-permute-start | bytes 737288 | tf_op jit(solution)/shard_map/ppermute | solution.py:446
  28.0 15.2 %copy-start.5 = (f32[2,30,8,256]{3,2,1,0:T(8,128)}, f32[2,30,8,256]{3,2,1,0:T(8,128)S(1)}, u32[]{:S(2)}) copy-start(f32[2,30,8,256]{3,2,1,0:T(8,128)S(1)} %collective-permute-done.refs_1_) | copy-start | bytes 1474564
  28.8 16.6 %collective-permute-start.4 = (f32[30,8,256]{2,1,0:T(8,128)}, f32[30,8,256]{2,1,0:T(8,128)S(1)}, u32[]{:S(2)}, u32[]{:S(2)}) collective-permute-start(f32[30,8,256]{2,1,0:T(8,128)} %slice_bitcast_fusion.1), channel_id=1, source_target_pairs={{0,2},{1,3},{2,4},{3,5},{4,6},{5,7},{6,8},{7,9},{8,10},{9,11},{10,... | collective-permute-start | bytes 737288 | tf_op jit(solution)/shard_map/ppermute | solution.py:446
  43.2 2.9 %copy-start.2 = (f32[8,32,128]{2,1,0:T(8,128)}, f32[8,32,128]{2,1,0:T(8,128)S(1)}, u32[]{:S(2)}) copy-start(f32[8,32,128]{2,1,0:T(8,128)S(1)} %all-to-all-done) | copy-start | bytes 393220
  43.2 0.8 copy-start.6
  44.0 0.8 copy-start.7
  44.8 1.3 copy-start.8
  45.4 0.7 copy-start.9
  53.6 27.5 %all-to-all-start.1 = ((f32[128,2,128]{2,1,0:T(2,128)}), f32[128,2,128]{2,1,0:T(2,128)S(1)}, u32[]{:S(2)}, u32[]{:S(2)}) async-start(f32[128,2,128]{2,1,0:T(2,128)} %bitcast.29), calls=%async_computation.1 | async-start | bytes 262144 | tf_op jit(solution)/shard_map/all_to_all | solution.py:486
  72.2 0.9 copy-start.3
  104.3 13.9 %all-to-all-start.3 = ((f32[128,1,128]{2,1,0:T(1,128)}), f32[128,1,128]{2,1,0:T(1,128)S(1)}, u32[]{:S(2)}, u32[]{:S(2)}) async-start(f32[128,1,128]{2,1,0:T(1,128)} %bitcast.31), calls=%async_computation.3 | async-start | bytes 131072 | tf_op jit(solution)/shard_map/all_to_all | solution.py:486
  108.9 1.0 copy-start.1

commit v3 on v2

--- a/solution.py
+++ b/solution.py
@@ -37,6 +37,7 @@
 R_WEIGHT = 24
 R_CELL = 27
 R_LIVE = 28
+R_DISP = 29
 R_ALL = 2 * 25
 
 f32 = jnp.float32
@@ -55,6 +56,15 @@
     rest = x - hi.astype(f32)
     mid = rest.astype(bf16)
     return hi, mid, (rest - mid.astype(f32)).astype(bf16)
+
+
+def stack(x):
+    return jnp.concatenate([x_half.astype(f32) for x_half in split(x)], axis=0).astype(bf16)
+
+
+def fold(product):
+    rows = product.shape[0] // 2
+    return product[0:rows] + product[rows:2 * rows]
 
 
 def dot(a, b, dims):
@@ -116,14 +126,14 @@
     return copies
 
 
-def pack_kernel(face, diag, rhs, state, load, place, node, weight, cell, adjoint, count,
-                own, rows,
+def pack_kernel(face, diag, rhs, state, load, place, node, weight, cell, disp, count,
+                own,
                 face_v, diag_v, rhs_v, state_v, load_v, place_v, node_v, weight_v, cell_v,
-                adjoint_v, own_v, rows_v, sems, out_sems):
+                disp_v, own_v, sems, out_sems):
     copies = start_copies(
         [(face, face_v), (diag, diag_v), (rhs, rhs_v), (state, state_v), (load, load_v),
          (place, place_v), (node, node_v), (weight, weight_v), (cell, cell_v),
-         (adjoint, adjoint_v)], sems)
+         (disp, disp_v)], sems)
     for copy in copies:
         copy.wait()
     live = live_row(count[0])
@@ -153,15 +163,13 @@
             put(R_WEIGHT + t, weight_v[t:t + 1, :])
         put(R_CELL, cell_v[...].astype(f32))
         put(R_LIVE, live)
-        for at in range(R_LIVE + 1, R_ALL):
+        for v in range(NVAR):
+            for j in range(3):
+                put(R_DISP + 3 * v + j, disp_v[v, j:j + 1, :])
+        for at in range(R_DISP + 3 * NVAR, R_ALL):
             put(at, jnp.zeros((1, HALF), f32))
         sent.append(pltpu.make_async_copy(own_v.at[half], own.at[half], out_sems.at[half]))
         sent[-1].start()
-    wide = spread(adjoint_v[...])
-    for s in range(STRUCT):
-        rows_v[s] = wide
-    sent.append(pltpu.make_async_copy(rows_v, rows, out_sems.at[2]))
-    sent[-1].start()
     for copy in sent:
         copy.wait()
 
@@ -180,7 +188,7 @@
     for t in range(TMAP):
         nodes = node[t:t + 1, :]
         pick = one_hot(iota((DEVS, SURF), 0) == row_of(nodes))
-        found = dot(struct_t[0], pick, NN) + dot(struct_t[1], pick, NN)
+        found = fold(dot(struct_t, pick, NN))
         gain = jnp.where(iota((PIECE_NODES, SURF), 0) == (nodes & 31), weight[t:t + 1, :], f32(0.0))
         for j in range(3):
             term = found[j * PIECE_NODES:(j + 1) * PIECE_NODES] * gain
@@ -194,44 +202,27 @@
             term = part if term is None else term + part
         shown.append(term)
     shown.append(jnp.zeros((8 - NVAR, SURF), f32))
-    return split(jnp.concatenate(shown, axis=0))
+    return stack(jnp.concatenate(shown, axis=0))
 
 
 def fluid_kernel(start, *refs):
     refs = list(refs)
     take = lambda n: [refs.pop(0) for _ in range(n)]
     pack_refs = take(len(PACKS))
-    struct_ref, disp_ref = take(2)
-    if not start:
-        (state_ref,) = take(1)
-    out, shares = take(2)
-    packs, x0, x1, source, places, struct_v, disp_v, chunks = take(8)
+    (struct_v,) = take(1)
     if not start:
         (state_v,) = take(1)
-    (sems,) = take(1)
+    out, shares = take(2)
+    x0, x1, source, places, chunks = take(5)
 
     side = SIDE
-    pairs = [(struct_ref, struct_v)]
+    packs = {}
     for ref, (at, count) in zip(pack_refs, PACKS):
-        pairs.append((ref, packs.at[pl.ds(side + at, count)] if count > 1 else packs.at[side + at]))
-    pairs.append((disp_ref, disp_v))
+        for i in range(count):
+            packs[side + at + i] = ref.at[i] if count > 1 else ref
+
+    base = 2 * (side + 1)
     if not start:
-        pairs.append((state_ref, state_v))
-    copies = start_copies(pairs, sems)
-    for copy in copies:
-        copy.wait()
-
-    base = 2 * (side + 1)
-    if start:
-        for h in range(-side, side + 2):
-            wanted = [(h, R_STATE)]
-            wanted += [(h - 1, R_OTHER)] * (h == -side) + [(h + 1, R_OTHER)] * (h == side + 1)
-            for at, row in wanted:
-                for v in range(NVAR):
-                    line = get_row(packs.at[side + h], row + v)
-                    for c in range(2):
-                        x0[base + 2 * at + c, v:v + 1, :] = line[:, c * LANES:(c + 1) * LANES]
-    else:
         chunks[...] = struct_v[pl.ds(3, DEVS, stride=4), :]
         for c in range(4):
             x0[base + c, 0:NVAR, :] = state_v[:, c * LANES:(c + 1) * LANES]
@@ -241,27 +232,34 @@
 
     if start:
         parts = [struct_v[pl.ds(half, DEVS, stride=2), :][:, 0:BLK] for half in range(2)]
-        struct_t = split(jnp.transpose(spread(components(parts))))
+        struct_t = stack(jnp.transpose(spread(components(parts))))
     else:
-        struct_t = split(jnp.transpose(struct_v[pl.ds(2, DEVS, stride=4), :]))
+        struct_t = stack(jnp.transpose(struct_v[pl.ds(2, DEVS, stride=4), :]))
     row_of = by_piece if start else by_device
-    halves = list(range(-side, side + 2))
-    for block in sorted(set(h // 2 for h in halves)):
-        present = [h for h in halves if h // 2 == block]
-        pack = packs.at[side + present[0]]
+    for which, (begin, count) in enumerate(PACKS):
+        present = list(range(begin, begin + count))
+        pack = packs[side + present[0]]
         loads = surface_loads(struct_t, pack, row_of)
         cell = get_row(pack, R_CELL).astype(jnp.int32)
         for h in present:
             at = one_hot(iota((HALF, SURF), 0) + (h % 2) * HALF == cell)
-            coupled = dot(loads[0], at, NT) + dot(loads[1], at, NT)
-            value = coupled[0:NVAR] + get_rows(packs.at[side + h], R_RHS, NVAR)
-            place = get_rows(packs.at[side + h], R_PLACE, FACES).astype(jnp.int32)
+            coupled = fold(dot(loads, at, NT))
+            value = coupled[0:NVAR] + get_rows(packs[side + h], R_RHS, NVAR)
+            place = get_rows(packs[side + h], R_PLACE, FACES).astype(jnp.int32)
             for c in range(2):
                 lanes = slice(c * LANES, (c + 1) * LANES)
                 chunk = 2 * (side + h) + c
                 source[chunk, 0:NVAR, :] = value[:, lanes]
                 places[chunk, 0:FACES, :] = place[:, lanes]
                 places[chunk, FACES:8, :] = jnp.full((8 - FACES, LANES), -1, jnp.int32)
+            if start:
+                wanted = [(h, R_STATE)]
+                wanted += [(h - 1, R_OTHER)] * (h == -side)
+                wanted += [(h + 1, R_OTHER)] * (h == side + 1)
+                for to, row in wanted:
+                    lines = get_rows(packs[side + h], row, NVAR)
+                    for c in range(2):
+                        x0[base + 2 * to + c, 0:NVAR, :] = lines[:, c * LANES:(c + 1) * LANES]
 
     def sweep_half(x_in, x_out, half, write):
         for c in range(2):
@@ -278,12 +276,12 @@
                     found = jnp.take_along_axis(row, lane_of, axis=1, mode="promise_in_bounds")
                     near = jnp.where(masks[o], found, f32(0.0) if o == 0 else near)
                 for v in range(NVAR):
-                    term = packs[half, G_FACE + u * NVAR + v, :, lanes] * near
+                    term = packs[half][G_FACE + u * NVAR + v, :, lanes] * near
                     sums[v] = term if sums[v] is None else sums[v] + term
             new = None
             for u in range(NVAR):
                 left = source[chunk, u:u + 1, :] - jnp.sum(sums[u], axis=0, keepdims=True)
-                term = packs[half, G_DIAG + u, 0:NVAR, lanes] * left
+                term = packs[half][G_DIAG + u, 0:NVAR, lanes] * left
                 new = term if new is None else new + term
             write(chunk, new)
 
@@ -303,13 +301,13 @@
             sweep_half(x_in, x_out, half, write)
         x_in, x_out = x_out, x_in
 
-    node, weight, cell, live = slots(packs.at[side])
+    node, weight, cell, live = slots(packs[side])
     at = one_hot(iota((CELL, SURF), 0) == cell)
-    hi, lo = split(out[...])
-    surface = dot(hi, at, NN) + dot(lo, at, NN)
+    state = jnp.concatenate([out[...], jnp.zeros((8 - NVAR, CELL), f32)], axis=0)
+    surface = fold(dot(stack(state), at, NN))
     sens = None
     for v in range(NVAR):
-        term = disp_v[v] * surface[v:v + 1, :]
+        term = get_rows(packs[side], R_DISP + 3 * v, 3) * surface[v:v + 1, :]
         sens = term if sens is None else sens + term
     sens = sens * live
     total = None
@@ -319,10 +317,9 @@
         gain = jnp.where(iota((PIECE_NODES, SURF), 0) == (nodes & 31),
                          weight[t:t + 1, :], f32(0.0))
         value = jnp.concatenate([gain * sens[j:j + 1, :] for j in range(3)], axis=0)
-        for part in split(value):
-            term = dot(pick, part, NT)
-            total = term if total is None else total + term
-    wide = spread(total)
+        term = dot(pick, stack(value), NT)
+        total = term if total is None else total + term
+    wide = spread(total[:, 0:PIECE] + total[:, PIECE:2 * PIECE])
     if not start:
         shares[...] = wide
     else:
@@ -339,24 +336,18 @@
 PACKS = ((0, 2), (-2, 2), (2, 2), (-4, 2), (4, 2), (-5, 1), (6, 1))
 
 
-def fluid(start, packs, struct_rows, disp, state=None):
-    args = list(packs) + [struct_rows, disp] + ([] if start else [state])
+def fluid(start, packs, struct_rows, state=None):
+    args = list(packs) + [struct_rows] + ([] if start else [state])
     halves = 2 * SIDE + 2
     scratch = [
-        pltpu.VMEM((halves, G_ALL, 8, HALF), f32),
         pltpu.VMEM((2 * halves + 4, 8, LANES), f32),
         pltpu.VMEM((2 * halves + 4, 8, LANES), f32),
         pltpu.VMEM((2 * halves, 8, LANES), f32),
         pltpu.VMEM((2 * halves, 8, LANES), jnp.int32),
-        pltpu.VMEM(struct_rows.shape, f32),
-        pltpu.VMEM((NVAR, 3, SURF), f32),
         pltpu.VMEM((DEVS, LANES), f32),
     ]
-    if not start:
-        scratch.append(pltpu.VMEM((NVAR, CELL), f32))
-    scratch.append(pltpu.SemaphoreType.DMA((len(args),)))
     outs = [(NVAR, CELL), (2 * DEVS if start else DEVS, LANES)]
-    return call(functools.partial(fluid_kernel, start), "fluid", outs, [ANY] * len(args), scratch, vmem=63)(*args)
+    return call(functools.partial(fluid_kernel, start), "fluid", outs, [VMEM] * len(args), scratch)(*args)
 
 
 def shell_kernel(whole_rows, struct_rows, blocks, columns, out):
@@ -447,19 +438,20 @@
 
     sizes = [(NVAR, NVAR, FACES, CELL), (NVAR, NVAR, CELL), (NVAR, CELL), (NVAR, CELL),
              (NVAR, 3, SURF), (FACES, CELL), (TMAP, SURF), (TMAP, SURF), (1, SURF),
-             (2 * FLUID, BLK)]
+             (NVAR, 3, SURF)]
     kinds = [f32] * 5 + [jnp.int32] * 2 + [f32, jnp.int32, f32]
     own_shape = (2, G_ALL, 8, HALF)
-    rows_shape = (STRUCT, 2 * FLUID, LANES)
-    own, rows = call(
-        pack_kernel, "pack", [own_shape, rows_shape], [ANY] * 10 + [SMEM],
+    (own,) = call(
+        pack_kernel, "pack", [own_shape], [ANY] * 10 + [SMEM],
         [pltpu.VMEM(s, k) for s, k in zip(sizes, kinds)]
-        + [pltpu.VMEM(own_shape, f32), pltpu.VMEM(rows_shape, f32),
-           pltpu.SemaphoreType.DMA((10,)), pltpu.SemaphoreType.DMA((3,))],
-        [ANY] * 2, vmem=63,
+        + [pltpu.VMEM(own_shape, f32), pltpu.SemaphoreType.DMA((10,)),
+           pltpu.SemaphoreType.DMA((2,))],
+        [ANY], vmem=63,
     )(face_blocks.transpose(1, 2, 0, 3), diag_inverse, fluid_rhs, fluid_adjoint,
       load_sens.transpose(1, 0, 2), face_index, transfer_node, transfer_weight,
-      surface_cell.reshape(1, SURF), struct_adjoint.reshape(2 * FLUID, BLK), surface_count)
+      surface_cell.reshape(1, SURF), disp_sens, surface_count)
+    rows = jnp.pad(struct_adjoint.reshape(2 * FLUID, BLK), ((0, 0), (0, LANES - BLK)))
+    rows = jnp.broadcast_to(rows, (STRUCT,) + rows.shape)
     low = shift(own, 1)
     high = shift(own, -1)
     low_two = shift(own, 2)
@@ -489,11 +481,11 @@
         return solved
 
     terms = shell(struct_rows, True)
-    state, shares = fluid(True, packs, struct_rows, disp_sens)
+    state, shares = fluid(True, packs, struct_rows)
     solved = solve(shares, terms, (4 * DEVS, LANES), [pltpu.VMEM((DEVS + 16, LANES), f32)])
     struct_rows = lax.all_to_all(solved, BOTH, 0, 0, tiled=True)
     terms = shell(struct_rows, False)
-    state, shares = fluid(False, packs, struct_rows, disp_sens, state)
+    state, shares = fluid(False, packs, struct_rows, state)
     solved = solve(shares, terms, (2 * FLUID, LANES), [])
     group = lax.all_to_all(solved, "fluid", 0, 0, tiled=True)
     return (state, group[:, 0:BLK].reshape(-1))

time: 132 us -> 129 us (0.977)
  Pallas kernels: 19.3 us -> 15.1 us
  waiting for transfers between devices: 16.1 us -> 17.8 us
    pallas_call x3, Pallas kernels: 16.6 us -> 12.5 us  [the longest x2 10.5 us: fluid(): call(functools.partial(fluid_kernel, start), 'fluid', outs, [VMEM] * len(...]
    unnamed x20 -> x10, local copies, waits for them, and re-layouts: 4.18 us -> 2.08 us
    ppermute x6, starting transfers between devices: 25.6 us -> 23.7 us  [shift(): return lax.ppermute(value, BOTH, pairs)]
  transfers between devices with their start and end apart: 9 -> 9, of which waited for: 5 -> 3; matrix products, arithmetic and copies ran while one was open for 3% -> 6% of each run, Pallas kernels for 1% -> 1%
where the time goes in v3:
time: 129 us; the launch traced here: 127 us
  starting transfers between devices  55.3 us (43%)
  blocking collectives  26.1 us (20%)
  waiting for transfers between devices  17.8 us (14%)
  Pallas kernels  15.1 us (12%)
  local copies, waits for them, and re-layouts  11 us (9%)
  between operations  1.46 us (1%)
    ppermute x6, starting transfers between devices, shift(): return lax.ppermute(value, BOTH, pairs)  23.7 us
    all_to_all x2, starting transfers between devices, solve(): received = lax.all_to_all(shares, BOTH, 0, 0, tiled=True)  23.6 us
    all_to_all x2, waiting for transfers between devices, solve(): received = lax.all_to_all(shares, BOTH, 0, 0, tiled=True)  15.5 us
    all_to_all x1, blocking collectives, body(): struct_rows = lax.all_to_all(solved, BOTH, 0, 0, tiled=True)  15.2 us
    all_to_all x1, blocking collectives, body(): group = lax.all_to_all(solved, 'fluid', 0, 0, tiled=True)  10.9 us
    pallas_call x2, Pallas kernels, fluid(): call(functools.partial(fluid_kernel, start), 'fluid', outs, [VMEM] * len(...  10.5 us
    all_to_all x1, starting transfers between devices, body(): lax.all_to_all(rows, 'struct', 0, 0, tiled=True).reshape(2 * DEVS, LANES)  8.01 us
    dynamic_slice x4, local copies, waits for them, and re-layouts, body(): take = lambda a, axis: lax.dynamic_slice_in_dim(a, mine, 2, axis)  3.17 us
  transfers between devices with their start and end apart: 9, of which 3 were waited for; matrix products, arithmetic and copies ran while one was open for 6% of the time, Pallas kernels for 1%

profile of v3, /device:TPU:0, one launch (start us, length us, event | category | flops | bytes accessed | tf_op | source)
XLA Modules:
  0.0 126.7 jit_solution(703652774331628081)
XLA Ops:
  0.6 0.0 copy-start
  1.3 2.0 %pack.1.refs_0_ = f32[2,30,8,256]{3,2,1,0:T(8,128)} custom-call(f32[5,5,6,512]{3,2,1,0:T(8,128)} %bitcast.28, f32[5,5,512]{2,1,0:T(8,128)} %diag.1, f32[5,512]{1,0:T(8,128)} %rhs.1, f32[5,512]{1,0:T(8,128)} %state.1, f32[5,3,256]{2,1,0:T(4,128)} %bitcast.30, s32[6,512]{1,0:T(8,128)} %place.1, s32[3,256]{1,0:T(4,128)} %node.1, f32[3,256]{1,0:T(4,128)} %weight.1, ...), custom_call_target="tpu_custom_call" | custom-call | tf_op jit(solution)/shard_map/pack/pallas_call | solution.py:444
  3.3 0.0 copy-start.2
  3.3 1.4 %collective-permute-start.3 = (f32[2,30,8,256]{3,2,1,0:T(8,128)}, f32[2,30,8,256]{3,2,1,0:T(8,128)S(1)}, u32[]{:S(2)}, u32[]{:S(2)}) collective-permute-start(f32[2,30,8,256]{3,2,1,0:T(8,128)} %pack.1.refs_0_), channel_id=1, source_target_pairs={{2,0},{3,1},{4,2},{5,3},{6,4},{7,5},{8,6},{9,7},{10,8},{11,9},{12,... | collective-permute-start | bytes 1474568 | tf_op jit(solution)/shard_map/ppermute | solution.py:437
  4.7 4.6 %collective-permute-start.2 = (f32[2,30,8,256]{3,2,1,0:T(8,128)}, f32[2,30,8,256]{3,2,1,0:T(8,128)S(1)}, u32[]{:S(2)}, u32[]{:S(2)}) collective-permute-start(f32[2,30,8,256]{3,2,1,0:T(8,128)} %pack.1.refs_0_), channel_id=1, source_target_pairs={{0,2},{1,3},{2,4},{3,5},{4,6},{5,7},{6,8},{7,9},{8,10},{9,11},{10,... | collective-permute-start | bytes 1474568 | tf_op jit(solution)/shard_map/ppermute | solution.py:437
  9.3 1.3 %collective-permute-start.1 = (f32[2,30,8,256]{3,2,1,0:T(8,128)}, f32[2,30,8,256]{3,2,1,0:T(8,128)S(1)}, u32[]{:S(2)}, u32[]{:S(2)}) collective-permute-start(f32[2,30,8,256]{3,2,1,0:T(8,128)} %pack.1.refs_0_), channel_id=1, source_target_pairs={{1,0},{2,1},{3,2},{4,3},{5,4},{6,5},{7,6},{8,7},{9,8},{10,9},{11,1... | collective-permute-start | bytes 1474568 | tf_op jit(solution)/shard_map/ppermute | solution.py:437
  10.6 4.6 %collective-permute-start = (f32[2,30,8,256]{3,2,1,0:T(8,128)}, f32[2,30,8,256]{3,2,1,0:T(8,128)S(1)}, u32[]{:S(2)}, u32[]{:S(2)}) collective-permute-start(f32[2,30,8,256]{3,2,1,0:T(8,128)} %pack.1.refs_0_), channel_id=1, source_target_pairs={{0,1},{1,2},{2,3},{3,4},{4,5},{5,6},{6,7},{7,8},{8,9},{9,10},{10,1... | collective-permute-start | bytes 1474568 | tf_op jit(solution)/shard_map/ppermute | solution.py:437
  15.2 0.8 reshape.37
  16.0 0.7 broadcast_in_dim.3
  16.7 8.0 %all-to-all-start = ((f32[8,32,128]{2,1,0:T(8,128)}), f32[8,32,128]{2,1,0:T(8,128)S(1)}, u32[]{:S(2)}, u32[]{:S(2)}) async-start(f32[8,32,128]{2,1,0:T(8,128)} %broadcast_in_dim.3), calls=%async_computation | async-start | bytes 262144 | tf_op jit(solution)/shard_map/all_to_all | solution.py:459
  24.7 2.1 %constant_dynamic-slice_fusion.2 = f32[4,2,9216]{2,1,0:T(2,128)} fusion(f32[4,32,9216]{2,1,0:T(8,128)} %param.29, s32[]{:T(128)S(6)} %select_n.11), kind=kLoop, calls=%fused_computation.4 | loop fusion | bytes 589828 | tf_op jit(solution)/shard_map/dynamic_slice | solution.py:462
  26.7 0.0 collective-permute-done.1.refs_2_
  26.8 0.7 slice_bitcast_fusion
  27.5 1.3 %collective-permute-start.5 = (f32[30,8,256]{2,1,0:T(8,128)}, f32[30,8,256]{2,1,0:T(8,128)S(1)}, u32[]{:S(2)}, u32[]{:S(2)}) collective-permute-start(f32[30,8,256]{2,1,0:T(8,128)} %slice_bitcast_fusion), channel_id=1, source_target_pairs={{2,0},{3,1},{4,2},{5,3},{6,4},{7,5},{8,6},{9,7},{10,8},{11,9},{12,... | collective-permute-start | bytes 737288 | tf_op jit(solution)/shard_map/ppermute | solution.py:437
  28.8 0.0 collective-permute-done.refs_1_
  28.8 0.7 slice_bitcast_fusion.1
  29.5 10.5 %collective-permute-start.4 = (f32[30,8,256]{2,1,0:T(8,128)}, f32[30,8,256]{2,1,0:T(8,128)S(1)}, u32[]{:S(2)}, u32[]{:S(2)}) collective-permute-start(f32[30,8,256]{2,1,0:T(8,128)} %slice_bitcast_fusion.1), channel_id=1, source_target_pairs={{0,2},{1,3},{2,4},{3,5},{4,6},{5,7},{6,8},{7,9},{8,10},{9,11},{10,... | collective-permute-start | bytes 737288 | tf_op jit(solution)/shard_map/ppermute | solution.py:437
  40.0 1.0 constant_dynamic-slice_fusion
  41.0 0.8 reshape.39
  41.8 0.0 all-to-all-done
  41.9 0.0 collective-permute-done.3.refs_4_
  41.9 0.0 collective-permute-done.2.refs_3_
  41.9 0.0 collective-permute-done.5.refs_6_
  41.9 2.2 %collective-permute-done.4.refs_5_ = f32[30,8,256]{2,1,0:T(8,128)S(1)} collective-permute-done((f32[30,8,256]{2,1,0:T(8,128)}, f32[30,8,256]{2,1,0:T(8,128)S(1)}, u32[]{:S(2)}, u32[]{:S(2)}) %collective-permute-start.4) | collective-permute-done | bytes 245792 | tf_op jit(solution)/shard_map/ppermute | solution.py:437
  44.0 0.0 copy-start.3
  44.1 0.0 copy-start.1
  44.1 1.1 copy-done.1
  45.2 5.5 %fluid.2 = (f32[5,512]{1,0:T(8,128)S(1)}, f32[256,128]{1,0:T(8,128)}) custom-call(f32[2,30,8,256]{3,2,1,0:T(8,128)S(1)} %copy-done.1, f32[2,30,8,256]{3,2,1,0:T(8,128)S(1)} %collective-permute-done.refs_1_, f32[2,30,8,256]{3,2,1,0:T(8,128)S(1)} %collective-permute-done.1.refs_2_, f32[2,30,8,256]{3,2,1,0:T(8,128)S(1)} %collective-permute-done.2.refs_3_, ...), custom_call_target="tpu_custom_call" | custom-call | tf_op jit(solution)/shard_map/fluid/pallas_call | solution.py:350
  50.7 19.0 %all-to-all-start.1 = ((f32[128,2,128]{2,1,0:T(2,128)}), f32[128,2,128]{2,1,0:T(2,128)S(1)}, u32[]{:S(2)}, u32[]{:S(2)}) async-start(f32[128,2,128]{2,1,0:T(2,128)} %bitcast.6), calls=%async_computation.1 | async-start | bytes 262144 | tf_op jit(solution)/shard_map/all_to_all | solution.py:478
  69.7 0.0 copy-done.3
  69.7 0.1 reshape.41.inverse
  69.8 1.3 reshape.40.blocks
  71.1 0.0 copy-done
  71.1 0.1 constant_dynamic-slice_fusion.1.columns
  71.2 0.8 shell.2
  72.0 7.1 %all-to-all-done.1 = f32[128,2,128]{2,1,0:T(2,128)S(1)} async-done(((f32[128,2,128]{2,1,0:T(2,128)}), f32[128,2,128]{2,1,0:T(2,128)S(1)}, u32[]{:S(2)}, u32[]{:S(2)}) %all-to-all-start.1) | async-done | bytes 131104 | tf_op jit(solution)/shard_map/all_to_all | solution.py:478
  79.1 0.7 solve.2
  79.7 15.2 %all_to_all.50 = f32[128,4,128]{2,1,0:T(4,128)S(1)} all-to-all(f32[128,4,128]{2,1,0:T(4,128)S(1)} %bitcast.24), channel_id=1, replica_groups=mesh['fluid'=16,'struct'=8] {'fluid','struct'}, dimensions={0} | all-to-all | bytes 524288 | tf_op jit(solution)/shard_map/all_to_all | solution.py:486
  94.9 0.0 copy-done.2
  95.0 0.0 copy-start.4
  95.0 0.9 copy-done.4
  95.9 5.0 %fluid.3 = (f32[5,512]{1,0:T(8,128)}, f32[128,128]{1,0:T(8,128)}) custom-call(f32[2,30,8,256]{3,2,1,0:T(8,128)S(1)} %copy-done.2, f32[2,30,8,256]{3,2,1,0:T(8,128)S(1)} %collective-permute-done.refs_1_, f32[2,30,8,256]{3,2,1,0:T(8,128)S(1)} %collective-permute-done.1.refs_2_, f32[2,30,8,256]{3,2,1,0:T(8,128)S(1)} %collective-permute-done.2.refs_3_, ...), custom_call_target="tpu_custom_call" | custom-call | tf_op jit(solution)/shard_map/fluid/pallas_call | solution.py:350
  100.9 4.6 %all-to-all-start.3 = ((f32[128,1,128]{2,1,0:T(1,128)}), f32[128,1,128]{2,1,0:T(1,128)S(1)}, u32[]{:S(2)}, u32[]{:S(2)}) async-start(f32[128,1,128]{2,1,0:T(1,128)} %bitcast.12), calls=%async_computation.3 | async-start | bytes 131072 | tf_op jit(solution)/shard_map/all_to_all | solution.py:478
  105.5 0.8 shell.3
  106.3 8.5 %all-to-all-done.3 = f32[128,1,128]{2,1,0:T(1,128)S(1)} async-done(((f32[128,1,128]{2,1,0:T(1,128)}), f32[128,1,128]{2,1,0:T(1,128)S(1)}, u32[]{:S(2)}, u32[]{:S(2)}) %all-to-all-start.3) | async-done | bytes 65568 | tf_op jit(solution)/shard_map/all_to_all | solution.py:478
  114.8 0.3 solve.3
  115.1 10.9 %all_to_all.51 = f32[16,2,128]{2,1,0:T(2,128)S(1)} all-to-all(f32[16,2,128]{2,1,0:T(2,128)S(1)} %bitcast.27), channel_id=1, replica_groups=mesh['fluid'=16,'struct'=8] {'fluid'}, dimensions={0} | all-to-all | bytes 32768 | tf_op jit(solution)/shard_map/all_to_all | solution.py:490
  126.0 0.7 reshape.43
  (2 shorter events, 0.0 us)
Async XLA Ops:
  0.6 70.5 %copy-start = (s32[4,32]{1,0:T(4,128)S(1)}, s32[4,32]{1,0:T(4,128)}, u32[]{:S(2)}) copy-start(s32[4,32]{1,0:T(4,128)} %param.31) | copy-start | bytes 1540
  3.3 91.7 %copy-start.2 = (f32[2,30,8,256]{3,2,1,0:T(8,128)S(1)}, f32[2,30,8,256]{3,2,1,0:T(8,128)}, u32[]{:S(2)}) copy-start(f32[2,30,8,256]{3,2,1,0:T(8,128)} %pack.1.refs_0_) | copy-start | bytes 1474564
  3.3 38.6 %collective-permute-start.3 = (f32[2,30,8,256]{3,2,1,0:T(8,128)}, f32[2,30,8,256]{3,2,1,0:T(8,128)S(1)}, u32[]{:S(2)}, u32[]{:S(2)}) collective-permute-start(f32[2,30,8,256]{3,2,1,0:T(8,128)} %pack.1.refs_0_), channel_id=1, source_target_pairs={{2,0},{3,1},{4,2},{5,3},{6,4},{7,5},{8,6},{9,7},{10,8},{11,9},{12,... | collective-permute-start | bytes 1474568 | tf_op jit(solution)/shard_map/ppermute | solution.py:437
  4.7 37.1 %collective-permute-start.2 = (f32[2,30,8,256]{3,2,1,0:T(8,128)}, f32[2,30,8,256]{3,2,1,0:T(8,128)S(1)}, u32[]{:S(2)}, u32[]{:S(2)}) collective-permute-start(f32[2,30,8,256]{3,2,1,0:T(8,128)} %pack.1.refs_0_), channel_id=1, source_target_pairs={{0,2},{1,3},{2,4},{3,5},{4,6},{5,7},{6,8},{7,9},{8,10},{9,11},{10,... | collective-permute-start | bytes 1474568 | tf_op jit(solution)/shard_map/ppermute | solution.py:437
  9.3 17.4 %collective-permute-start.1 = (f32[2,30,8,256]{3,2,1,0:T(8,128)}, f32[2,30,8,256]{3,2,1,0:T(8,128)S(1)}, u32[]{:S(2)}, u32[]{:S(2)}) collective-permute-start(f32[2,30,8,256]{3,2,1,0:T(8,128)} %pack.1.refs_0_), channel_id=1, source_target_pairs={{1,0},{2,1},{3,2},{4,3},{5,4},{6,5},{7,6},{8,7},{9,8},{10,9},{11,1... | collective-permute-start | bytes 1474568 | tf_op jit(solution)/shard_map/ppermute | solution.py:437
  10.6 18.2 %collective-permute-start = (f32[2,30,8,256]{3,2,1,0:T(8,128)}, f32[2,30,8,256]{3,2,1,0:T(8,128)S(1)}, u32[]{:S(2)}, u32[]{:S(2)}) collective-permute-start(f32[2,30,8,256]{3,2,1,0:T(8,128)} %pack.1.refs_0_), channel_id=1, source_target_pairs={{0,1},{1,2},{2,3},{3,4},{4,5},{5,6},{6,7},{7,8},{8,9},{9,10},{10,1... | collective-permute-start | bytes 1474568 | tf_op jit(solution)/shard_map/ppermute | solution.py:437
  16.7 25.2 %all-to-all-start = ((f32[8,32,128]{2,1,0:T(8,128)}), f32[8,32,128]{2,1,0:T(8,128)S(1)}, u32[]{:S(2)}, u32[]{:S(2)}) async-start(f32[8,32,128]{2,1,0:T(8,128)} %broadcast_in_dim.3), calls=%async_computation | async-start | bytes 262144 | tf_op jit(solution)/shard_map/all_to_all | solution.py:459
  27.5 14.4 %collective-permute-start.5 = (f32[30,8,256]{2,1,0:T(8,128)}, f32[30,8,256]{2,1,0:T(8,128)S(1)}, u32[]{:S(2)}, u32[]{:S(2)}) collective-permute-start(f32[30,8,256]{2,1,0:T(8,128)} %slice_bitcast_fusion), channel_id=1, source_target_pairs={{2,0},{3,1},{4,2},{5,3},{6,4},{7,5},{8,6},{9,7},{10,8},{11,9},{12,... | collective-permute-start | bytes 737288 | tf_op jit(solution)/shard_map/ppermute | solution.py:437
  29.5 14.5 %collective-permute-start.4 = (f32[30,8,256]{2,1,0:T(8,128)}, f32[30,8,256]{2,1,0:T(8,128)S(1)}, u32[]{:S(2)}, u32[]{:S(2)}) collective-permute-start(f32[30,8,256]{2,1,0:T(8,128)} %slice_bitcast_fusion.1), channel_id=1, source_target_pairs={{0,2},{1,3},{2,4},{3,5},{4,6},{5,7},{6,8},{7,9},{8,10},{9,11},{10,... | collective-permute-start | bytes 737288 | tf_op jit(solution)/shard_map/ppermute | solution.py:437
  44.0 25.6 %copy-start.3 = (f32[30,8,256]{2,1,0:T(8,128)}, f32[30,8,256]{2,1,0:T(8,128)S(1)}, u32[]{:S(2)}) copy-start(f32[30,8,256]{2,1,0:T(8,128)S(1)} %collective-permute-done.4.refs_5_) | copy-start | bytes 737284
  44.1 1.1 copy-start.1
  50.7 28.4 %all-to-all-start.1 = ((f32[128,2,128]{2,1,0:T(2,128)}), f32[128,2,128]{2,1,0:T(2,128)S(1)}, u32[]{:S(2)}, u32[]{:S(2)}) async-start(f32[128,2,128]{2,1,0:T(2,128)} %bitcast.6), calls=%async_computation.1 | async-start | bytes 262144 | tf_op jit(solution)/shard_map/all_to_all | solution.py:478
  95.0 0.9 copy-start.4
  100.9 13.9 %all-to-all-start.3 = ((f32[128,1,128]{2,1,0:T(1,128)}), f32[128,1,128]{2,1,0:T(1,128)S(1)}, u32[]{:S(2)}, u32[]{:S(2)}) async-start(f32[128,1,128]{2,1,0:T(1,128)} %bitcast.12), calls=%async_computation.3 | async-start | bytes 131072 | tf_op jit(solution)/shard_map/all_to_all | solution.py:478

commit v4 on v3

--- a/solution.py
+++ b/solution.py
@@ -333,7 +333,7 @@
         shares[pl.ds(1, DEVS, stride=2), :] = chunks[...]
 
 
-PACKS = ((0, 2), (-2, 2), (2, 2), (-4, 2), (4, 2), (-5, 1), (6, 1))
+PACKS = ((0, 2), (-4, 2), (4, 2), (-2, 2), (2, 2), (-5, 1), (6, 1))
 
 
 def fluid(start, packs, struct_rows, state=None):
@@ -465,7 +465,7 @@
     columns = take(shell_columns, 1)
     rhs_rows = take(struct_rhs.reshape(2 * FLUID, BLK), 0)
 
-    packs = [own, low, high, low_two, high_two, shift(low[1], 2), shift(high[0], -2)]
+    packs = [own, low_two, high_two, low, high, shift(low[1], 2), shift(high[0], -2)]
     relay = ((lax.axis_index(BOTH)) // CHUNKS).astype(jnp.int32).reshape(1)
 
     def shell(struct_rows, start):

time: 129 us -> 124 us (0.961)
  starting transfers between devices: 55.3 us -> 44.8 us
  waiting for transfers between devices: 17.8 us -> 23.4 us
    ppermute x6, starting transfers between devices: 23.7 us -> 17.7 us  [shift(): return lax.ppermute(value, BOTH, pairs)]
    all_to_all x1, waiting for transfers between devices: 0.05 us -> 6.02 us  [body(): lax.all_to_all(rows, 'struct', 0, 0, tiled=True).reshape(2 * DEVS, LANES)]
    all_to_all x2, starting transfers between devices: 23.6 us -> 19.1 us  [solve(): received = lax.all_to_all(shares, BOTH, 0, 0, tiled=True)]
  transfers between devices with their start and end apart: 9 -> 9, of which waited for: 3 -> 4; matrix products, arithmetic and copies ran while one was open for 6% -> 7% of each run, Pallas kernels for 1% -> 1%
where the time goes in v4:
time: 124 us; the launch traced here: 122 us
  starting transfers between devices  44.8 us (36%)
  blocking collectives  26.1 us (21%)
  waiting for transfers between devices  23.4 us (19%)
  Pallas kernels  15.4 us (12%)
  local copies, waits for them, and re-layouts  11 us (9%)
  between operations  1.46 us (1%)
    all_to_all x2, starting transfers between devices, solve(): received = lax.all_to_all(shares, BOTH, 0, 0, tiled=True)  19.1 us
    ppermute x6, starting transfers between devices, shift(): return lax.ppermute(value, BOTH, pairs)  17.7 us
    all_to_all x2, waiting for transfers between devices, solve(): received = lax.all_to_all(shares, BOTH, 0, 0, tiled=True)  15.5 us
    all_to_all x1, blocking collectives, body(): struct_rows = lax.all_to_all(solved, BOTH, 0, 0, tiled=True)  15.2 us
    all_to_all x1, blocking collectives, body(): group = lax.all_to_all(solved, 'fluid', 0, 0, tiled=True)  10.9 us
    pallas_call x2, Pallas kernels, fluid(): call(functools.partial(fluid_kernel, start), 'fluid', outs, [VMEM] * len(...  10.7 us
    all_to_all x1, starting transfers between devices, body(): lax.all_to_all(rows, 'struct', 0, 0, tiled=True).reshape(2 * DEVS, LANES)  8.01 us
    all_to_all x1, waiting for transfers between devices, body(): lax.all_to_all(rows, 'struct', 0, 0, tiled=True).reshape(2 * DEVS, LANES)  6.02 us
  transfers between devices with their start and end apart: 9, of which 4 were waited for; matrix products, arithmetic and copies ran while one was open for 7% of the time, Pallas kernels for 1%

profile of v4, /device:TPU:0, one launch (start us, length us, event | category | flops | bytes accessed | tf_op | source)
XLA Modules:
  0.0 122.1 jit_solution(5773994997748257449)
XLA Ops:
  0.6 0.0 copy-start
  1.3 2.0 %pack.1.refs_0_ = f32[2,30,8,256]{3,2,1,0:T(8,128)} custom-call(f32[5,5,6,512]{3,2,1,0:T(8,128)} %bitcast.28, f32[5,5,512]{2,1,0:T(8,128)} %diag.1, f32[5,512]{1,0:T(8,128)} %rhs.1, f32[5,512]{1,0:T(8,128)} %state.1, f32[5,3,256]{2,1,0:T(4,128)} %bitcast.30, s32[6,512]{1,0:T(8,128)} %place.1, s32[3,256]{1,0:T(4,128)} %node.1, f32[3,256]{1,0:T(4,128)} %weight.1, ...), custom_call_target="tpu_custom_call" | custom-call | tf_op jit(solution)/shard_map/pack/pallas_call | solution.py:444
  3.3 0.0 copy-start.2
  3.3 1.4 %collective-permute-start.3 = (f32[2,30,8,256]{3,2,1,0:T(8,128)}, f32[2,30,8,256]{3,2,1,0:T(8,128)S(1)}, u32[]{:S(2)}, u32[]{:S(2)}) collective-permute-start(f32[2,30,8,256]{3,2,1,0:T(8,128)} %pack.1.refs_0_), channel_id=1, source_target_pairs={{1,0},{2,1},{3,2},{4,3},{5,4},{6,5},{7,6},{8,7},{9,8},{10,9},{11,1... | collective-permute-start | bytes 1474568 | tf_op jit(solution)/shard_map/ppermute | solution.py:437
  4.7 4.6 %collective-permute-start.2 = (f32[2,30,8,256]{3,2,1,0:T(8,128)}, f32[2,30,8,256]{3,2,1,0:T(8,128)S(1)}, u32[]{:S(2)}, u32[]{:S(2)}) collective-permute-start(f32[2,30,8,256]{3,2,1,0:T(8,128)} %pack.1.refs_0_), channel_id=1, source_target_pairs={{0,1},{1,2},{2,3},{3,4},{4,5},{5,6},{6,7},{7,8},{8,9},{9,10},{10,1... | collective-permute-start | bytes 1474568 | tf_op jit(solution)/shard_map/ppermute | solution.py:437
  9.3 1.3 %collective-permute-start.1 = (f32[2,30,8,256]{3,2,1,0:T(8,128)}, f32[2,30,8,256]{3,2,1,0:T(8,128)S(1)}, u32[]{:S(2)}, u32[]{:S(2)}) collective-permute-start(f32[2,30,8,256]{3,2,1,0:T(8,128)} %pack.1.refs_0_), channel_id=1, source_target_pairs={{2,0},{3,1},{4,2},{5,3},{6,4},{7,5},{8,6},{9,7},{10,8},{11,9},{12,... | collective-permute-start | bytes 1474568 | tf_op jit(solution)/shard_map/ppermute | solution.py:437
  10.6 4.6 %collective-permute-start = (f32[2,30,8,256]{3,2,1,0:T(8,128)}, f32[2,30,8,256]{3,2,1,0:T(8,128)S(1)}, u32[]{:S(2)}, u32[]{:S(2)}) collective-permute-start(f32[2,30,8,256]{3,2,1,0:T(8,128)} %pack.1.refs_0_), channel_id=1, source_target_pairs={{0,2},{1,3},{2,4},{3,5},{4,6},{5,7},{6,8},{7,9},{8,10},{9,11},{10,... | collective-permute-start | bytes 1474568 | tf_op jit(solution)/shard_map/ppermute | solution.py:437
  15.2 0.8 reshape.37
  16.0 0.7 broadcast_in_dim.3
  16.7 8.0 %all-to-all-start = ((f32[8,32,128]{2,1,0:T(8,128)}), f32[8,32,128]{2,1,0:T(8,128)S(1)}, u32[]{:S(2)}, u32[]{:S(2)}) async-start(f32[8,32,128]{2,1,0:T(8,128)} %broadcast_in_dim.3), calls=%async_computation | async-start | bytes 262144 | tf_op jit(solution)/shard_map/all_to_all | solution.py:459
  24.7 2.1 %constant_dynamic-slice_fusion.2 = f32[4,2,9216]{2,1,0:T(2,128)} fusion(f32[4,32,9216]{2,1,0:T(8,128)} %param.29, s32[]{:T(128)S(6)} %select_n.11), kind=kLoop, calls=%fused_computation.4 | loop fusion | bytes 589828 | tf_op jit(solution)/shard_map/dynamic_slice | solution.py:462
  26.7 0.0 collective-permute-done.3.refs_4_
  26.8 0.7 slice_bitcast_fusion
  27.5 1.3 %collective-permute-start.5 = (f32[30,8,256]{2,1,0:T(8,128)}, f32[30,8,256]{2,1,0:T(8,128)S(1)}, u32[]{:S(2)}, u32[]{:S(2)}) collective-permute-start(f32[30,8,256]{2,1,0:T(8,128)} %slice_bitcast_fusion), channel_id=1, source_target_pairs={{2,0},{3,1},{4,2},{5,3},{6,4},{7,5},{8,6},{9,7},{10,8},{11,9},{12,... | collective-permute-start | bytes 737288 | tf_op jit(solution)/shard_map/ppermute | solution.py:437
  28.8 0.0 collective-permute-done.2.refs_3_
  28.8 0.7 slice_bitcast_fusion.1
  29.5 4.6 %collective-permute-start.4 = (f32[30,8,256]{2,1,0:T(8,128)}, f32[30,8,256]{2,1,0:T(8,128)S(1)}, u32[]{:S(2)}, u32[]{:S(2)}) collective-permute-start(f32[30,8,256]{2,1,0:T(8,128)} %slice_bitcast_fusion.1), channel_id=1, source_target_pairs={{0,2},{1,3},{2,4},{3,5},{4,6},{5,7},{6,8},{7,9},{8,10},{9,11},{10,... | collective-permute-start | bytes 737288 | tf_op jit(solution)/shard_map/ppermute | solution.py:437
  34.1 1.0 constant_dynamic-slice_fusion
  35.1 0.8 reshape.39
  35.8 6.0 %all-to-all-done = f32[8,32,128]{2,1,0:T(8,128)S(1)} async-done(((f32[8,32,128]{2,1,0:T(8,128)}), f32[8,32,128]{2,1,0:T(8,128)S(1)}, u32[]{:S(2)}, u32[]{:S(2)}) %all-to-all-start) | async-done | bytes 131104 | tf_op jit(solution)/shard_map/all_to_all | solution.py:459
  41.9 0.0 collective-permute-done.1.refs_2_
  41.9 0.0 collective-permute-done.refs_1_
  41.9 0.0 collective-permute-done.5.refs_6_
  41.9 1.8 %collective-permute-done.4.refs_5_ = f32[30,8,256]{2,1,0:T(8,128)S(1)} collective-permute-done((f32[30,8,256]{2,1,0:T(8,128)}, f32[30,8,256]{2,1,0:T(8,128)S(1)}, u32[]{:S(2)}, u32[]{:S(2)}) %collective-permute-start.4) | collective-permute-done | bytes 245792 | tf_op jit(solution)/shard_map/ppermute | solution.py:437
  43.7 0.0 copy-start.3
  43.7 0.0 copy-start.1
  43.7 1.1 copy-done.1
  44.8 5.6 %fluid.2 = (f32[5,512]{1,0:T(8,128)S(1)}, f32[256,128]{1,0:T(8,128)}) custom-call(f32[2,30,8,256]{3,2,1,0:T(8,128)S(1)} %copy-done.1, f32[2,30,8,256]{3,2,1,0:T(8,128)S(1)} %collective-permute-done.refs_1_, f32[2,30,8,256]{3,2,1,0:T(8,128)S(1)} %collective-permute-done.1.refs_2_, f32[2,30,8,256]{3,2,1,0:T(8,128)S(1)} %collective-permute-done.2.refs_3_, ...), custom_call_target="tpu_custom_call" | custom-call | tf_op jit(solution)/shard_map/fluid/pallas_call | solution.py:350
  50.4 14.5 %all-to-all-start.1 = ((f32[128,2,128]{2,1,0:T(2,128)}), f32[128,2,128]{2,1,0:T(2,128)S(1)}, u32[]{:S(2)}, u32[]{:S(2)}) async-start(f32[128,2,128]{2,1,0:T(2,128)} %bitcast.6), calls=%async_computation.1 | async-start | bytes 262144 | tf_op jit(solution)/shard_map/all_to_all | solution.py:478
  65.0 0.0 copy-done.3
  65.0 0.1 reshape.41.inverse
  65.1 1.3 %reshape.40.blocks = f32[4,2,96,96]{3,2,1,0:T(8,128)S(1)} reshape(f32[4,2,9216]{2,1,0:T(2,128)} %constant_dynamic-slice_fusion.2) | data formatting | bytes 589824 | tf_op jit(solution)/shard_map/reshape | solution.py:463
  66.3 0.0 copy-done
  66.4 0.1 constant_dynamic-slice_fusion.1.columns
  66.4 0.8 shell.2
  67.3 7.1 %all-to-all-done.1 = f32[128,2,128]{2,1,0:T(2,128)S(1)} async-done(((f32[128,2,128]{2,1,0:T(2,128)}), f32[128,2,128]{2,1,0:T(2,128)S(1)}, u32[]{:S(2)}, u32[]{:S(2)}) %all-to-all-start.1) | async-done | bytes 131104 | tf_op jit(solution)/shard_map/all_to_all | solution.py:478
  74.4 0.7 solve.2
  75.0 15.2 %all_to_all.50 = f32[128,4,128]{2,1,0:T(4,128)S(1)} all-to-all(f32[128,4,128]{2,1,0:T(4,128)S(1)} %bitcast.24), channel_id=1, replica_groups=mesh['fluid'=16,'struct'=8] {'fluid','struct'}, dimensions={0} | all-to-all | bytes 524288 | tf_op jit(solution)/shard_map/all_to_all | solution.py:486
  90.2 0.0 copy-done.2
  90.2 0.0 copy-start.4
  90.2 0.9 copy-done.4
  91.2 5.1 %fluid.3 = (f32[5,512]{1,0:T(8,128)}, f32[128,128]{1,0:T(8,128)}) custom-call(f32[2,30,8,256]{3,2,1,0:T(8,128)S(1)} %copy-done.2, f32[2,30,8,256]{3,2,1,0:T(8,128)S(1)} %collective-permute-done.refs_1_, f32[2,30,8,256]{3,2,1,0:T(8,128)S(1)} %collective-permute-done.1.refs_2_, f32[2,30,8,256]{3,2,1,0:T(8,128)S(1)} %collective-permute-done.2.refs_3_, ...), custom_call_target="tpu_custom_call" | custom-call | tf_op jit(solution)/shard_map/fluid/pallas_call | solution.py:350
  96.2 4.6 %all-to-all-start.3 = ((f32[128,1,128]{2,1,0:T(1,128)}), f32[128,1,128]{2,1,0:T(1,128)S(1)}, u32[]{:S(2)}, u32[]{:S(2)}) async-start(f32[128,1,128]{2,1,0:T(1,128)} %bitcast.12), calls=%async_computation.3 | async-start | bytes 131072 | tf_op jit(solution)/shard_map/all_to_all | solution.py:478
  100.9 0.8 shell.3
  101.7 8.5 %all-to-all-done.3 = f32[128,1,128]{2,1,0:T(1,128)S(1)} async-done(((f32[128,1,128]{2,1,0:T(1,128)}), f32[128,1,128]{2,1,0:T(1,128)S(1)}, u32[]{:S(2)}, u32[]{:S(2)}) %all-to-all-start.3) | async-done | bytes 65568 | tf_op jit(solution)/shard_map/all_to_all | solution.py:478
  110.2 0.3 solve.3
  110.5 10.9 %all_to_all.51 = f32[16,2,128]{2,1,0:T(2,128)S(1)} all-to-all(f32[16,2,128]{2,1,0:T(2,128)S(1)} %bitcast.27), channel_id=1, replica_groups=mesh['fluid'=16,'struct'=8] {'fluid'}, dimensions={0} | all-to-all | bytes 32768 | tf_op jit(solution)/shard_map/all_to_all | solution.py:490
  121.4 0.7 reshape.43
  (2 shorter events, 0.0 us)
Async XLA Ops:
  0.6 65.7 %copy-start = (s32[4,32]{1,0:T(4,128)S(1)}, s32[4,32]{1,0:T(4,128)}, u32[]{:S(2)}) copy-start(s32[4,32]{1,0:T(4,128)} %param.31) | copy-start | bytes 1540
  3.3 86.9 %copy-start.2 = (f32[2,30,8,256]{3,2,1,0:T(8,128)S(1)}, f32[2,30,8,256]{3,2,1,0:T(8,128)}, u32[]{:S(2)}) copy-start(f32[2,30,8,256]{3,2,1,0:T(8,128)} %pack.1.refs_0_) | copy-start | bytes 1474564
  3.3 23.4 %collective-permute-start.3 = (f32[2,30,8,256]{3,2,1,0:T(8,128)}, f32[2,30,8,256]{3,2,1,0:T(8,128)S(1)}, u32[]{:S(2)}, u32[]{:S(2)}) collective-permute-start(f32[2,30,8,256]{3,2,1,0:T(8,128)} %pack.1.refs_0_), channel_id=1, source_target_pairs={{1,0},{2,1},{3,2},{4,3},{5,4},{6,5},{7,6},{8,7},{9,8},{10,9},{11,1... | collective-permute-start | bytes 1474568 | tf_op jit(solution)/shard_map/ppermute | solution.py:437
  4.7 24.0 %collective-permute-start.2 = (f32[2,30,8,256]{3,2,1,0:T(8,128)}, f32[2,30,8,256]{3,2,1,0:T(8,128)S(1)}, u32[]{:S(2)}, u32[]{:S(2)}) collective-permute-start(f32[2,30,8,256]{3,2,1,0:T(8,128)} %pack.1.refs_0_), channel_id=1, source_target_pairs={{0,1},{1,2},{2,3},{3,4},{4,5},{5,6},{6,7},{7,8},{8,9},{9,10},{10,1... | collective-permute-start | bytes 1474568 | tf_op jit(solution)/shard_map/ppermute | solution.py:437
  9.3 32.5 %collective-permute-start.1 = (f32[2,30,8,256]{3,2,1,0:T(8,128)}, f32[2,30,8,256]{3,2,1,0:T(8,128)S(1)}, u32[]{:S(2)}, u32[]{:S(2)}) collective-permute-start(f32[2,30,8,256]{3,2,1,0:T(8,128)} %pack.1.refs_0_), channel_id=1, source_target_pairs={{2,0},{3,1},{4,2},{5,3},{6,4},{7,5},{8,6},{9,7},{10,8},{11,9},{12,... | collective-permute-start | bytes 1474568 | tf_op jit(solution)/shard_map/ppermute | solution.py:437
  10.6 31.3 %collective-permute-start = (f32[2,30,8,256]{3,2,1,0:T(8,128)}, f32[2,30,8,256]{3,2,1,0:T(8,128)S(1)}, u32[]{:S(2)}, u32[]{:S(2)}) collective-permute-start(f32[2,30,8,256]{3,2,1,0:T(8,128)} %pack.1.refs_0_), channel_id=1, source_target_pairs={{0,2},{1,3},{2,4},{3,5},{4,6},{5,7},{6,8},{7,9},{8,10},{9,11},{10,... | collective-permute-start | bytes 1474568 | tf_op jit(solution)/shard_map/ppermute | solution.py:437
  16.7 25.2 %all-to-all-start = ((f32[8,32,128]{2,1,0:T(8,128)}), f32[8,32,128]{2,1,0:T(8,128)S(1)}, u32[]{:S(2)}, u32[]{:S(2)}) async-start(f32[8,32,128]{2,1,0:T(8,128)} %broadcast_in_dim.3), calls=%async_computation | async-start | bytes 262144 | tf_op jit(solution)/shard_map/all_to_all | solution.py:459
  27.5 14.4 %collective-permute-start.5 = (f32[30,8,256]{2,1,0:T(8,128)}, f32[30,8,256]{2,1,0:T(8,128)S(1)}, u32[]{:S(2)}, u32[]{:S(2)}) collective-permute-start(f32[30,8,256]{2,1,0:T(8,128)} %slice_bitcast_fusion), channel_id=1, source_target_pairs={{2,0},{3,1},{4,2},{5,3},{6,4},{7,5},{8,6},{9,7},{10,8},{11,9},{12,... | collective-permute-start | bytes 737288 | tf_op jit(solution)/shard_map/ppermute | solution.py:437
  29.5 14.1 %collective-permute-start.4 = (f32[30,8,256]{2,1,0:T(8,128)}, f32[30,8,256]{2,1,0:T(8,128)S(1)}, u32[]{:S(2)}, u32[]{:S(2)}) collective-permute-start(f32[30,8,256]{2,1,0:T(8,128)} %slice_bitcast_fusion.1), channel_id=1, source_target_pairs={{0,2},{1,3},{2,4},{3,5},{4,6},{5,7},{6,8},{7,9},{8,10},{9,11},{10,... | collective-permute-start | bytes 737288 | tf_op jit(solution)/shard_map/ppermute | solution.py:437
  43.7 21.3 %copy-start.3 = (f32[30,8,256]{2,1,0:T(8,128)}, f32[30,8,256]{2,1,0:T(8,128)S(1)}, u32[]{:S(2)}) copy-start(f32[30,8,256]{2,1,0:T(8,128)S(1)} %collective-permute-done.4.refs_5_) | copy-start | bytes 737284
  43.7 1.1 copy-start.1
  50.4 23.9 %all-to-all-start.1 = ((f32[128,2,128]{2,1,0:T(2,128)}), f32[128,2,128]{2,1,0:T(2,128)S(1)}, u32[]{:S(2)}, u32[]{:S(2)}) async-start(f32[128,2,128]{2,1,0:T(2,128)} %bitcast.6), calls=%async_computation.1 | async-start | bytes 262144 | tf_op jit(solution)/shard_map/all_to_all | solution.py:478
  90.2 0.9 copy-start.4
  96.2 13.9 %all-to-all-start.3 = ((f32[128,1,128]{2,1,0:T(1,128)}), f32[128,1,128]{2,1,0:T(1,128)S(1)}, u32[]{:S(2)}, u32[]{:S(2)}) async-start(f32[128,1,128]{2,1,0:T(1,128)} %bitcast.12), calls=%async_computation.3 | async-start | bytes 131072 | tf_op jit(solution)/shard_map/all_to_all | solution.py:478

commit v5 on v4

--- a/solution.py
+++ b/solution.py
@@ -365,7 +365,8 @@
         out[half:half + 1, :] = total
 
 
-def solve_kernel(received, rhs, shell, inverse, relay, out, *padded):
+def solve_kernel(held, received, rhs, shell, inverse, relay, *refs):
+    out, *padded = refs[held:]
     start = bool(padded)
     lines = received[pl.ds(0, DEVS, stride=2), :] if start else received[...]
     parts = split3(jnp.sum(lines, axis=0, keepdims=True)[:, 0:PIECE])
@@ -474,15 +475,18 @@
         )(struct_rows, blocks, columns)
         return terms
 
-    def solve(shares, terms, shape, scratch):
+    def solve(shares, terms, shape, scratch, held=()):
         received = lax.all_to_all(shares, BOTH, 0, 0, tiled=True)
-        (solved,) = call(solve_kernel, "solve", [shape], [VMEM] * 4 + [SMEM], scratch)(
-            received, rhs_rows, terms, inverse, relay)
+        (solved,) = call(
+            functools.partial(solve_kernel, len(held)), "solve", [shape],
+            [VMEM] * 4 + [SMEM] + [VMEM] * len(held), scratch,
+        )(received, rhs_rows, terms, inverse, relay, *held)
         return solved
 
     terms = shell(struct_rows, True)
     state, shares = fluid(True, packs, struct_rows)
-    solved = solve(shares, terms, (4 * DEVS, LANES), [pltpu.VMEM((DEVS + 16, LANES), f32)])
+    solved = solve(shares, terms, (4 * DEVS, LANES), [pltpu.VMEM((DEVS + 16, LANES), f32)],
+                   packs[5:])
     struct_rows = lax.all_to_all(solved, BOTH, 0, 0, tiled=True)
     terms = shell(struct_rows, False)
     state, shares = fluid(False, packs, struct_rows, state)

time: 124 us -> 123 us (level)
  local copies, waits for them, and re-layouts: 11 us -> 7.55 us
  Pallas kernels: 15.4 us -> 17.4 us
  waiting for transfers between devices: 23.4 us -> 25.3 us
    pallas_call x2, Pallas kernels: 10.7 us -> 12.7 us  [fluid(): call(functools.partial(fluid_kernel, start), 'fluid', outs, [VMEM] * len(...]
    all_to_all x1, waiting for transfers between devices: 6.02 us -> 7.79 us  [body(): lax.all_to_all(rows, 'struct', 0, 0, tiled=True).reshape(2 * DEVS, LANES)]
    all_to_all x2, starting transfers between devices: 19.1 us -> 17.6 us  [solve(): received = lax.all_to_all(shares, BOTH, 0, 0, tiled=True)]
  transfers between devices with their start and end apart: 9 -> 9, of which waited for: 4 -> 4; matrix products, arithmetic and copies ran while one was open for 7% -> 5% of each run, Pallas kernels for 1% -> 1%
where the time goes in v5:
time: 123 us; the launch traced here: 122 us
  starting transfers between devices  43.7 us (36%)
  blocking collectives  26.1 us (21%)
  waiting for transfers between devices  25.3 us (21%)
  Pallas kernels  17.4 us (14%)
  local copies, waits for them, and re-layouts  7.55 us (6%)
  between operations  1.45 us (1%)
    ppermute x6, starting transfers between devices, shift(): return lax.ppermute(value, BOTH, pairs)  18.9 us
    all_to_all x2, starting transfers between devices, solve(): received = lax.all_to_all(shares, BOTH, 0, 0, tiled=True)  17.6 us
    all_to_all x2, waiting for transfers between devices, solve(): received = lax.all_to_all(shares, BOTH, 0, 0, tiled=True)  16.5 us
    all_to_all x1, blocking collectives, body(): struct_rows = lax.all_to_all(solved, BOTH, 0, 0, tiled=True)  15.2 us
    pallas_call x2, Pallas kernels, fluid(): call(functools.partial(fluid_kernel, start), 'fluid', outs, [VMEM] * len(...  12.7 us
    all_to_all x1, blocking collectives, body(): group = lax.all_to_all(solved, 'fluid', 0, 0, tiled=True)  10.9 us
    all_to_all x1, waiting for transfers between devices, body(): lax.all_to_all(rows, 'struct', 0, 0, tiled=True).reshape(2 * DEVS, LANES)  7.79 us
    all_to_all x1, starting transfers between devices, body(): lax.all_to_all(rows, 'struct', 0, 0, tiled=True).reshape(2 * DEVS, LANES)  7.26 us
  transfers between devices with their start and end apart: 9, of which 4 were waited for; matrix products, arithmetic and copies ran while one was open for 5% of the time, Pallas kernels for 1%

profile of v5, /device:TPU:0, one launch (start us, length us, event | category | flops | bytes accessed | tf_op | source)
XLA Modules:
  0.0 121.5 jit_solution(1010189410192712956)
XLA Ops:
  0.6 0.0 copy-start
  1.3 2.0 %pack.1.refs_0_ = f32[2,30,8,256]{3,2,1,0:T(8,128)} custom-call(f32[5,5,6,512]{3,2,1,0:T(8,128)} %bitcast.28, f32[5,5,512]{2,1,0:T(8,128)} %diag.1, f32[5,512]{1,0:T(8,128)} %rhs.1, f32[5,512]{1,0:T(8,128)} %state.1, f32[5,3,256]{2,1,0:T(4,128)} %bitcast.30, s32[6,512]{1,0:T(8,128)} %place.1, s32[3,256]{1,0:T(4,128)} %node.1, f32[3,256]{1,0:T(4,128)} %weight.1, ...), custom_call_target="tpu_custom_call" | custom-call | tf_op jit(solution)/shard_map/pack/pallas_call | solution.py:445
  3.3 0.0 copy-start.2
  3.3 1.4 %collective-permute-start.3 = (f32[2,30,8,256]{3,2,1,0:T(8,128)}, f32[2,30,8,256]{3,2,1,0:T(8,128)S(1)}, u32[]{:S(2)}, u32[]{:S(2)}) collective-permute-start(f32[2,30,8,256]{3,2,1,0:T(8,128)} %pack.1.refs_0_), channel_id=1, source_target_pairs={{1,0},{2,1},{3,2},{4,3},{5,4},{6,5},{7,6},{8,7},{9,8},{10,9},{11,1... | collective-permute-start | bytes 1474568 | tf_op jit(solution)/shard_map/ppermute | solution.py:438
  4.7 4.6 %collective-permute-start.2 = (f32[2,30,8,256]{3,2,1,0:T(8,128)}, f32[2,30,8,256]{3,2,1,0:T(8,128)S(1)}, u32[]{:S(2)}, u32[]{:S(2)}) collective-permute-start(f32[2,30,8,256]{3,2,1,0:T(8,128)} %pack.1.refs_0_), channel_id=1, source_target_pairs={{0,1},{1,2},{2,3},{3,4},{4,5},{5,6},{6,7},{7,8},{8,9},{9,10},{10,1... | collective-permute-start | bytes 1474568 | tf_op jit(solution)/shard_map/ppermute | solution.py:438
  9.3 1.3 %collective-permute-start.1 = (f32[2,30,8,256]{3,2,1,0:T(8,128)}, f32[2,30,8,256]{3,2,1,0:T(8,128)S(1)}, u32[]{:S(2)}, u32[]{:S(2)}) collective-permute-start(f32[2,30,8,256]{3,2,1,0:T(8,128)} %pack.1.refs_0_), channel_id=1, source_target_pairs={{2,0},{3,1},{4,2},{5,3},{6,4},{7,5},{8,6},{9,7},{10,8},{11,9},{12,... | collective-permute-start | bytes 1474568 | tf_op jit(solution)/shard_map/ppermute | solution.py:438
  10.6 5.3 %collective-permute-start = (f32[2,30,8,256]{3,2,1,0:T(8,128)}, f32[2,30,8,256]{3,2,1,0:T(8,128)}, u32[]{:S(2)}, u32[]{:S(2)}) collective-permute-start(f32[2,30,8,256]{3,2,1,0:T(8,128)} %pack.1.refs_0_), channel_id=1, source_target_pairs={{0,2},{1,3},{2,4},{3,5},{4,6},{5,7},{6,8},{7,9},{8,10},{9,11},{10,... | collective-permute-start | bytes 1474568 | tf_op jit(solution)/shard_map/ppermute | solution.py:438
  16.0 0.8 reshape.37
  16.7 0.7 broadcast_in_dim.3
  17.4 7.3 %all-to-all-start = ((f32[8,32,128]{2,1,0:T(8,128)}), f32[8,32,128]{2,1,0:T(8,128)S(1)}, u32[]{:S(2)}, u32[]{:S(2)}) async-start(f32[8,32,128]{2,1,0:T(8,128)} %broadcast_in_dim.3), calls=%async_computation | async-start | bytes 262144 | tf_op jit(solution)/shard_map/all_to_all | solution.py:460
  24.7 1.4 %constant_dynamic-slice_fusion.2 = f32[4,2,9216]{2,1,0:T(2,128)S(1)} fusion(f32[4,32,9216]{2,1,0:T(8,128)} %param.29, s32[]{:T(128)S(6)} %select_n.11), kind=kLoop, calls=%fused_computation.4 | loop fusion | bytes 589828 | tf_op jit(solution)/shard_map/dynamic_slice | solution.py:463
  26.0 0.0 collective-permute-done.3.refs_4_
  26.1 1.3 %collective-permute-start.5 = (f32[30,8,256]{2,1,0:T(8,128)S(1)}, f32[30,8,256]{2,1,0:T(8,128)S(1)}, u32[]{:S(2)}, u32[]{:S(2)}) collective-permute-start(f32[30,8,256]{2,1,0:T(8,128)S(1)} %slice_bitcast_fusion), channel_id=1, source_target_pairs={{2,0},{3,1},{4,2},{5,3},{6,4},{7,5},{8,6},{9,7},{10,8},{11,9},{12,... | collective-permute-start | bytes 737288 | tf_op jit(solution)/shard_map/ppermute | solution.py:438
  27.4 0.0 collective-permute-done.2.refs_3_
  27.4 0.7 slice_bitcast_fusion.1
  28.1 5.0 %collective-permute-start.4 = (f32[30,8,256]{2,1,0:T(8,128)}, f32[30,8,256]{2,1,0:T(8,128)S(1)}, u32[]{:S(2)}, u32[]{:S(2)}) collective-permute-start(f32[30,8,256]{2,1,0:T(8,128)} %slice_bitcast_fusion.1), channel_id=1, source_target_pairs={{0,2},{1,3},{2,4},{3,5},{4,6},{5,7},{6,8},{7,9},{8,10},{9,11},{10,... | collective-permute-start | bytes 737288 | tf_op jit(solution)/shard_map/ppermute | solution.py:438
  33.1 1.0 constant_dynamic-slice_fusion
  34.1 0.8 reshape.39
  34.9 7.8 %all-to-all-done = f32[8,32,128]{2,1,0:T(8,128)S(1)} async-done(((f32[8,32,128]{2,1,0:T(8,128)}), f32[8,32,128]{2,1,0:T(8,128)S(1)}, u32[]{:S(2)}, u32[]{:S(2)}) %all-to-all-start) | async-done | bytes 131104 | tf_op jit(solution)/shard_map/all_to_all | solution.py:460
  42.6 0.0 collective-permute-done.1.refs_2_
  42.7 0.0 collective-permute-done.refs_1_
  42.7 0.0 collective-permute-done.5.refs_6_.refs_1_
  42.7 1.0 collective-permute-done.4.refs_5_.refs_0_
  43.7 0.0 copy-start.1
  43.7 1.0 copy-done.1
  44.7 6.6 %fluid.2 = (f32[5,512]{1,0:T(8,128)S(1)}, f32[256,128]{1,0:T(8,128)}) custom-call(f32[2,30,8,256]{3,2,1,0:T(8,128)S(1)} %copy-done.1, f32[2,30,8,256]{3,2,1,0:T(8,128)} %collective-permute-done.refs_1_, f32[2,30,8,256]{3,2,1,0:T(8,128)S(1)} %collective-permute-done.1.refs_2_, f32[2,30,8,256]{3,2,1,0:T(8,128)S(1)} %collective-permute-done.2.refs_3_, ...), custom_call_target="tpu_custom_call" | custom-call | tf_op jit(solution)/shard_map/fluid/pallas_call | solution.py:350
  51.3 13.1 %all-to-all-start.1 = ((f32[128,2,128]{2,1,0:T(2,128)}), f32[128,2,128]{2,1,0:T(2,128)S(1)}, u32[]{:S(2)}, u32[]{:S(2)}) async-start(f32[128,2,128]{2,1,0:T(2,128)} %bitcast.6), calls=%async_computation.1 | async-start | bytes 262144 | tf_op jit(solution)/shard_map/all_to_all | solution.py:479
  64.5 0.1 reshape.41.inverse
  64.6 0.3 reshape.40.blocks
  64.9 0.0 copy-done
  64.9 0.1 constant_dynamic-slice_fusion.1.columns
  65.0 0.8 shell.2
  65.8 8.1 %all-to-all-done.1 = f32[128,2,128]{2,1,0:T(2,128)S(1)} async-done(((f32[128,2,128]{2,1,0:T(2,128)}), f32[128,2,128]{2,1,0:T(2,128)S(1)}, u32[]{:S(2)}, u32[]{:S(2)}) %all-to-all-start.1) | async-done | bytes 131104 | tf_op jit(solution)/shard_map/all_to_all | solution.py:479
  73.9 0.7 solve.2
  74.5 15.2 %all_to_all.50 = f32[128,4,128]{2,1,0:T(4,128)S(1)} all-to-all(f32[128,4,128]{2,1,0:T(4,128)S(1)} %bitcast.24), channel_id=1, replica_groups=mesh['fluid'=16,'struct'=8] {'fluid','struct'}, dimensions={0} | all-to-all | bytes 524288 | tf_op jit(solution)/shard_map/all_to_all | solution.py:490
  89.7 0.0 copy-done.2
  89.7 6.1 %fluid.3 = (f32[5,512]{1,0:T(8,128)}, f32[128,128]{1,0:T(8,128)}) custom-call(f32[2,30,8,256]{3,2,1,0:T(8,128)S(1)} %copy-done.2, f32[2,30,8,256]{3,2,1,0:T(8,128)} %collective-permute-done.refs_1_, f32[2,30,8,256]{3,2,1,0:T(8,128)S(1)} %collective-permute-done.1.refs_2_, f32[2,30,8,256]{3,2,1,0:T(8,128)S(1)} %collective-permute-done.2.refs_3_, ...), custom_call_target="tpu_custom_call" | custom-call | tf_op jit(solution)/shard_map/fluid/pallas_call | solution.py:350
  95.8 4.5 %all-to-all-start.3 = ((f32[128,1,128]{2,1,0:T(1,128)}), f32[128,1,128]{2,1,0:T(1,128)S(1)}, u32[]{:S(2)}, u32[]{:S(2)}) async-start(f32[128,1,128]{2,1,0:T(1,128)} %bitcast.12), calls=%async_computation.3 | async-start | bytes 131072 | tf_op jit(solution)/shard_map/all_to_all | solution.py:479
  100.3 0.8 shell.3
  101.2 8.5 %all-to-all-done.3 = f32[128,1,128]{2,1,0:T(1,128)S(1)} async-done(((f32[128,1,128]{2,1,0:T(1,128)}), f32[128,1,128]{2,1,0:T(1,128)S(1)}, u32[]{:S(2)}, u32[]{:S(2)}) %all-to-all-start.3) | async-done | bytes 65568 | tf_op jit(solution)/shard_map/all_to_all | solution.py:479
  109.6 0.3 solve.3
  109.9 10.9 %all_to_all.51 = f32[16,2,128]{2,1,0:T(2,128)S(1)} all-to-all(f32[16,2,128]{2,1,0:T(2,128)S(1)} %bitcast.27), channel_id=1, replica_groups=mesh['fluid'=16,'struct'=8] {'fluid'}, dimensions={0} | all-to-all | bytes 32768 | tf_op jit(solution)/shard_map/all_to_all | solution.py:494
  120.9 0.7 reshape.43
  (3 shorter events, 0.0 us)
Async XLA Ops:
  0.6 64.2 %copy-start = (s32[4,32]{1,0:T(4,128)S(1)}, s32[4,32]{1,0:T(4,128)}, u32[]{:S(2)}) copy-start(s32[4,32]{1,0:T(4,128)} %param.31) | copy-start | bytes 1540
  3.3 86.4 %copy-start.2 = (f32[2,30,8,256]{3,2,1,0:T(8,128)S(1)}, f32[2,30,8,256]{3,2,1,0:T(8,128)}, u32[]{:S(2)}) copy-start(f32[2,30,8,256]{3,2,1,0:T(8,128)} %pack.1.refs_0_) | copy-start | bytes 1474564
  3.3 22.7 %collective-permute-start.3 = (f32[2,30,8,256]{3,2,1,0:T(8,128)}, f32[2,30,8,256]{3,2,1,0:T(8,128)S(1)}, u32[]{:S(2)}, u32[]{:S(2)}) collective-permute-start(f32[2,30,8,256]{3,2,1,0:T(8,128)} %pack.1.refs_0_), channel_id=1, source_target_pairs={{1,0},{2,1},{3,2},{4,3},{5,4},{6,5},{7,6},{8,7},{9,8},{10,9},{11,1... | collective-permute-start | bytes 1474568 | tf_op jit(solution)/shard_map/ppermute | solution.py:438
  4.7 22.6 %collective-permute-start.2 = (f32[2,30,8,256]{3,2,1,0:T(8,128)}, f32[2,30,8,256]{3,2,1,0:T(8,128)S(1)}, u32[]{:S(2)}, u32[]{:S(2)}) collective-permute-start(f32[2,30,8,256]{3,2,1,0:T(8,128)} %pack.1.refs_0_), channel_id=1, source_target_pairs={{0,1},{1,2},{2,3},{3,4},{4,5},{5,6},{6,7},{7,8},{8,9},{9,10},{10,1... | collective-permute-start | bytes 1474568 | tf_op jit(solution)/shard_map/ppermute | solution.py:438
  9.3 33.3 %collective-permute-start.1 = (f32[2,30,8,256]{3,2,1,0:T(8,128)}, f32[2,30,8,256]{3,2,1,0:T(8,128)S(1)}, u32[]{:S(2)}, u32[]{:S(2)}) collective-permute-start(f32[2,30,8,256]{3,2,1,0:T(8,128)} %pack.1.refs_0_), channel_id=1, source_target_pairs={{2,0},{3,1},{4,2},{5,3},{6,4},{7,5},{8,6},{9,7},{10,8},{11,9},{12,... | collective-permute-start | bytes 1474568 | tf_op jit(solution)/shard_map/ppermute | solution.py:438
  10.6 32.0 %collective-permute-start = (f32[2,30,8,256]{3,2,1,0:T(8,128)}, f32[2,30,8,256]{3,2,1,0:T(8,128)}, u32[]{:S(2)}, u32[]{:S(2)}) collective-permute-start(f32[2,30,8,256]{3,2,1,0:T(8,128)} %pack.1.refs_0_), channel_id=1, source_target_pairs={{0,2},{1,3},{2,4},{3,5},{4,6},{5,7},{6,8},{7,9},{8,10},{9,11},{10,... | collective-permute-start | bytes 1474568 | tf_op jit(solution)/shard_map/ppermute | solution.py:438
  17.4 25.2 %all-to-all-start = ((f32[8,32,128]{2,1,0:T(8,128)}), f32[8,32,128]{2,1,0:T(8,128)S(1)}, u32[]{:S(2)}, u32[]{:S(2)}) async-start(f32[8,32,128]{2,1,0:T(8,128)} %broadcast_in_dim.3), calls=%async_computation | async-start | bytes 262144 | tf_op jit(solution)/shard_map/all_to_all | solution.py:460
  26.1 16.6 %collective-permute-start.5 = (f32[30,8,256]{2,1,0:T(8,128)S(1)}, f32[30,8,256]{2,1,0:T(8,128)S(1)}, u32[]{:S(2)}, u32[]{:S(2)}) collective-permute-start(f32[30,8,256]{2,1,0:T(8,128)S(1)} %slice_bitcast_fusion), channel_id=1, source_target_pairs={{2,0},{3,1},{4,2},{5,3},{6,4},{7,5},{8,6},{9,7},{10,8},{11,9},{12,... | collective-permute-start | bytes 737288 | tf_op jit(solution)/shard_map/ppermute | solution.py:438
  28.1 15.6 %collective-permute-start.4 = (f32[30,8,256]{2,1,0:T(8,128)}, f32[30,8,256]{2,1,0:T(8,128)S(1)}, u32[]{:S(2)}, u32[]{:S(2)}) collective-permute-start(f32[30,8,256]{2,1,0:T(8,128)} %slice_bitcast_fusion.1), channel_id=1, source_target_pairs={{0,2},{1,3},{2,4},{3,5},{4,6},{5,7},{6,8},{7,9},{8,10},{9,11},{10,... | collective-permute-start | bytes 737288 | tf_op jit(solution)/shard_map/ppermute | solution.py:438
  43.7 1.0 copy-start.1
  51.3 22.5 %all-to-all-start.1 = ((f32[128,2,128]{2,1,0:T(2,128)}), f32[128,2,128]{2,1,0:T(2,128)S(1)}, u32[]{:S(2)}, u32[]{:S(2)}) async-start(f32[128,2,128]{2,1,0:T(2,128)} %bitcast.6), calls=%async_computation.1 | async-start | bytes 262144 | tf_op jit(solution)/shard_map/all_to_all | solution.py:479
  95.8 13.8 %all-to-all-start.3 = ((f32[128,1,128]{2,1,0:T(1,128)}), f32[128,1,128]{2,1,0:T(1,128)S(1)}, u32[]{:S(2)}, u32[]{:S(2)}) async-start(f32[128,1,128]{2,1,0:T(1,128)} %bitcast.12), calls=%async_computation.3 | async-start | bytes 131072 | tf_op jit(solution)/shard_map/all_to_all | solution.py:479
